TPU v7x, 32 devices: a whole 2x2x4 slice. The times are simulated.
32 devices in a mesh: dp: 8 (over z, y), tensor: 4 (over x, core).
Axes of the slice: x: 2, y: 2, z: 4, core: 2. Of those that a mesh axis runs over, the one named last changes fastest.
Arguments:
- hidden_in: bfloat16 [16384, 768], P(('dp', 'tensor')), may hold values from -33 to 33
- positions: int32 [16384], P('dp'), may hold values from 0 to 2047, as said below
- mixer_gain: float32 [768], replicated, may hold values from 0.5 to 1.5
- mixer_shift: float32 [768], replicated, may hold values from -2 to 2
- feed_gain: float32 [768], replicated, may hold values from 0.5 to 1.5
- feed_shift: float32 [768], replicated, may hold values from -2 to 2
- triple_weight: bfloat16 [768, 3, 768], P('dp', None, 'tensor'), may hold values from -3 to 3
- pair_bias: float32 [2, 768], P(None, 'tensor'), may hold values from -2 to 2
- output_weight: bfloat16 [768, 768], P('tensor', 'dp'), may hold values from -1.75 to 1.75
- up_weight: bfloat16 [768, 3072], P('dp', 'tensor'), may hold values from -0.21875 to 0.21875
- up_bias: float32 [3072], P('tensor'), may hold values from -2 to 2
- down_weight: bfloat16 [3072, 768], P('tensor', 'dp'), may hold values from -0.109375 to 0.109375
- out_bias: float32 [768], replicated, may hold values from -2 to 2
- out_grad: bfloat16 [16384, 768], P(('dp', 'tensor')), may hold values from -6 to 6
Outputs:
- result: float32 [16384, 768], P(('dp', 'tensor'))
- grad_hidden: float32 [16384, 768], P(('dp', 'tensor'))
- grad_mixer_gain: float32 [768], replicated
- grad_mixer_shift: float32 [768], replicated
- grad_feed_gain: float32 [768], replicated
- grad_feed_shift: float32 [768], replicated
- grad_triple: float32 [768, 3, 768], P('dp', None, 'tensor')
- grad_pair_bias: float32 [2, 768], P(None, 'tensor')
- grad_output: float32 [768, 768], P('tensor', 'dp')
- grad_up: float32 [768, 3072], P('dp', 'tensor')
- grad_up_bias: float32 [3072], P('tensor')
- grad_down: float32 [3072, 768], P('tensor', 'dp')
- grad_out_bias: float32 [768], replicated
Inputs may be any that keep to these rules, and one draw needn't show every extreme that they name: `positions`: documents follow one another without gaps from the stream's first token; each has an eighth of 2048 to 2048 tokens (the last one may be cut by the stream's end) and one has exactly 2048; a token's position counts from its document's first token.
All inputs are finite; a program needn't handle non-finite values.
Results may differ from a plain program's by a relative error of at most 0.0086.
Values may be sent and summed in bfloat16 or wider, within the bound.
No kernel may reach another device: no remote copies, remote signals or barrier semaphores. Data moves between devices by JAX's collectives and lax.ppermute only.
A program may use at most 192 MiB of HBM per device.

v0:
```python
import functools
import math

import jax
import jax.numpy as jnp
from jax import lax
from jax.experimental import pallas as pl
from jax.experimental.pallas import tpu as pltpu
from jax.sharding import PartitionSpec as P

HD = 64
ROT = 16
DOC_MOST = 2048
EPSILON = 1e-05
NEG = -1e30
TQ = 256
TK = 256
NK = 2
TR = 512
FR = 512
PR = 512
bf16 = jnp.bfloat16
f32 = jnp.float32
NN = (((1,), (0,)), ((), ()))
NT = (((1,), (1,)), ((), ()))
TN = (((0,), (0,)), ((), ()))
TT = (((0,), (1,)), ((), ()))
VMEM_LIMIT = 56 * 2**20
COST = pl.CostEstimate(flops=1000, bytes_accessed=1000, transcendentals=0)


def mm(left, right, dims=NN):
    return lax.dot_general(left, right, dims, preferred_element_type=f32)


def swap(value, axis, mask):
    count = lax.axis_size(axis)
    return lax.ppermute(value, axis, [(i, i ^ mask) for i in range(count)])


def shift(value, axis, distance):
    count = lax.axis_size(axis)
    route = [(i, i + distance) for i in range(count) if 0 <= i + distance < count]
    return lax.ppermute(value, axis, route)


def bit_count(axis):
    return lax.axis_size(axis).bit_length() - 1


def after(value, *others):
    return lax.optimization_barrier((value, *others))[0]


def gather_tensor(own):
    near = swap(own, "tensor", 1)
    far = swap(own, "tensor", 2)
    diagonal = swap(far, "tensor", 1)
    return [own, near, far, diagonal]


def scatter_core(blocks, rows):
    back = jnp.concatenate([blocks[rows : 2 * rows], blocks[3 * rows :]], axis=0)
    near = swap(back, "tensor", 1).astype(f32)
    far = (blocks[2 * rows : 3 * rows].astype(f32) + near[rows:]).astype(bf16)
    return blocks[:rows].astype(f32) + near[:rows], far


def split(held, rows, left, bit):
    above = 1 << sum(b > bit for b in left)
    return held.reshape(above, 2, -1, held.shape[-1])


def gather_dp(own, order, gates=()):
    me = lax.axis_index("dp")
    rows, cols = own.shape
    held, done = own, []
    parts = []
    for n, bit in enumerate(order):
        if n == 0 and gates and gates[0] is not None:
            held = after(held, gates[0])
        other = swap(held, "dp", 1 << bit)
        if n + 1 < len(gates) and gates[n + 1] is not None:
            other = after(other, gates[n + 1])
        high = ((me >> bit) & 1) == 1
        above = 1 << sum(b > bit for b in done)
        one, two = held.reshape(above, -1, cols), other.reshape(above, -1, cols)
        held = jnp.stack([jnp.where(high, two, one), jnp.where(high, one, two)], axis=1).reshape(-1, cols)
        done.append(bit)
        parts.append(held)
    return held, parts


def two_parts(sums):
    first = lax.reduce_precision(sums, 8, 7)
    return first, lax.reduce_precision(sums - first, 8, 7)


def scatter_dp(whole, rows, order, gates=(), sums=None):
    me = lax.axis_index("dp")
    cols = whole.shape[1]
    left = sorted(order, reverse=True)
    held = whole
    parts = []
    for n, bit in enumerate(order):
        pairs = split(held, rows, left, bit)
        high = ((me >> bit) & 1) == 1
        send = jnp.where(high, pairs[:, 0], pairs[:, 1]).astype(bf16).reshape(-1, cols)
        keep = jnp.where(high, pairs[:, 1], pairs[:, 0]).astype(f32).reshape(-1, cols)
        count = send.shape[0]
        if sums is not None:
            first, second = two_parts(sums)
            send = jnp.concatenate([send, first.astype(bf16), second.astype(bf16)], axis=0)
        if n < len(gates) and gates[n] is not None:
            send = after(send, gates[n])
        other = swap(send, "dp", 1 << bit).astype(f32)
        held = keep + other[:count]
        if sums is not None:
            sums = (first + second) + (other[count : count + 8] + other[count + 8 :])
        left.remove(bit)
        parts.append(held)
    return held, parts, sums


def sum_over(value, axis):
    for bit in range(bit_count(axis)):
        value = value + swap(value, axis, 1 << bit)
    return value


def normalize(values):
    centred = values - jnp.mean(values, axis=-1, keepdims=True)
    inv_std = lax.rsqrt(jnp.mean(centred * centred, axis=-1, keepdims=True) + EPSILON)
    return (centred * inv_std, inv_std)


def rows_spec(cols, tile=TR):
    return pl.BlockSpec((tile, cols), lambda i: (i, 0))


def whole_spec(shape):
    return pl.BlockSpec(shape, lambda i: (0,) * len(shape))


def heads_spec(heads, cols=128, tile=TR):
    return pl.BlockSpec((heads, tile, cols), lambda i: (0, i, 0))


def piece_specs(count, rows, cols, tile=TR):
    per = rows // tile
    return [pl.BlockSpec((tile, cols), lambda i, p=p: (jnp.clip(i - p * per, 0, per - 1), 0)) for p in range(count)]


def pick(refs, rows):
    at = pl.program_id(0) // (rows // refs[0].shape[0])
    value = refs[0][...]
    for n, ref in enumerate(refs[1:]):
        value = jnp.where(at == n + 1, ref[...], value)
    return value


def rotation_rows(cos, sin):
    ones = jnp.ones((128 - ROT, cos.shape[1]), f32)
    return jnp.concatenate([cos, cos, ones], axis=0).T, jnp.concatenate([-sin, sin, ones * 0.0], axis=0).T


def rotate(x, cos_rows, sin_rows):
    lane = lax.broadcasted_iota(jnp.int32, x.shape, 1)
    partner = jnp.where(lane < ROT // 2, pltpu.roll(x, 128 - ROT // 2, 1), pltpu.roll(x, ROT // 2, 1))
    return x * cos_rows + partner * sin_rows


def pre_kernel(*refs, pieces, blk):
    hids, refs = refs[:pieces], refs[pieces:]
    gains_ref, w_ref, bias_ref, cos_ref, sin_ref, mixer_ref, kv_ref, q_ref = refs
    heads = kv_ref.shape[0]
    normed, _ = normalize(pick(hids, blk).astype(f32))
    mixer = (normed * gains_ref[0:1] + gains_ref[1:2]).astype(bf16)
    mixer_ref[...] = mixer
    proj = mm(mixer, w_ref[...]) + bias_ref[...]
    cos_rows, sin_rows = rotation_rows(cos_ref[...], sin_ref[...])
    lane = lax.broadcasted_iota(jnp.int32, (TR, 128), 1)
    for h in range(heads):
        kv_ref[h] = rotate(proj[:, h * 128 : (h + 1) * 128], cos_rows, sin_rows).astype(bf16)
        at = heads * 128 + (h // 2) * 128
        x = proj[:, at : at + 128]
        if h % 2:
            x = pltpu.roll(x, HD, 1)
        x = jnp.where(lane < HD, rotate(x, cos_rows, sin_rows) * (1.0 / math.sqrt(HD)), 0.0)
        q_ref[h] = x.astype(bf16)


def pre(hids, gains, w, bias, cos, sin, heads):
    blk, D = hids[0].shape
    T = blk * len(hids)
    return pl.pallas_call(
        functools.partial(pre_kernel, pieces=len(hids), blk=blk),
        grid=(T // TR,),
        in_specs=piece_specs(len(hids), blk, D) + [
            whole_spec(gains.shape),
            whole_spec(w.shape),
            whole_spec(bias.shape),
            pl.BlockSpec((8, TR), lambda i: (0, i)),
            pl.BlockSpec((8, TR), lambda i: (0, i)),
        ],
        out_specs=[rows_spec(D)] + [heads_spec(heads)] * 2,
        out_shape=[jax.ShapeDtypeStruct((T, D), bf16)] + [jax.ShapeDtypeStruct((heads, T, 128), bf16)] * 2,
        compiler_params=pltpu.CompilerParams(vmem_limit_bytes=VMEM_LIMIT),
        cost_estimate=COST,
        name="pre",
    )(*hids, gains, w, bias, cos, sin)


def gelu_parts(h):
    mag = jnp.abs(h) * (1.0 / math.sqrt(2.0))
    t = 1.0 / (1.0 + 0.3275911 * mag)
    poly = t * (0.254829592 + t * (-0.284496736 + t * (1.421413741 + t * (-1.453152027 + t * 1.061405429))))
    bell = jnp.exp(-0.5 * h * h)
    tail = 0.5 * poly * bell
    return (jnp.where(h >= 0, 1.0 - tail, tail), bell * (1.0 / math.sqrt(2.0 * math.pi)))


def ffn_kernel(*refs, pieces, blk):
    hids, gs, refs = refs[:pieces], refs[pieces : 2 * pieces], refs[2 * pieces :]
    gains_ref, w_ref, bias_ref, normed_ref, g_ref, branch_ref, back_ref, do_ref, grad_ref, sums_ref, acc_ref = refs
    heads = do_ref.shape[0]
    F = bias_ref.shape[1]
    step = pl.program_id(0)
    normed, _ = normalize(pick(hids, blk).astype(f32))
    normed_ref[...] = normed.astype(bf16)
    feed = (normed * gains_ref[0:1] + gains_ref[1:2]).astype(bf16)
    g = pick(gs, blk)
    g_ref[...] = g
    up, down = w_ref[:, :F], w_ref[:, F : 2 * F]
    hidden = mm(feed, up) + bias_ref[...]
    cumulative, density = gelu_parts(hidden)
    act = (hidden * cumulative).astype(bf16)
    hg = (mm(g, down) * (cumulative + hidden * density)).astype(bf16)
    branch_ref[...] = mm(act, down, NT).astype(bf16)
    back = mm(hg, up, NT)
    back_ref[...] = (back * gains_ref[0:1]).astype(bf16)

    @pl.when(step == 0)
    def _():
        sums_ref[...] = jnp.zeros_like(sums_ref)
        acc_ref[...] = jnp.zeros_like(acc_ref)

    acc_ref[:, :F] += mm(feed, hg, TN)
    acc_ref[:, F:] += mm(g, act, TN)
    sums_ref[3:4] += jnp.sum(back * normed, axis=0, keepdims=True)
    sums_ref[4:5] += jnp.sum(back, axis=0, keepdims=True)
    sums_ref[5:6] += jnp.sum(hg.astype(f32), axis=0, keepdims=True)

    @pl.when(step < blk // FR)
    def _():
        sums_ref[6:7] += jnp.sum(g.astype(f32), axis=0, keepdims=True)

    @pl.when(step == pl.num_programs(0) - 1)
    def _():
        grad_ref[...] = acc_ref[...].astype(bf16)

    do = mm(g, w_ref[:, 2 * F :])
    lane = lax.broadcasted_iota(jnp.int32, (FR, 128), 1)
    for h in range(heads):
        at = (h // 2) * 128
        x = do[:, at : at + 128]
        if h % 2 == 0:
            x = pltpu.roll(x, HD, 1)
        do_ref[h] = jnp.where(lane < HD, 0.0, x).astype(bf16)


def ffn(hids, gs, gains, w, bias, heads):
    blk, D = gs[0].shape
    T = blk * len(gs)
    F = bias.shape[1]
    rows = rows_spec(D, FR)
    return pl.pallas_call(
        functools.partial(ffn_kernel, pieces=len(gs), blk=blk),
        grid=(T // FR,),
        in_specs=piece_specs(len(gs), blk, D, FR) * 2 + [whole_spec(gains.shape), whole_spec(w.shape), whole_spec(bias.shape)],
        out_specs=[rows] * 4 + [heads_spec(heads, 128, FR), whole_spec((D, 2 * F)), whole_spec((8, D))],
        out_shape=[jax.ShapeDtypeStruct((T, D), bf16)] * 4
        + [
            jax.ShapeDtypeStruct((heads, T, 128), bf16),
            jax.ShapeDtypeStruct((D, 2 * F), bf16),
            jax.ShapeDtypeStruct((8, D), f32),
        ],
        scratch_shapes=[pltpu.VMEM((D, 2 * F), f32)],
        compiler_params=pltpu.CompilerParams(vmem_limit_bytes=VMEM_LIMIT),
        cost_estimate=COST,
        name="ffn",
    )(*hids, *gs, gains, w, bias)


def attn_kernel(*refs, T, blk, heads, late):
    if late:
        (place_ref, first_ref, start_ref, tail_ref, kv_ref, q_ref, do_ref, cos_ref, sin_ref, carry_ref, o_in, dq_in,
         o_ref, dq_ref, dtail_ref, low_ref, high_ref, *refs) = refs
    else:
        (place_ref, first_ref, start_ref, tail_ref, kv_ref, q_ref, do_ref, cos_ref, sin_ref,
         o_ref, dq_ref, dtail_ref, carry_ref, *refs) = refs
    kv_scr, dkv_scr, s_scr, dp_scr, o_acc, dq_acc, qd_scr = refs
    half = T // 2
    base = half if late else 0
    t = place_ref[0]
    inner = (t & 1) * blk
    H = range(heads)

    def half_at(n):
        return pl.ds(pl.multiple_of((n ^ (t >> 1)) * half, half), half)

    for n, (ref, part) in enumerate([(tail_ref, 1), (kv_ref, 0), (kv_ref, 1)] if late else [(tail_ref, 0), (tail_ref, 1), (kv_ref, 0)]):
        kv_scr[:, n * half : (n + 1) * half] = ref[:, half_at(part), :]
    if late:
        dkv_scr[:, :T] = carry_ref[...]
        dkv_scr[:, T:] = jnp.zeros_like(dkv_scr[:, T:])
        o_ref[:, half_at(0)] = o_in[...]
        dq_ref[:, half_at(0)] = dq_in[...]
    else:
        dkv_scr[...] = jnp.zeros_like(dkv_scr)

    def place(row):
        return (row - base) ^ inner

    def q_tile(qi, c):
        q0 = pl.multiple_of(base + qi * TQ, TQ)
        qr = pl.multiple_of(q0 ^ (t * blk), TQ)
        out = qr if late else pl.multiple_of(place(q0), TQ)
        for h in H:
            qd_scr[h, :TQ] = q_ref[h, pl.ds(qr, TQ), :]
            qd_scr[h, TQ:] = do_ref[h, pl.ds(qr, TQ), :]
        start = start_ref[:, pl.ds(qr, TQ)]
        qidx = q0 + T + lax.broadcasted_iota(jnp.int32, (1, TQ), 1)
        first = first_ref[base // TQ + qi]
        stop = (q0 + T) // TK + TQ // TK
        count = stop - first

        def over(body, init):
            pairs = count // NK
            state = lax.fori_loop(0, pairs, lambda i, c: body(first + i * NK, c, NK), init)
            return lax.fori_loop(first + pairs * NK, stop, lambda i, c: body(i, c, 1), state)

        def pass1(ki, state, nk):
            rows = nk * TK
            slot = ki - first
            j = ki * TK + lax.broadcasted_iota(jnp.int32, (rows, TQ), 0)
            ok = (j >= start) & (j <= qidx)
            ats = [pl.multiple_of(place((ki + n) * TK), TK) for n in range(nk)]
            sdps = [mm(jnp.concatenate([kv_scr[h, pl.ds(at, TK), :] for at in ats], axis=0), qd_scr[h], NT) for h in H]
            stats = []
            for h in H:
                m8, l8, d8 = state[3 * h : 3 * h + 3]
                s = jnp.where(ok, sdps[h][:, :TQ], NEG)
                dp = sdps[h][:, TQ:]
                for n in range(nk):
                    s_scr[slot + n, h] = s[n * TK : (n + 1) * TK]
                    dp_scr[slot + n, h] = dp[n * TK : (n + 1) * TK]
                s3 = s.reshape(rows // 8, 8, TQ)
                m_new = jnp.maximum(m8, jnp.max(s3, axis=0))
                alpha = jnp.exp(m8 - m_new)
                e = jnp.exp(s3 - m_new[None])
                l8 = l8 * alpha + jnp.sum(e, axis=0)
                d8 = d8 * alpha + jnp.sum(e * dp.reshape(rows // 8, 8, TQ), axis=0)
                stats += [m_new, l8, d8]
            return tuple(stats)

        z8 = jnp.zeros((8, TQ), f32)
        state = over(pass1, (jnp.full((8, TQ), NEG, f32), z8, z8) * heads)
        lses, deltas = [], []
        for h in H:
            m8, l8, d8 = state[3 * h : 3 * h + 3]
            m = jnp.max(m8, axis=0, keepdims=True)
            w = jnp.exp(m8 - m)
            total = jnp.sum(l8 * w, axis=0, keepdims=True)
            lses.append(m + jnp.log(total))
            deltas.append(jnp.sum(d8 * w, axis=0, keepdims=True) / total)
        o_acc[...] = jnp.zeros_like(o_acc)
        dq_acc[...] = jnp.zeros_like(dq_acc)

        def pass2(ki, c2, nk):
            slot = ki - first
            ats = [pl.multiple_of(place((ki + n) * TK), TK) for n in range(nk)]
            for h in H:
                dq = dq_acc[h]
                o = o_acc[h]
                for n in range(nk):
                    p = jnp.exp(s_scr[slot + n, h] - lses[h])
                    ds = (p * (dp_scr[slot + n, h] - deltas[h])).astype(bf16)
                    p = p.astype(bf16)
                    dkv_scr[h, pl.ds(ats[n], TK), :] += mm(jnp.concatenate([ds, p], axis=1), qd_scr[h])
                    kvt = kv_scr[h, pl.ds(ats[n], TK), :].T
                    dq += mm(kvt[:HD], ds)
                    o += mm(kvt[HD:], p)
                dq_acc[h] = dq
                o_acc[h] = o
            return c2

        over(pass2, 0)
        cos = cos_ref[:, pl.ds(qr, TQ)]
        sin = sin_ref[:, pl.ds(qr, TQ)]
        for h in H:
            o_ref[h * HD : (h + 1) * HD, pl.ds(out, TQ)] = o_acc[h].astype(bf16)
            dq = dq_acc[h] * (1.0 / math.sqrt(HD))
            a, b = dq[: ROT // 2], dq[ROT // 2 : ROT]
            dq = jnp.concatenate([a * cos + b * sin, b * cos - a * sin, dq[ROT:]], axis=0)
            dq_ref[h * HD : (h + 1) * HD, pl.ds(out, TQ)] = dq.astype(bf16)
        return c

    lax.fori_loop(0, half // TQ, q_tile, 0)
    dtail_ref[...] = dkv_scr[:, :half].astype(bf16)
    if late:
        low_ref[...] = dkv_scr[:, half:T]
        high_ref[...] = dkv_scr[:, T:]
    else:
        carry_ref[...] = dkv_scr[:, half:]


def attention(place, first, start, tail, kv, q, do, cos, sin, blk, early=()):
    heads, T, _ = q.shape
    W = heads * HD
    late = len(early) > 0
    vmem = pl.BlockSpec(memory_space=pltpu.VMEM)
    smem = pl.BlockSpec(memory_space=pltpu.SMEM)
    slots = DOC_MOST // TK + TQ // TK
    span = T if late else T // 2
    outs = [((W, span), bf16), ((W, span), bf16), ((heads, T // 2, 128), bf16)]
    outs += [((heads, T // 2, 128), f32)] * 2 if late else [((heads, T, 128), f32)]
    return pl.pallas_call(
        functools.partial(attn_kernel, T=T, blk=blk, heads=heads, late=late),
        in_specs=[smem, smem] + [vmem] * (7 + len(early)),
        out_specs=[vmem] * len(outs),
        scratch_shapes=[
            pltpu.VMEM((heads, T + T // 2, 128), bf16),
            pltpu.VMEM((heads, T + T // 2, 128), f32),
            pltpu.VMEM((slots, heads, TK, TQ), f32),
            pltpu.VMEM((slots, heads, TK, TQ), f32),
            pltpu.VMEM((heads, HD, TQ), f32),
            pltpu.VMEM((heads, HD, TQ), f32),
            pltpu.VMEM((heads, 2 * TQ, 128), bf16),
        ],
        out_shape=[jax.ShapeDtypeStruct(*out) for out in outs],
        compiler_params=pltpu.CompilerParams(vmem_limit_bytes=VMEM_LIMIT),
        cost_estimate=COST,
        name="attn",
    )(place, first, start, tail, kv, q, do, cos, sin, *early)


def mid_kernel(o_ref, dq_ref, mixer_ref, g_ref, branch_ref, w_ref, out_ref, grad_ref, acc_ref):
    W = o_ref.shape[0]
    step = pl.program_id(0)
    o = o_ref[...]
    rows = o.astype(f32).T.astype(bf16)
    out_ref[...] = (mm(rows, w_ref[:, :W], NT) + branch_ref[...].astype(f32)).astype(bf16)

    @pl.when(step == 0)
    def _():
        acc_ref[...] = jnp.zeros_like(acc_ref)

    acc_ref[:W] += mm(dq_ref[...], mixer_ref[...])
    acc_ref[W:] += mm(o, g_ref[...])

    @pl.when(step == pl.num_programs(0) - 1)
    def _():
        grad_ref[...] = acc_ref[...].T.astype(bf16)


def mid(o, dq, mixer, g, branch, w):
    T, D = mixer.shape
    W = o.shape[0]
    cols = pl.BlockSpec((W, TR), lambda i: (0, i))
    return pl.pallas_call(
        mid_kernel,
        grid=(T // TR,),
        in_specs=[cols, cols, rows_spec(D), rows_spec(D), rows_spec(D), whole_spec(w.shape)],
        out_specs=[rows_spec(D), whole_spec((D, 2 * W))],
        out_shape=[jax.ShapeDtypeStruct((T, D), bf16), jax.ShapeDtypeStruct((D, 2 * W), bf16)],
        scratch_shapes=[pltpu.VMEM((2 * W, D), f32)],
        compiler_params=pltpu.CompilerParams(vmem_limit_bytes=VMEM_LIMIT),
        cost_estimate=COST,
        name="mid",
    )(o, dq, mixer, g, branch, w)


def post_kernel(place_ref, dkv_ref, ahead_ref, dq_ref, cos_ref, sin_ref, normed_ref, mixer_ref, back_ref, gain_ref, w_ref, *refs):
    heads = dkv_ref.shape[0]
    W = heads * HD
    step = pl.program_id(0)
    if len(refs) == 8:
        _, acc_in, sums_in, mid_ref, *refs = refs
    else:
        acc_in = mid_ref = None
        sums_in, *refs = refs
    hat_ref, grad_ref, sums_ref, acc_ref = refs

    @pl.when(step == 0)
    def _():
        sums_ref[...] = sums_in[...]
        acc_ref[...] = jnp.zeros_like(acc_ref) if acc_in is None else acc_in[...]

    cos_rows, sin_rows = rotation_rows(cos_ref[...], sin_ref[...])
    kv = jnp.concatenate(
        [rotate(dkv_ref[h] + ahead_ref[h].astype(f32), cos_rows, -sin_rows).astype(bf16) for h in range(heads)], axis=1
    )
    acc_ref[...] += mm(mixer_ref[...], kv, TN)
    dq = dq_ref[...].astype(f32).T.astype(bf16)
    part = mm(kv, w_ref[:, : 2 * W], NT) + mm(dq, w_ref[:, 2 * W : 3 * W], NT)
    hat_ref[...] = (part * gain_ref[...] + back_ref[...].astype(f32)).astype(bf16)
    sums_ref[0:1] += jnp.sum(part * normed_ref[...].astype(f32), axis=0, keepdims=True)
    sums_ref[1:2] += jnp.sum(part, axis=0, keepdims=True)
    sums_ref[2:3, : 2 * W] += jnp.sum(kv.astype(f32), axis=0, keepdims=True)
    sums_ref[2:3, 2 * W : 3 * W] += jnp.sum(dq.astype(f32), axis=0, keepdims=True)

    @pl.when(step == pl.num_programs(0) - 1)
    def _():
        grad_ref[:, : 2 * W] = acc_ref[...].astype(grad_ref.dtype)
        if mid_ref is not None:
            grad_ref[:, 2 * W :] = mid_ref[...]


def post(part, place, dkv, ahead, dq, cos, sin, normed, mixer, back, gain, w, early=()):
    T, D = mixer.shape
    heads = dkv.shape[0]
    W = heads * HD
    per = T // 2 // PR

    def at(i, place):
        return (part ^ (place[0] >> 1)) * per + i

    def inner(i, place):
        return i

    def rows(index):
        return pl.BlockSpec((PR, D), lambda i, place: (index(i, place), 0))

    def cols(count):
        return pl.BlockSpec((count, PR), lambda i, place: (0, at(i, place)))

    def fixed(shape):
        return pl.BlockSpec(shape, lambda i, place: (0,) * len(shape))

    half = pl.BlockSpec((heads, PR, 128), lambda i, place: (0, i, 0))
    late = len(early) > 1
    specs = [half, half, cols(W), cols(8), cols(8), rows(at), rows(at), rows(at), fixed(gain.shape), fixed(w.shape)]
    if late:
        specs += [pl.BlockSpec(memory_space=pl.ANY), fixed((D, 2 * W)), fixed((8, D)), fixed((D, 2 * W))]
    else:
        specs += [fixed((8, D))]
    return pl.pallas_call(
        post_kernel,
        grid_spec=pltpu.PrefetchScalarGridSpec(
            num_scalar_prefetch=1,
            grid=(per,),
            in_specs=specs,
            out_specs=[rows(at), fixed((D, (4 if late else 2) * W)), fixed((8, D))],
            scratch_shapes=[pltpu.VMEM((D, 2 * W), f32)],
        ),
        out_shape=[
            jax.ShapeDtypeStruct((T, D), bf16),
            jax.ShapeDtypeStruct((D, 4 * W), bf16) if late else jax.ShapeDtypeStruct((D, 2 * W), f32),
            jax.ShapeDtypeStruct((8, D), f32),
        ],
        input_output_aliases={11: 0} if late else {},
        compiler_params=pltpu.CompilerParams(vmem_limit_bytes=VMEM_LIMIT),
        cost_estimate=COST,
        name="post",
    )(place, dkv, ahead, dq, cos, sin, normed, mixer, back, gain, w, *early)


def shards(
    hidden_in, positions, mixer_gain, mixer_shift, feed_gain, feed_shift, triple_weight,
    pair_bias, output_weight, up_weight, up_bias, down_weight, out_bias, out_grad,
):
    T = positions.shape[0]
    blk, D = hidden_in.shape
    W = pair_bias.shape[1]
    heads = W // HD
    chunk = triple_weight.shape[0]
    t = lax.axis_index("tensor").astype(jnp.int32)

    F = up_weight.shape[1]
    bits = bit_count("dp")
    down_order = list(reversed(range(bits)))
    mixed_order = down_order[:-2] + [0, 1]
    q_w, k_w, v_w = (triple_weight[:, i].reshape(chunk, heads, HD) for i in range(3))
    kv_w = jnp.concatenate([k_w, v_w], axis=2).reshape(chunk, 2 * W)
    pad = (-W) % 128
    no_cols = jnp.zeros((chunk, pad), bf16)
    qkv_w, qkv_parts = gather_dp(jnp.concatenate([kv_w, q_w.reshape(chunk, W), no_cols], axis=1), down_order)
    hids = gather_tensor(hidden_in)
    gs = gather_tensor(after(out_grad, hids[2]))

    pos = jnp.concatenate([lax.dynamic_slice(positions, ((r ^ t) * blk,), (blk,)) for r in range(T // blk)])
    inverse = 1.0 / 10000.0 ** (jnp.arange(ROT // 2, dtype=f32) * (2.0 / ROT))
    angles = pos.astype(f32)[None, :] * inverse[:, None]
    cos, sin = jnp.cos(angles), jnp.sin(angles)
    rows = jnp.arange(T, dtype=jnp.int32) ^ (t * blk)
    start = (rows + T - pos)[None]
    q_starts = jnp.arange(0, T, TQ, dtype=jnp.int32)
    first = (q_starts + T - positions[::TQ]) // TK

    gains = jnp.stack([mixer_gain, mixer_shift, feed_gain, feed_shift])
    v_bias = pair_bias[1].reshape(heads, HD)
    kv_bias = jnp.concatenate([jnp.zeros_like(v_bias), v_bias], axis=1).reshape(2 * W)
    bias = jnp.concatenate([kv_bias, pair_bias[0], jnp.zeros((pad,), f32)])[None]
    mixer_in, kv, q = pre(hids, gains, qkv_w, bias, cos, sin, heads)
    tail = shift(kv, "dp", 1)
    ffn_own = jnp.concatenate([up_weight, down_weight.T, output_weight.T, no_cols], axis=1)
    ffn_w, _ = gather_dp(ffn_own, mixed_order, [qkv_parts[-2]] + [qkv_w] * (bits - 2) + [kv])
    normed, g, branch, back, do, ffn_grad, ffn_sums = ffn(hids, gs, gains[2:], ffn_w, up_bias[None], heads)
    spots = t[None]
    attn_args = (spots, first, start, tail, kv, q, do, cos, sin, blk)
    *early, dtail_low, carry = attention(*attn_args)
    ahead_low = shift(dtail_low, "dp", -1)
    o, dq, dtail_high, dkv_low, dkv_high = attention(*attn_args, early=(carry, *early))
    ahead_high = shift(dtail_high, "dp", -1)
    post_args = (dq, cos, sin, normed, mixer_in, back, mixer_gain[None], qkv_w)
    early = post(0, spots, dkv_low, ahead_low, *post_args, early=(ffn_sums,))
    ffn_order = mixed_order[::-1]
    branch, mid_grad = mid(after(o, early[2]), dq, mixer_in, g, branch, ffn_w[:, 2 * F :])
    branch_own, branch_far = scatter_core(branch, blk)
    ffn_grads, ffn_parts, _ = scatter_dp(ffn_grad, chunk, ffn_order, [tail, branch])
    ahead_high = after(ahead_high, branch_far)
    hat, mix_grad, sums = post(1, spots, dkv_high, ahead_high, *post_args, early=(*early, mid_grad))
    hat_own, hat_far = scatter_core(hat, blk)
    summed = branch_own + swap(branch_far, "tensor", 2).astype(f32)
    result = hidden_in.astype(f32) + summed + out_bias
    hat_far = after(hat_far, summed)
    grad_hat = hat_own + swap(hat_far, "tensor", 2).astype(f32)
    mix_grads, _, sums = scatter_dp(mix_grad, chunk, down_order[::-1], [ffn_parts[1], hat_far, grad_hat], sums)
    own, inv_std = normalize(hidden_in.astype(f32))
    first_mean = jnp.mean(grad_hat, axis=-1, keepdims=True)
    second_mean = jnp.mean(grad_hat * own, axis=-1, keepdims=True)
    grad_hidden = out_grad.astype(f32) + inv_std * (grad_hat - first_mean - own * second_mean)
    norm_sums = sum_over(sums, "tensor")
    head_sums = sums[2, : 2 * W].reshape(heads, 2, HD)[:, 1].reshape(W)
    pair_grad = jnp.stack([sums[2, 2 * W : 3 * W], head_sums])
    kv_grads = mix_grads[:, : 2 * W].reshape(chunk, heads, 2, HD)
    triple_grad = jnp.stack(
        [mix_grads[:, 2 * W : 3 * W], kv_grads[:, :, 0].reshape(chunk, W), kv_grads[:, :, 1].reshape(chunk, W)], axis=1
    )
    return (
        result,
        grad_hidden,
        norm_sums[0],
        norm_sums[1],
        norm_sums[3],
        norm_sums[4],
        triple_grad,
        pair_grad,
        mix_grads[:, 3 * W :].T,
        ffn_grads[:, :F],
        sums[5],
        ffn_grads[:, F:].T,
        norm_sums[6],
    )


def solution(mesh):
    rows = P(("dp", "tensor"), None)
    in_specs = (
        rows, P("dp"), P(), P(), P(), P(), P("dp", None, "tensor"), P(None, "tensor"), P("tensor", "dp"),
        P("dp", "tensor"), P("tensor"), P("tensor", "dp"), P(), rows,
    )
    out_specs = (
        rows, rows, P(), P(), P(), P(), P("dp", None, "tensor"), P(None, "tensor"), P("tensor", "dp"),
        P("dp", "tensor"), P("tensor"), P("tensor", "dp"), P(),
    )
    return jax.shard_map(shards, mesh=mesh, in_specs=in_specs, out_specs=out_specs, check_vma=False)
```

profile of v0, /device:TPU:0, one launch (start us, length us, event | category | flops | bytes accessed | tf_op | source)
XLA Modules:
  0.0 309.4 jit_solution(16370854318339195133)
XLA Ops:
  2.1 4.1 %collective-permute-start.3 = (bf16[96,640]{1,0:T(8,128)(2,1)S(1)}, bf16[96,640]{1,0:T(8,128)(2,1)S(1)}, u32[]{:S(2)}, u32[]{:S(2)}) collective-permute-start(bf16[96,640]{1,0:T(8,128)(2,1)S(1)} %pad_maximum_fusion.12), channel_id=1, source_target_pairs={{0,16},{4,20},{8,24},{12,28},{16,0},{20,4},{24,8},{28,12},{1,17},{... | collective-permute-start | bytes 368648 | tf_op jit(solution)/shard_map/ppermute | solution.py:38
  6.1 6.0 %collective-permute-done.3 = bf16[96,640]{1,0:T(8,128)(2,1)S(1)} collective-permute-done((bf16[96,640]{1,0:T(8,128)(2,1)S(1)}, bf16[96,640]{1,0:T(8,128)(2,1)S(1)}, u32[]{:S(2)}, u32[]{:S(2)}) %collective-permute-start.3) | collective-permute-done | bytes 122912 | tf_op jit(solution)/shard_map/ppermute | solution.py:38
  14.6 4.9 %collective-permute-done.4 = bf16[192,640]{1,0:T(8,128)(2,1)S(1)} collective-permute-done((bf16[192,640]{1,0:T(8,128)(2,1)S(1)}, bf16[192,640]{1,0:T(8,128)(2,1)S(1)}, u32[]{:S(2)}, u32[]{:S(2)}) %collective-permute-start.4) | collective-permute-done | bytes 245792 | tf_op jit(solution)/shard_map/ppermute | solution.py:38
  22.5 3.3 %collective-permute-start.10 = (bf16[96,1792]{1,0:T(8,128)(2,1)S(1)}, bf16[96,1792]{1,0:T(8,128)(2,1)S(1)}, u32[]{:S(2)}, u32[]{:S(2)}) collective-permute-start(bf16[96,1792]{1,0:T(8,128)(2,1)S(1)} %concatenate.65), channel_id=1, source_target_pairs={{0,16},{4,20},{8,24},{12,28},{16,0},{20,4},{24,8},{28,12},{1,17},{... | collective-permute-start | bytes 1032200 | tf_op jit(solution)/shard_map/ppermute | solution.py:38
  25.8 6.4 %collective-permute-done.1.refs_2_ = bf16[512,768]{1,0:T(8,128)(2,1)S(1)} collective-permute-done((bf16[512,768]{1,0:T(8,128)(2,1)S(1)}, bf16[512,768]{1,0:T(8,128)(2,1)S(1)}, u32[]{:S(2)}, u32[]{:S(2)}) %collective-permute-start.1) | collective-permute-done | bytes 786464 | tf_op jit(solution)/shard_map/ppermute | solution.py:38
  34.9 5.8 %collective-permute-done.10 = bf16[96,1792]{1,0:T(8,128)(2,1)S(1)} collective-permute-done((bf16[96,1792]{1,0:T(8,128)(2,1)S(1)}, bf16[96,1792]{1,0:T(8,128)(2,1)S(1)}, u32[]{:S(2)}, u32[]{:S(2)}) %collective-permute-start.10) | collective-permute-done | bytes 344096 | tf_op jit(solution)/shard_map/ppermute | solution.py:38
  44.8 10.7 %pre.1 = (bf16[2048,768]{1,0:T(8,128)(2,1)}, bf16[3,2048,128]{2,1,0:T(8,128)(2,1)}, bf16[3,2048,128]{2,1,0:T(8,128)(2,1)}) custom-call(bf16[512,768]{1,0:T(8,128)(2,1)} %refs_0_.3, bf16[512,768]{1,0:T(8,128)(2,1)} %copy-done.7, bf16[512,768]{1,0:T(8,128)(2,1)} %copy-done.6, bf16[512,768]{1,0:T(8,128)(2,1)} %copy-done.8, ...), custom_call_target="tpu_custom_call" | custom-call | flops 1000 | bytes 1000 | tf_op jit(solution)/shard_map/pre/pallas_call | solution.py:196
  55.5 1.7 collective-permute-done.11
  61.9 2.7 collective-permute-start.6
  65.2 12.5 %collective-permute-done.8.refs_6_ = bf16[512,768]{1,0:T(8,128)(2,1)} collective-permute-done((bf16[512,768]{1,0:T(8,128)(2,1)}, bf16[512,768]{1,0:T(8,128)(2,1)}, u32[]{:S(2)}, u32[]{:S(2)}) %collective-permute-start.8) | collective-permute-done | bytes 786464 | tf_op jit(solution)/shard_map/ppermute | solution.py:38
  77.8 11.0 %collective-permute-done.12 = bf16[384,1792]{1,0:T(8,128)(2,1)} collective-permute-done((bf16[384,1792]{1,0:T(8,128)(2,1)S(1)}, bf16[384,1792]{1,0:T(8,128)(2,1)}, u32[]{:S(2)}, u32[]{:S(2)}) %collective-permute-start.12) | collective-permute-done | bytes 1376288 | tf_op jit(solution)/shard_map/ppermute | solution.py:38
  92.3 30.6 %ffn.1 = (bf16[2048,768]{1,0:T(8,128)(2,1)}, bf16[2048,768]{1,0:T(8,128)(2,1)}, bf16[2048,768]{1,0:T(8,128)(2,1)}, bf16[2048,768]{1,0:T(8,128)(2,1)}, bf16[3,204...) custom-call(bf16[512,768]{1,0:T(8,128)(2,1)} %refs_0_.3, bf16[512,768]{1,0:T(8,128)(2,1)} %copy-done.7, ...), custom_call_target="tpu_custom_call" | custom-call | flops 1000 | bytes 1000 | tf_op jit(solution)/shard_map/ffn/pallas_call | solution.py:277
  122.8 1.8 broadcast_select_fusion.1
  124.6 1.8 collective-permute-start.19
  127.0 13.7 %attn.2 = (bf16[192,1024]{1,0:T(8,128)(2,1)}, bf16[192,1024]{1,0:T(8,128)(2,1)}, bf16[3,1024,128]{2,1,0:T(8,128)(2,1)}, f32[3,2048,128]{2,1,0:T(8,128)}) custom-call(s32[1]{0:T(128)} %bitcast.refs_0_.place_ref, s32[8]{0:T(128)} %and_select_fusion.refs_1_, s32[1,2048]{1,0:T(1,128)} %add_subtract_fusion.refs_2_, bf16[3,2048,128]{2,1,0:T(8,128)(2,1)} %copy-done.4, ...), custom_call_target="tpu_custom_call" | custom-call | flops 1000 | bytes 1000 | tf_op jit(solution)/shard_map/attn/pallas_call | solution.py:428
  142.2 1.8 slice.238.w_ref
  144.0 27.1 %attn.3 = (bf16[192,2048]{1,0:T(8,128)(2,1)}, bf16[192,2048]{1,0:T(8,128)(2,1)}, bf16[3,1024,128]{2,1,0:T(8,128)(2,1)}, f32[3,1024,128]{2,1,0:T(8,128)}, f32[3,1024,128]{2,1,0:T(8,128)}) custom-call(s32[1]{0:T(128)} %bitcast.refs_0_.place_ref, s32[8]{0:T(128)} %and_select_fusion.refs_1_, s32[1,2048]{1,0:T(1,128)} %add_subtract_fusion.refs_2_, ...), custom_call_target="tpu_custom_call" | custom-call | flops 1000 | bytes 1000 | tf_op jit(solution)/shard_map/attn/pallas_call | solution.py:428
  172.0 7.8 %post.2 = (bf16[2048,768]{1,0:T(8,128)(2,1)}, f32[768,384]{1,0:T(8,128)}, f32[8,768]{1,0:T(8,128)}) custom-call(s32[1]{0:T(128)} %bitcast.refs_0_.place_ref, f32[3,1024,128]{2,1,0:T(8,128)} %get-tuple-element.63.dkv_ref, bf16[3,1024,128]{2,1,0:T(8,128)(2,1)} %copy-done.10, bf16[192,2048]{1,0:T(8,128)(2,1)} %get-tuple-element.65.dq_ref, ...), custom_call_target="tpu_custom_call" | custom-call | flops 1000 | bytes 1000 | tf_op jit(solution)/shard_map/post/pallas_call | solution.py:548
  179.8 9.0 %mid.1 = (bf16[2048,768]{1,0:T(8,128)(2,1)}, bf16[768,384]{1,0:T(8,128)(2,1)}) custom-call(bf16[192,2048]{1,0:T(8,128)(2,1)} %get-tuple-element.71.o_ref, bf16[192,2048]{1,0:T(8,128)(2,1)} %get-tuple-element.65.dq_ref, bf16[2048,768]{1,0:T(8,128)(2,1)} %get-tuple-element.67.mixer_ref, bf16[2048,768]{1,0:T(8,128)(2,1)} %get-tuple-element.72.g_ref, ...), custom_call_target="tpu_custom_call" | custom-call | flops 1000 | bytes 1000 | tf_op jit(solution)/shard_map/mid/pallas_call | solution.py:471
  191.2 12.8 %collective-permute-done.20 = bf16[192,1536]{1,0:T(8,128)(2,1)S(1)} collective-permute-done((bf16[192,1536]{1,0:T(8,128)(2,1)S(1)}, bf16[192,1536]{1,0:T(8,128)(2,1)S(1)}, u32[]{:S(2)}, u32[]{:S(2)}) %collective-permute-start.20) | collective-permute-done | bytes 589856 | tf_op jit(solution)/shard_map/ppermute | solution.py:38
  204.2 7.1 %collective-permute-start.26 = (bf16[96,1536]{1,0:T(8,128)(2,1)S(1)}, bf16[96,1536]{1,0:T(8,128)(2,1)S(1)}, u32[]{:S(2)}, u32[]{:S(2)}) collective-permute-start(bf16[96,1536]{1,0:T(8,128)(2,1)S(1)} %fusion.16), channel_id=1, source_target_pairs={{0,16},{4,20},{8,24},{12,28},{16,0},{20,4},{24,8},{28,12},{1,17},{... | collective-permute-start | bytes 884744 | tf_op jit(solution)/shard_map/ppermute | solution.py:38
  213.1 10.9 %collective-permute-done.26 = bf16[96,1536]{1,0:T(8,128)(2,1)S(1)} collective-permute-done((bf16[96,1536]{1,0:T(8,128)(2,1)S(1)}, bf16[96,1536]{1,0:T(8,128)(2,1)S(1)}, u32[]{:S(2)}, u32[]{:S(2)}) %collective-permute-start.26) | collective-permute-done | bytes 294944 | tf_op jit(solution)/shard_map/ppermute | solution.py:38
  227.0 2.3 collective-permute-done.16.ahead_ref
  229.3 8.4 %post.3 = (bf16[2048,768]{1,0:T(8,128)(2,1)}, bf16[768,768]{1,0:T(8,128)(2,1)}, f32[8,768]{1,0:T(8,128)}) custom-call(s32[1]{0:T(128)} %bitcast.refs_0_.place_ref, f32[3,1024,128]{2,1,0:T(8,128)} %get-tuple-element.75.dkv_ref, bf16[3,1024,128]{2,1,0:T(8,128)(2,1)} %collective-permute-done.16.ahead_ref, ...), custom_call_target="tpu_custom_call", output_to_operand_aliasing={{0}: (11, {})} | custom-call | flops 1000 | bytes 1000 | tf_op jit(solution)/shard_map/post/pallas_call | solution.py:548
  239.2 6.6 %collective-permute-start.21 = (bf16[400,768]{1,0:T(8,128)(2,1)S(1)}, bf16[400,768]{1,0:T(8,128)(2,1)S(1)}, u32[]{:S(2)}, u32[]{:S(2)}) collective-permute-start(bf16[400,768]{1,0:T(8,128)(2,1)S(1)} %pad_maximum_fusion.6), channel_id=1, source_target_pairs={{0,4},{4,0},{8,12},{12,8},{16,20},{20,16},{24,28},{28,24},{1,5},{5... | collective-permute-start | bytes 1843208 | tf_op jit(solution)/shard_map/ppermute | solution.py:38
  248.5 7.8 %collective-permute-done.21 = bf16[400,768]{1,0:T(8,128)(2,1)S(1)} collective-permute-done((bf16[400,768]{1,0:T(8,128)(2,1)S(1)}, bf16[400,768]{1,0:T(8,128)(2,1)S(1)}, u32[]{:S(2)}, u32[]{:S(2)}) %collective-permute-start.21) | collective-permute-done | bytes 614432 | tf_op jit(solution)/shard_map/ppermute | solution.py:38
  256.7 10.2 %collective-permute-done.15 = bf16[512,768]{1,0:T(8,128)(2,1)S(1)} collective-permute-done((bf16[512,768]{1,0:T(8,128)(2,1)S(1)}, bf16[512,768]{1,0:T(8,128)(2,1)S(1)}, u32[]{:S(2)}, u32[]{:S(2)}) %collective-permute-start.15) | collective-permute-done | bytes 786464 | tf_op jit(solution)/shard_map/ppermute | solution.py:38
  269.0 4.7 %collective-permute-start.22 = (bf16[208,768]{1,0:T(8,128)(2,1)S(1)}, bf16[208,768]{1,0:T(8,128)(2,1)S(1)}, u32[]{:S(2)}, u32[]{:S(2)}) collective-permute-start(bf16[208,768]{1,0:T(8,128)(2,1)S(1)} %pad_maximum_fusion.8), channel_id=1, source_target_pairs={{0,8},{4,12},{8,0},{12,4},{16,24},{20,28},{24,16},{28,20},{1,9},{5... | collective-permute-start | bytes 958472 | tf_op jit(solution)/shard_map/ppermute | solution.py:38
  275.4 5.7 %collective-permute-done.22 = bf16[208,768]{1,0:T(8,128)(2,1)S(1)} collective-permute-done((bf16[208,768]{1,0:T(8,128)(2,1)S(1)}, bf16[208,768]{1,0:T(8,128)(2,1)S(1)}, u32[]{:S(2)}, u32[]{:S(2)}) %collective-permute-start.22) | collective-permute-done | bytes 319520 | tf_op jit(solution)/shard_map/ppermute | solution.py:38
  281.3 11.4 %collective-permute-done.18 = bf16[512,768]{1,0:T(8,128)(2,1)S(1)} collective-permute-done((bf16[512,768]{1,0:T(8,128)(2,1)S(1)}, bf16[512,768]{1,0:T(8,128)(2,1)S(1)}, u32[]{:S(2)}, u32[]{:S(2)}) %collective-permute-start.18) | collective-permute-done | bytes 786464 | tf_op jit(solution)/shard_map/ppermute | solution.py:38
  293.5 2.9 fusion.7
  296.4 6.4 %collective-permute-done.23 = bf16[112,768]{1,0:T(8,128)(2,1)S(1)} collective-permute-done((bf16[112,768]{1,0:T(8,128)(2,1)S(1)}, bf16[112,768]{1,0:T(8,128)(2,1)S(1)}, u32[]{:S(2)}, u32[]{:S(2)}) %collective-permute-start.23) | collective-permute-done | bytes 172064 | tf_op jit(solution)/shard_map/ppermute | solution.py:38
  (182 shorter events, 48.3 us)
Async XLA Ops:
  0.6 12.4 %copy-start = (bf16[512,768]{1,0:T(8,128)(2,1)S(1)}, bf16[512,768]{1,0:T(8,128)(2,1)}, u32[]{:S(2)}) copy-start(bf16[512,768]{1,0:T(8,128)(2,1)} %refs_0_.3) | copy-start | bytes 2359300
  2.1 10.0 %collective-permute-start.3 = (bf16[96,640]{1,0:T(8,128)(2,1)S(1)}, bf16[96,640]{1,0:T(8,128)(2,1)S(1)}, u32[]{:S(2)}, u32[]{:S(2)}) collective-permute-start(bf16[96,640]{1,0:T(8,128)(2,1)S(1)} %pad_maximum_fusion.12), channel_id=1, source_target_pairs={{0,16},{4,20},{8,24},{12,28},{16,0},{20,4},{24,8},{28,12},{1,17},{... | collective-permute-start | bytes 368648 | tf_op jit(solution)/shard_map/ppermute | solution.py:38
  12.3 9.0 %copy-start.11 = (bf16[96,768]{1,0:T(8,128)(2,1)S(1)}, bf16[96,768]{1,0:T(8,128)(2,1)}, u32[]{:S(2)}) copy-start(bf16[96,768]{1,0:T(8,128)(2,1)} %param.23) | copy-start | bytes 442372
  12.3 7.2 %collective-permute-start.4 = (bf16[192,640]{1,0:T(8,128)(2,1)S(1)}, bf16[192,640]{1,0:T(8,128)(2,1)S(1)}, u32[]{:S(2)}, u32[]{:S(2)}) collective-permute-start(bf16[192,640]{1,0:T(8,128)(2,1)S(1)} %bitcast.146), channel_id=1, source_target_pairs={{0,8},{4,12},{8,0},{12,4},{16,24},{20,28},{24,16},{28,20},{1,9},{5... | collective-permute-start | bytes 737288 | tf_op jit(solution)/shard_map/ppermute | solution.py:38
  13.1 19.2 %collective-permute-start.1 = (bf16[512,768]{1,0:T(8,128)(2,1)S(1)}, bf16[512,768]{1,0:T(8,128)(2,1)S(1)}, u32[]{:S(2)}, u32[]{:S(2)}) collective-permute-start(bf16[512,768]{1,0:T(8,128)(2,1)S(1)} %copy-done), channel_id=1, source_target_pairs={{0,2},{1,3},{2,0},{3,1},{4,6},{5,7},{6,4},{7,5},{8,10},{9,11},{10,... | collective-permute-start | bytes 2359304 | tf_op jit(solution)/shard_map/ppermute | solution.py:38
  14.5 29.1 %collective-permute-start = (bf16[512,768]{1,0:T(8,128)(2,1)S(1)}, bf16[512,768]{1,0:T(8,128)(2,1)S(1)}, u32[]{:S(2)}, u32[]{:S(2)}) collective-permute-start(bf16[512,768]{1,0:T(8,128)(2,1)S(1)} %copy-done), channel_id=1, source_target_pairs={{0,1},{1,0},{2,3},{3,2},{4,5},{5,4},{6,7},{7,6},{8,9},{9,8},{10,11... | collective-permute-start | bytes 2359304 | tf_op jit(solution)/shard_map/ppermute | solution.py:38
  19.7 12.6 %collective-permute-start.5 = (bf16[384,640]{1,0:T(8,128)(2,1)S(1)}, bf16[384,640]{1,0:T(8,128)(2,1)}, u32[]{:S(2)}, u32[]{:S(2)}) collective-permute-start(bf16[384,640]{1,0:T(8,128)(2,1)S(1)} %bitcast.134), channel_id=1, source_target_pairs={{0,4},{4,0},{8,12},{12,8},{16,20},{20,16},{24,28},{28,24},{1,5},{5... | collective-permute-start | bytes 1474568 | tf_op jit(solution)/shard_map/ppermute | solution.py:38
  22.5 18.2 %collective-permute-start.10 = (bf16[96,1792]{1,0:T(8,128)(2,1)S(1)}, bf16[96,1792]{1,0:T(8,128)(2,1)S(1)}, u32[]{:S(2)}, u32[]{:S(2)}) collective-permute-start(bf16[96,1792]{1,0:T(8,128)(2,1)S(1)} %concatenate.65), channel_id=1, source_target_pairs={{0,16},{4,20},{8,24},{12,28},{16,0},{20,4},{24,8},{28,12},{1,17},{... | collective-permute-start | bytes 1032200 | tf_op jit(solution)/shard_map/ppermute | solution.py:38
  32.2 11.4 %collective-permute-start.2 = (bf16[512,768]{1,0:T(8,128)(2,1)S(1)}, bf16[512,768]{1,0:T(8,128)(2,1)S(1)}, u32[]{:S(2)}, u32[]{:S(2)}) collective-permute-start(bf16[512,768]{1,0:T(8,128)(2,1)S(1)} %collective-permute-done.1.refs_2_), channel_id=1, source_target_pairs={{0,1},{1,0},{2,3},{3,2},{4,5},{5,4},{6,7},{7,6},{8,9},{9,8},{10,11... | collective-permute-start | bytes 2359304 | tf_op jit(solution)/shard_map/ppermute | solution.py:38
  40.8 16.5 %collective-permute-start.11 = (bf16[192,1792]{1,0:T(8,128)(2,1)S(1)}, bf16[192,1792]{1,0:T(8,128)(2,1)S(1)}, u32[]{:S(2)}, u32[]{:S(2)}) collective-permute-start(bf16[192,1792]{1,0:T(8,128)(2,1)S(1)} %bitcast.140), channel_id=1, source_target_pairs={{0,4},{4,0},{8,12},{12,8},{16,20},{20,16},{24,28},{28,24},{1,5},{5... | collective-permute-start | bytes 2064392 | tf_op jit(solution)/shard_map/ppermute | solution.py:38
  42.0 13.6 %copy-start.13 = (f32[1,768]{1,0:T(1,128)}, f32[1,768]{1,0:T(1,128)S(1)}, u32[]{:S(2)}) copy-start(f32[1,768]{1,0:T(1,128)S(1)} %stack.64.gain_ref) | copy-start | bytes 9220
  57.5 31.2 %collective-permute-start.12 = (bf16[384,1792]{1,0:T(8,128)(2,1)S(1)}, bf16[384,1792]{1,0:T(8,128)(2,1)}, u32[]{:S(2)}, u32[]{:S(2)}) collective-permute-start(bf16[384,1792]{1,0:T(8,128)(2,1)S(1)} %bitcast.129), channel_id=1, source_target_pairs={{0,8},{4,12},{8,0},{12,4},{16,24},{20,28},{24,16},{28,20},{1,9},{5... | collective-permute-start | bytes 4128776 | tf_op jit(solution)/shard_map/ppermute | solution.py:38
  59.2 18.6 %collective-permute-start.8 = (bf16[512,768]{1,0:T(8,128)(2,1)}, bf16[512,768]{1,0:T(8,128)(2,1)}, u32[]{:S(2)}, u32[]{:S(2)}) collective-permute-start(bf16[512,768]{1,0:T(8,128)(2,1)} %refs_4_), channel_id=1, source_target_pairs={{0,2},{1,3},{2,0},{3,1},{4,6},{5,7},{6,4},{7,5},{8,10},{9,11},{10,... | collective-permute-start | bytes 2359304 | tf_op jit(solution)/shard_map/ppermute | solution.py:38
  61.9 62.7 %collective-permute-start.6 = (bf16[3,2048,128]{2,1,0:T(8,128)(2,1)S(1)}, bf16[3,2048,128]{2,1,0:T(8,128)(2,1)S(1)}, u32[]{:S(2)}, u32[]{:S(2)}) collective-permute-start(bf16[3,2048,128]{2,1,0:T(8,128)(2,1)S(1)} %copy-done.3), channel_id=1, source_target_pairs={{0,4},{4,8},{8,12},{12,16},{16,20},{20,24},{24,28},{1,5},{5,9},{9,... | collective-permute-start | bytes 4718600 | tf_op jit(solution)/shard_map/ppermute | solution.py:44
  65.2 27.0 %collective-permute-start.7 = (bf16[512,768]{1,0:T(8,128)(2,1)}, bf16[512,768]{1,0:T(8,128)(2,1)}, u32[]{:S(2)}, u32[]{:S(2)}) collective-permute-start(bf16[512,768]{1,0:T(8,128)(2,1)} %refs_4_), channel_id=1, source_target_pairs={{0,1},{1,0},{2,3},{3,2},{4,5},{5,4},{6,7},{7,6},{8,9},{9,8},{10,11... | collective-permute-start | bytes 2359304 | tf_op jit(solution)/shard_map/ppermute | solution.py:38
  77.8 14.5 %collective-permute-start.9 = (bf16[512,768]{1,0:T(8,128)(2,1)}, bf16[512,768]{1,0:T(8,128)(2,1)}, u32[]{:S(2)}, u32[]{:S(2)}) collective-permute-start(bf16[512,768]{1,0:T(8,128)(2,1)} %collective-permute-done.8.refs_6_), channel_id=1, source_target_pairs={{0,1},{1,0},{2,3},{3,2},{4,5},{5,4},{6,7},{7,6},{8,9},{9,8},{10,11... | collective-permute-start | bytes 2359304 | tf_op jit(solution)/shard_map/ppermute | solution.py:38
  124.6 65.6 %collective-permute-start.19 = (bf16[384,1536]{1,0:T(8,128)(2,1)S(1)}, bf16[384,1536]{1,0:T(8,128)(2,1)S(1)}, u32[]{:S(2)}, u32[]{:S(2)}) collective-permute-start(bf16[384,1536]{1,0:T(8,128)(2,1)S(1)} %bitcast.135), channel_id=1, source_target_pairs={{0,8},{4,12},{8,0},{12,4},{16,24},{20,28},{24,16},{28,20},{1,9},{5... | collective-permute-start | bytes 3538952 | tf_op jit(solution)/shard_map/ppermute | solution.py:38
  140.7 30.4 %collective-permute-start.13 = (bf16[3,1024,128]{2,1,0:T(8,128)(2,1)}, bf16[3,1024,128]{2,1,0:T(8,128)(2,1)S(1)}, u32[]{:S(2)}, u32[]{:S(2)}) collective-permute-start(bf16[3,1024,128]{2,1,0:T(8,128)(2,1)} %get-tuple-element.64), channel_id=1, source_target_pairs={{4,0},{8,4},{12,8},{16,12},{20,16},{24,20},{28,24},{5,1},{9,5},{13... | collective-permute-start | bytes 2359304 | tf_op jit(solution)/shard_map/ppermute | solution.py:44
  190.8 13.2 %collective-permute-start.20 = (bf16[192,1536]{1,0:T(8,128)(2,1)S(1)}, bf16[192,1536]{1,0:T(8,128)(2,1)S(1)}, u32[]{:S(2)}, u32[]{:S(2)}) collective-permute-start(bf16[192,1536]{1,0:T(8,128)(2,1)S(1)} %bitcast.141), channel_id=1, source_target_pairs={{0,4},{4,0},{8,12},{12,8},{16,20},{20,16},{24,28},{28,24},{1,5},{5... | collective-permute-start | bytes 1769480 | tf_op jit(solution)/shard_map/ppermute | solution.py:38
  191.0 33.0 %collective-permute-start.14 = (bf16[1024,768]{1,0:T(8,128)(2,1)S(1)}, bf16[1024,768]{1,0:T(8,128)(2,1)S(1)}, u32[]{:S(2)}, u32[]{:S(2)}) collective-permute-start(bf16[1024,768]{1,0:T(8,128)(2,1)S(1)} %pad_maximum_fusion.1), channel_id=1, source_target_pairs={{0,1},{1,0},{2,3},{3,2},{4,5},{5,4},{6,7},{7,6},{8,9},{9,8},{10,11... | collective-permute-start | bytes 4718600 | tf_op jit(solution)/shard_map/ppermute | solution.py:38
  191.2 20.1 %copy-start.1 = (bf16[512,768]{1,0:T(8,128)(2,1)S(1)}, bf16[512,768]{1,0:T(8,128)(2,1)}, u32[]{:S(2)}) copy-start(bf16[512,768]{1,0:T(8,128)(2,1)} %refs_0_.3) | copy-start | bytes 2359300
  204.2 19.7 %collective-permute-start.26 = (bf16[96,1536]{1,0:T(8,128)(2,1)S(1)}, bf16[96,1536]{1,0:T(8,128)(2,1)S(1)}, u32[]{:S(2)}, u32[]{:S(2)}) collective-permute-start(bf16[96,1536]{1,0:T(8,128)(2,1)S(1)} %fusion.16), channel_id=1, source_target_pairs={{0,16},{4,20},{8,24},{12,28},{16,0},{20,4},{24,8},{28,12},{1,17},{... | collective-permute-start | bytes 884744 | tf_op jit(solution)/shard_map/ppermute | solution.py:38
  211.5 17.8 %collective-permute-start.16 = (bf16[3,1024,128]{2,1,0:T(8,128)(2,1)S(1)}, bf16[3,1024,128]{2,1,0:T(8,128)(2,1)}, u32[]{:S(2)}, u32[]{:S(2)}) collective-permute-start(bf16[3,1024,128]{2,1,0:T(8,128)(2,1)S(1)} %copy-done.23), channel_id=1, source_target_pairs={{4,0},{8,4},{12,8},{16,12},{20,16},{24,20},{28,24},{5,1},{9,5},{13... | collective-permute-start | bytes 2359304 | tf_op jit(solution)/shard_map/ppermute | solution.py:44
  239.2 17.2 %collective-permute-start.21 = (bf16[400,768]{1,0:T(8,128)(2,1)S(1)}, bf16[400,768]{1,0:T(8,128)(2,1)S(1)}, u32[]{:S(2)}, u32[]{:S(2)}) collective-permute-start(bf16[400,768]{1,0:T(8,128)(2,1)S(1)} %pad_maximum_fusion.6), channel_id=1, source_target_pairs={{0,4},{4,0},{8,12},{12,8},{16,20},{20,16},{24,28},{28,24},{1,5},{5... | collective-permute-start | bytes 1843208 | tf_op jit(solution)/shard_map/ppermute | solution.py:38
  246.0 22.6 %collective-permute-start.17 = (bf16[1024,768]{1,0:T(8,128)(2,1)S(1)}, bf16[1024,768]{1,0:T(8,128)(2,1)S(1)}, u32[]{:S(2)}, u32[]{:S(2)}) collective-permute-start(bf16[1024,768]{1,0:T(8,128)(2,1)S(1)} %pad_maximum_fusion.2), channel_id=1, source_target_pairs={{0,1},{1,0},{2,3},{3,2},{4,5},{5,4},{6,7},{7,6},{8,9},{9,8},{10,11... | collective-permute-start | bytes 4718600 | tf_op jit(solution)/shard_map/ppermute | solution.py:38
  247.0 19.9 %collective-permute-start.15 = (bf16[512,768]{1,0:T(8,128)(2,1)S(1)}, bf16[512,768]{1,0:T(8,128)(2,1)S(1)}, u32[]{:S(2)}, u32[]{:S(2)}) collective-permute-start(bf16[512,768]{1,0:T(8,128)(2,1)S(1)} %copy-done.9), channel_id=1, source_target_pairs={{0,2},{1,3},{2,0},{3,1},{4,6},{5,7},{6,4},{7,5},{8,10},{9,11},{10,... | collective-permute-start | bytes 2359304 | tf_op jit(solution)/shard_map/ppermute | solution.py:38
  256.5 10.4 %copy-start.21 = (f32[768]{0:T(1024)S(1)}, f32[768]{0:T(1024)}, u32[]{:S(2)}) copy-start(f32[768]{0:T(1024)} %param.26) | copy-start | bytes 9220
  269.0 12.1 %collective-permute-start.22 = (bf16[208,768]{1,0:T(8,128)(2,1)S(1)}, bf16[208,768]{1,0:T(8,128)(2,1)S(1)}, u32[]{:S(2)}, u32[]{:S(2)}) collective-permute-start(bf16[208,768]{1,0:T(8,128)(2,1)S(1)} %pad_maximum_fusion.8), channel_id=1, source_target_pairs={{0,8},{4,12},{8,0},{12,4},{16,24},{20,28},{24,16},{28,20},{1,9},{5... | collective-permute-start | bytes 958472 | tf_op jit(solution)/shard_map/ppermute | solution.py:38
  273.8 18.9 %collective-permute-start.18 = (bf16[512,768]{1,0:T(8,128)(2,1)S(1)}, bf16[512,768]{1,0:T(8,128)(2,1)S(1)}, u32[]{:S(2)}, u32[]{:S(2)}) collective-permute-start(bf16[512,768]{1,0:T(8,128)(2,1)S(1)} %fusion.10), channel_id=1, source_target_pairs={{0,2},{1,3},{2,0},{3,1},{4,6},{5,7},{6,4},{7,5},{8,10},{9,11},{10,... | collective-permute-start | bytes 2359304 | tf_op jit(solution)/shard_map/ppermute | solution.py:38
  293.4 9.4 %collective-permute-start.23 = (bf16[112,768]{1,0:T(8,128)(2,1)S(1)}, bf16[112,768]{1,0:T(8,128)(2,1)S(1)}, u32[]{:S(2)}, u32[]{:S(2)}) collective-permute-start(bf16[112,768]{1,0:T(8,128)(2,1)S(1)} %pad_maximum_fusion.11), channel_id=1, source_target_pairs={{0,16},{4,20},{8,24},{12,28},{16,0},{20,4},{24,8},{28,12},{1,17},{... | collective-permute-start | bytes 516104 | tf_op jit(solution)/shard_map/ppermute | solution.py:38
  303.5 1.4 collective-permute-start.24
  304.9 3.9 %collective-permute-start.25 = (f32[8,768]{1,0:T(8,128)S(1)}, f32[8,768]{1,0:T(8,128)S(1)}, u32[]{:S(2)}, u32[]{:S(2)}) collective-permute-start(f32[8,768]{1,0:T(8,128)S(1)} %add.157), channel_id=1, source_target_pairs={{0,2},{1,3},{2,0},{3,1},{4,6},{5,7},{6,4},{7,5},{8,10},{9,11},{10,... | collective-permute-start | bytes 73736 | tf_op jit(solution)/shard_map/ppermute | solution.py:38
  (19 other events, 83.8 us)
where the time goes:
time: 310 us; the launch traced here: 309 us
  waiting for transfers between devices  117 us (38%)
  Pallas kernels  107 us (35%)
  starting transfers between devices  45.5 us (15%)
  other arithmetic  21.1 us (7%)
  local copies, waits for them, and re-layouts  17.4 us (6%)
    ppermute x24, waiting for transfers between devices, swap(): return lax.ppermute(value, axis, [(i, i ^ mask) for i in range(count)])  114 us
    pallas_call x2, Pallas kernels, attention(): pl.pallas_call(functools.partial(attn_kernel, T=T, blk=blk, heads=heads,...  40.8 us
    ppermute x24, starting transfers between devices, swap(): return lax.ppermute(value, axis, [(i, i ^ mask) for i in range(count)])  39.8 us
    pallas_call x1, Pallas kernels, ffn(): pl.pallas_call(functools.partial(ffn_kernel, pieces=len(gs), blk=blk), gr...  30.6 us
    pallas_call x2, Pallas kernels, post(): pl.pallas_call(post_kernel, grid_spec=pltpu.PrefetchScalarGridSpec(num_sc...  16.2 us
    pallas_call x1, Pallas kernels, pre(): pl.pallas_call(functools.partial(pre_kernel, pieces=len(hids), blk=blk),...  10.7 us
    pallas_call x1, Pallas kernels, mid(): pl.pallas_call(mid_kernel, grid=(T // TR,), in_specs=[cols, cols, rows_sp...  9 us
  transfers between devices with their start and end apart: 27, of which 16 were waited for; matrix products, arithmetic and copies ran while one was open for 9% of the time, Pallas kernels for 32%

commit v1 on v0

--- a/solution.py
+++ b/solution.py
@@ -26,7 +26,10 @@
 TN = (((0,), (0,)), ((), ()))
 TT = (((0,), (1,)), ((), ()))
 VMEM_LIMIT = 56 * 2**20
-COST = pl.CostEstimate(flops=1000, bytes_accessed=1000, transcendentals=0)
+
+
+def cost(us):
+    return pl.CostEstimate(flops=int(us * 1.15e9), bytes_accessed=1000, transcendentals=0)
 
 
 def mm(left, right, dims=NN):
@@ -49,7 +52,7 @@
 
 
 def after(value, *others):
-    return lax.optimization_barrier((value, *others))[0]
+    return lax.optimization_barrier((value, others))[0]
 
 
 def gather_tensor(own):
@@ -96,30 +99,26 @@
     return first, lax.reduce_precision(sums - first, 8, 7)
 
 
-def scatter_dp(whole, rows, order, gates=(), sums=None):
-    me = lax.axis_index("dp")
-    cols = whole.shape[1]
-    left = sorted(order, reverse=True)
-    held = whole
-    parts = []
-    for n, bit in enumerate(order):
-        pairs = split(held, rows, left, bit)
-        high = ((me >> bit) & 1) == 1
-        send = jnp.where(high, pairs[:, 0], pairs[:, 1]).astype(bf16).reshape(-1, cols)
-        keep = jnp.where(high, pairs[:, 1], pairs[:, 0]).astype(f32).reshape(-1, cols)
-        count = send.shape[0]
-        if sums is not None:
-            first, second = two_parts(sums)
-            send = jnp.concatenate([send, first.astype(bf16), second.astype(bf16)], axis=0)
-        if n < len(gates) and gates[n] is not None:
-            send = after(send, gates[n])
-        other = swap(send, "dp", 1 << bit).astype(f32)
-        held = keep + other[:count]
-        if sums is not None:
-            sums = (first + second) + (other[count : count + 8] + other[count + 8 :])
-        left.remove(bit)
-        parts.append(held)
-    return held, parts, sums
+def scatter_step(held, rows, left, bit, gate=None, landed=None, sums=None):
+    cols = held.shape[1]
+    pairs = split(held, rows, left, bit)
+    high = ((lax.axis_index("dp") >> bit) & 1) == 1
+    send = jnp.where(high, pairs[:, 0], pairs[:, 1]).astype(bf16).reshape(-1, cols)
+    keep = jnp.where(high, pairs[:, 1], pairs[:, 0]).astype(f32).reshape(-1, cols)
+    count = send.shape[0]
+    if sums is not None:
+        first, second = two_parts(sums)
+        send = jnp.concatenate([send, first.astype(bf16), second.astype(bf16)], axis=0)
+    if gate is not None:
+        send = after(send, gate)
+    other = swap(send, "dp", 1 << bit)
+    if landed is not None:
+        other = after(other, landed)
+    other = other.astype(f32)
+    held = keep + other[:count]
+    if sums is None:
+        return held
+    return held, (first + second) + (other[count : count + 8] + other[count + 8 :])
 
 
 def sum_over(value, axis):
@@ -206,7 +205,7 @@
         out_specs=[rows_spec(D)] + [heads_spec(heads)] * 2,
         out_shape=[jax.ShapeDtypeStruct((T, D), bf16)] + [jax.ShapeDtypeStruct((heads, T, 128), bf16)] * 2,
         compiler_params=pltpu.CompilerParams(vmem_limit_bytes=VMEM_LIMIT),
-        cost_estimate=COST,
+        cost_estimate=cost(0.5),
         name="pre",
     )(*hids, gains, w, bias, cos, sin)
 
@@ -222,7 +221,7 @@
 
 def ffn_kernel(*refs, pieces, blk):
     hids, gs, refs = refs[:pieces], refs[pieces : 2 * pieces], refs[2 * pieces :]
-    gains_ref, w_ref, bias_ref, normed_ref, g_ref, branch_ref, back_ref, do_ref, grad_ref, sums_ref, acc_ref = refs
+    gains_ref, up_ref, down_ref, bias_ref, normed_ref, g_ref, branch_ref, back_ref, do_ref, grad_ref, sums_ref, acc_ref = refs
     heads = do_ref.shape[0]
     F = bias_ref.shape[1]
     step = pl.program_id(0)
@@ -231,7 +230,7 @@
     feed = (normed * gains_ref[0:1] + gains_ref[1:2]).astype(bf16)
     g = pick(gs, blk)
     g_ref[...] = g
-    up, down = w_ref[:, :F], w_ref[:, F : 2 * F]
+    up, down = up_ref[...], down_ref[:, :F]
     hidden = mm(feed, up) + bias_ref[...]
     cumulative, density = gelu_parts(hidden)
     act = (hidden * cumulative).astype(bf16)
@@ -259,7 +258,7 @@
     def _():
         grad_ref[...] = acc_ref[...].astype(bf16)
 
-    do = mm(g, w_ref[:, 2 * F :])
+    do = mm(g, down_ref[:, F:])
     lane = lax.broadcasted_iota(jnp.int32, (FR, 128), 1)
     for h in range(heads):
         at = (h // 2) * 128
@@ -269,7 +268,7 @@
         do_ref[h] = jnp.where(lane < HD, 0.0, x).astype(bf16)
 
 
-def ffn(hids, gs, gains, w, bias, heads):
+def ffn(hids, gs, gains, up, down, bias, heads):
     blk, D = gs[0].shape
     T = blk * len(gs)
     F = bias.shape[1]
@@ -277,7 +276,8 @@
     return pl.pallas_call(
         functools.partial(ffn_kernel, pieces=len(gs), blk=blk),
         grid=(T // FR,),
-        in_specs=piece_specs(len(gs), blk, D, FR) * 2 + [whole_spec(gains.shape), whole_spec(w.shape), whole_spec(bias.shape)],
+        in_specs=piece_specs(len(gs), blk, D, FR) * 2
+        + [whole_spec(array.shape) for array in (gains, up, down, bias)],
         out_specs=[rows] * 4 + [heads_spec(heads, 128, FR), whole_spec((D, 2 * F)), whole_spec((8, D))],
         out_shape=[jax.ShapeDtypeStruct((T, D), bf16)] * 4
         + [
@@ -287,9 +287,9 @@
         ],
         scratch_shapes=[pltpu.VMEM((D, 2 * F), f32)],
         compiler_params=pltpu.CompilerParams(vmem_limit_bytes=VMEM_LIMIT),
-        cost_estimate=COST,
+        cost_estimate=cost(0.5),
         name="ffn",
-    )(*hids, *gs, gains, w, bias)
+    )(*hids, *gs, gains, up, down, bias)
 
 
 def attn_kernel(*refs, T, blk, heads, late):
@@ -439,8 +439,8 @@
             pltpu.VMEM((heads, 2 * TQ, 128), bf16),
         ],
         out_shape=[jax.ShapeDtypeStruct(*out) for out in outs],
-        compiler_params=pltpu.CompilerParams(vmem_limit_bytes=VMEM_LIMIT),
-        cost_estimate=COST,
+        compiler_params=pltpu.CompilerParams(vmem_limit_bytes=40 * 2**20),
+        cost_estimate=cost(0.1),
         name="attn",
     )(place, first, start, tail, kv, q, do, cos, sin, *early)
 
@@ -476,7 +476,7 @@
         out_shape=[jax.ShapeDtypeStruct((T, D), bf16), jax.ShapeDtypeStruct((D, 2 * W), bf16)],
         scratch_shapes=[pltpu.VMEM((2 * W, D), f32)],
         compiler_params=pltpu.CompilerParams(vmem_limit_bytes=VMEM_LIMIT),
-        cost_estimate=COST,
+        cost_estimate=cost(9),
         name="mid",
     )(o, dq, mixer, g, branch, w)
 
@@ -561,7 +561,7 @@
         ],
         input_output_aliases={11: 0} if late else {},
         compiler_params=pltpu.CompilerParams(vmem_limit_bytes=VMEM_LIMIT),
-        cost_estimate=COST,
+        cost_estimate=cost(8),
         name="post",
     )(place, dkv, ahead, dq, cos, sin, normed, mixer, back, gain, w, *early)
 
@@ -603,35 +603,43 @@
     kv_bias = jnp.concatenate([jnp.zeros_like(v_bias), v_bias], axis=1).reshape(2 * W)
     bias = jnp.concatenate([kv_bias, pair_bias[0], jnp.zeros((pad,), f32)])[None]
     mixer_in, kv, q = pre(hids, gains, qkv_w, bias, cos, sin, heads)
-    tail = shift(kv, "dp", 1)
-    ffn_own = jnp.concatenate([up_weight, down_weight.T, output_weight.T, no_cols], axis=1)
-    ffn_w, _ = gather_dp(ffn_own, mixed_order, [qkv_parts[-2]] + [qkv_w] * (bits - 2) + [kv])
-    normed, g, branch, back, do, ffn_grad, ffn_sums = ffn(hids, gs, gains[2:], ffn_w, up_bias[None], heads)
+    up_w, up_parts = gather_dp(up_weight, down_order, [qkv_parts[-2]] + [None] * (bits - 2) + [qkv_w, kv])
+    down_own = jnp.concatenate([down_weight.T, output_weight.T, no_cols], axis=1)
+    down_w, _ = gather_dp(down_own, down_order, [up_parts[0]] + [None] * (bits - 2) + [(kv, up_w, gs[2])])
+    tail = shift(after(kv, down_w), "dp", 1)
+    normed, g, branch, back, do, ffn_grad, ffn_sums = ffn(hids, gs, gains[2:], up_w, down_w, up_bias[None], heads)
     spots = t[None]
     attn_args = (spots, first, start, tail, kv, q, do, cos, sin, blk)
     *early, dtail_low, carry = attention(*attn_args)
     ahead_low = shift(dtail_low, "dp", -1)
+    ffn_order = down_order[::-1]
     o, dq, dtail_high, dkv_low, dkv_high = attention(*attn_args, early=(carry, *early))
-    ahead_high = shift(dtail_high, "dp", -1)
+    ahead_high = shift(after(dtail_high, ahead_low), "dp", -1)
+    ffn_first = scatter_step(ffn_grad, chunk, ffn_order, ffn_order[0], tail, o)
     post_args = (dq, cos, sin, normed, mixer_in, back, mixer_gain[None], qkv_w)
-    early = post(0, spots, dkv_low, ahead_low, *post_args, early=(ffn_sums,))
-    ffn_order = mixed_order[::-1]
-    branch, mid_grad = mid(after(o, early[2]), dq, mixer_in, g, branch, ffn_w[:, 2 * F :])
+    branch, mid_grad = mid(o, dq, mixer_in, g, branch, down_w[:, F:])
     branch_own, branch_far = scatter_core(branch, blk)
-    ffn_grads, ffn_parts, _ = scatter_dp(ffn_grad, chunk, ffn_order, [tail, branch])
-    ahead_high = after(ahead_high, branch_far)
+    branch_across = swap(branch_far, "tensor", 2)
+    result = hidden_in.astype(f32) + branch_own + branch_across.astype(f32) + out_bias
+    early = post(0, spots, dkv_low, after(ahead_low, ffn_first, branch_far), *post_args, early=(ffn_sums,))
     hat, mix_grad, sums = post(1, spots, dkv_high, ahead_high, *post_args, early=(*early, mid_grad))
     hat_own, hat_far = scatter_core(hat, blk)
-    summed = branch_own + swap(branch_far, "tensor", 2).astype(f32)
-    result = hidden_in.astype(f32) + summed + out_bias
-    hat_far = after(hat_far, summed)
-    grad_hat = hat_own + swap(hat_far, "tensor", 2).astype(f32)
-    mix_grads, _, sums = scatter_dp(mix_grad, chunk, down_order[::-1], [ffn_parts[1], hat_far, grad_hat], sums)
+    hat_across = swap(hat_far, "tensor", 2)
+    grad_hat = hat_own + hat_across.astype(f32)
+    mix_order = down_order[::-1]
+    mix_grads = mix_grad
+    for n, bit in enumerate(mix_order):
+        landed = [(hat_far, branch_across), hat_across][n] if n < 2 else None
+        mix_grads, sums = scatter_step(mix_grads, chunk, mix_order[n:], bit, None, landed, sums)
+    ffn_grads = scatter_step(ffn_first, chunk, ffn_order[1:], ffn_order[1], None, mid_grad)
+    for n in range(2, bits):
+        ffn_grads = scatter_step(ffn_grads, chunk, ffn_order[n:], ffn_order[n], None, hat_across)
     own, inv_std = normalize(hidden_in.astype(f32))
     first_mean = jnp.mean(grad_hat, axis=-1, keepdims=True)
     second_mean = jnp.mean(grad_hat * own, axis=-1, keepdims=True)
     grad_hidden = out_grad.astype(f32) + inv_std * (grad_hat - first_mean - own * second_mean)
-    norm_sums = sum_over(sums, "tensor")
+    norm_sums = sums + swap(sums, "tensor", 1)
+    norm_sums = norm_sums + swap(norm_sums, "tensor", 2)
     head_sums = sums[2, : 2 * W].reshape(heads, 2, HD)[:, 1].reshape(W)
     pair_grad = jnp.stack([sums[2, 2 * W : 3 * W], head_sums])
     kv_grads = mix_grads[:, : 2 * W].reshape(chunk, heads, 2, HD)

time: 310 us -> 262 us (0.85)
  waiting for transfers between devices: 117 us -> 59 us
  starting transfers between devices: 45.5 us -> 61.1 us
  Pallas kernels: 107 us -> 92.3 us
  local copies, waits for them, and re-layouts: 17.4 us -> 26.6 us
    ppermute x24 -> x27, waiting for transfers between devices: 114 us -> 56.8 us  [swap(): return lax.ppermute(value, axis, [(i, i ^ mask) for i in range(count)])]
    pallas_call x2, Pallas kernels: 40.8 us -> 24.9 us  [attention(): pl.pallas_call(functools.partial(attn_kernel, T=T, blk=blk, heads=heads,...]
    ppermute x24 -> x27, starting transfers between devices: 39.8 us -> 54.5 us  [swap(): return lax.ppermute(value, axis, [(i, i ^ mask) for i in range(count)])]
    unnamed x52 -> x64, local copies, waits for them, and re-layouts: 4.93 us -> 10.9 us
  transfers between devices with their start and end apart: 27 -> 30, of which waited for: 16 -> 12; matrix products, arithmetic and copies ran while one was open for 9% -> 13% of each run, Pallas kernels for 32% -> 35%
where the time goes in v1:
time: 262 us; the launch traced here: 261 us
  Pallas kernels  92.3 us (35%)
  starting transfers between devices  61.1 us (23%)
  waiting for transfers between devices  59 us (23%)
  local copies, waits for them, and re-layouts  26.6 us (10%)
  other arithmetic  20 us (8%)
    ppermute x27, waiting for transfers between devices, swap(): return lax.ppermute(value, axis, [(i, i ^ mask) for i in range(count)])  56.8 us
    ppermute x27, starting transfers between devices, swap(): return lax.ppermute(value, axis, [(i, i ^ mask) for i in range(count)])  54.5 us
    pallas_call x1, Pallas kernels, ffn(): pl.pallas_call(functools.partial(ffn_kernel, pieces=len(gs), blk=blk), gr...  30.9 us
    pallas_call x2, Pallas kernels, attention(): pl.pallas_call(functools.partial(attn_kernel, T=T, blk=blk, heads=heads,...  24.9 us
    pallas_call x2, Pallas kernels, post(): pl.pallas_call(post_kernel, grid_spec=pltpu.PrefetchScalarGridSpec(num_sc...  16.3 us
    unnamed x64, local copies, waits for them, and re-layouts  10.9 us
    pallas_call x1, Pallas kernels, pre(): pl.pallas_call(functools.partial(pre_kernel, pieces=len(hids), blk=blk),...  10.7 us
    pallas_call x1, Pallas kernels, mid(): pl.pallas_call(mid_kernel, grid=(T // TR,), in_specs=[cols, cols, rows_sp...  9.53 us
  transfers between devices with their start and end apart: 30, of which 12 were waited for; matrix products, arithmetic and copies ran while one was open for 13% of the time, Pallas kernels for 35%

profile of v1, /device:TPU:0, one launch (start us, length us, event | category | flops | bytes accessed | tf_op | source)
XLA Modules:
  0.0 260.6 jit_solution(14573662545020037389)
XLA Ops:
  0.6 3.0 %collective-permute-start.1 = (bf16[512,768]{1,0:T(8,128)(2,1)}, bf16[512,768]{1,0:T(8,128)(2,1)S(1)}, u32[]{:S(2)}, u32[]{:S(2)}) collective-permute-start(bf16[512,768]{1,0:T(8,128)(2,1)} %refs_0_.3), channel_id=1, source_target_pairs={{0,2},{1,3},{2,0},{3,1},{4,6},{5,7},{6,4},{7,5},{8,10},{9,11},{10,... | collective-permute-start | bytes 2359304 | tf_op jit(solution)/shard_map/ppermute | solution.py:41
  5.0 2.6 %collective-permute-start.3 = (bf16[96,640]{1,0:T(8,128)(2,1)S(1)}, bf16[96,640]{1,0:T(8,128)(2,1)S(1)}, u32[]{:S(2)}, u32[]{:S(2)}) collective-permute-start(bf16[96,640]{1,0:T(8,128)(2,1)S(1)} %pad_maximum_fusion.16), channel_id=1, source_target_pairs={{0,16},{4,20},{8,24},{12,28},{16,0},{20,4},{24,8},{28,12},{1,17},{... | collective-permute-start | bytes 368648 | tf_op jit(solution)/shard_map/ppermute | solution.py:41
  9.4 4.9 %collective-permute-done.3 = bf16[96,640]{1,0:T(8,128)(2,1)S(1)} collective-permute-done((bf16[96,640]{1,0:T(8,128)(2,1)S(1)}, bf16[96,640]{1,0:T(8,128)(2,1)S(1)}, u32[]{:S(2)}, u32[]{:S(2)}) %collective-permute-start.3) | collective-permute-done | bytes 122912 | tf_op jit(solution)/shard_map/ppermute | solution.py:41
  16.2 5.9 %collective-permute-done.4 = bf16[192,640]{1,0:T(8,128)(2,1)S(1)} collective-permute-done((bf16[192,640]{1,0:T(8,128)(2,1)S(1)}, bf16[192,640]{1,0:T(8,128)(2,1)S(1)}, u32[]{:S(2)}, u32[]{:S(2)}) %collective-permute-start.4) | collective-permute-done | bytes 245792 | tf_op jit(solution)/shard_map/ppermute | solution.py:41
  23.9 2.7 %collective-permute-start.6 = (bf16[96,768]{1,0:T(8,128)(2,1)S(1)}, bf16[96,768]{1,0:T(8,128)(2,1)S(1)}, u32[]{:S(2)}, u32[]{:S(2)}) collective-permute-start(bf16[96,768]{1,0:T(8,128)(2,1)S(1)} %copy-done.20), channel_id=1, source_target_pairs={{0,16},{4,20},{8,24},{12,28},{16,0},{20,4},{24,8},{28,12},{1,17},{... | collective-permute-start | bytes 442376 | tf_op jit(solution)/shard_map/ppermute | solution.py:41
  26.8 6.2 %collective-permute-done.6 = bf16[96,768]{1,0:T(8,128)(2,1)S(1)} collective-permute-done((bf16[96,768]{1,0:T(8,128)(2,1)S(1)}, bf16[96,768]{1,0:T(8,128)(2,1)S(1)}, u32[]{:S(2)}, u32[]{:S(2)}) %collective-permute-start.6) | collective-permute-done | bytes 147488 | tf_op jit(solution)/shard_map/ppermute | solution.py:41
  33.8 3.4 %collective-permute-start.7 = (bf16[96,1024]{1,0:T(8,128)(2,1)S(1)}, bf16[96,1024]{1,0:T(8,128)(2,1)S(1)}, u32[]{:S(2)}, u32[]{:S(2)}) collective-permute-start(bf16[96,1024]{1,0:T(8,128)(2,1)S(1)} %pad_maximum_fusion.14), channel_id=1, source_target_pairs={{0,16},{4,20},{8,24},{12,28},{16,0},{20,4},{24,8},{28,12},{1,17},{... | collective-permute-start | bytes 589832 | tf_op jit(solution)/shard_map/ppermute | solution.py:41
  39.2 6.2 %collective-permute-done.9 = bf16[192,768]{1,0:T(8,128)(2,1)S(1)} collective-permute-done((bf16[192,768]{1,0:T(8,128)(2,1)S(1)}, bf16[192,768]{1,0:T(8,128)(2,1)S(1)}, u32[]{:S(2)}, u32[]{:S(2)}) %collective-permute-start.9) | collective-permute-done | bytes 294944 | tf_op jit(solution)/shard_map/ppermute | solution.py:41
  49.8 10.7 %pre.1 = (bf16[2048,768]{1,0:T(8,128)(2,1)}, bf16[3,2048,128]{2,1,0:T(8,128)(2,1)}, bf16[3,2048,128]{2,1,0:T(8,128)(2,1)}) custom-call(bf16[512,768]{1,0:T(8,128)(2,1)} %refs_0_.3, bf16[512,768]{1,0:T(8,128)(2,1)} %copy-done.16, bf16[512,768]{1,0:T(8,128)(2,1)} %copy-done.15, bf16[512,768]{1,0:T(8,128)(2,1)} %copy-done.17, ...), custom_call_target="tpu_custom_call" | custom-call | flops 575000000 | bytes 1000 | tf_op jit(solution)/shard_map/pre/pallas_call | solution.py:195
  61.9 3.1 %collective-permute-done.11.refs_6_ = bf16[512,768]{1,0:T(8,128)(2,1)} collective-permute-done((bf16[512,768]{1,0:T(8,128)(2,1)}, bf16[512,768]{1,0:T(8,128)(2,1)}, u32[]{:S(2)}, u32[]{:S(2)}) %collective-permute-start.11) | collective-permute-done | bytes 786464 | tf_op jit(solution)/shard_map/ppermute | solution.py:41
  67.5 14.1 %collective-permute-done.12 = bf16[384,1024]{1,0:T(8,128)(2,1)S(1)} collective-permute-done((bf16[384,1024]{1,0:T(8,128)(2,1)S(1)}, bf16[384,1024]{1,0:T(8,128)(2,1)S(1)}, u32[]{:S(2)}, u32[]{:S(2)}) %collective-permute-start.12) | collective-permute-done | bytes 786464 | tf_op jit(solution)/shard_map/ppermute | solution.py:41
  83.9 3.7 %collective-permute-start.13 = (bf16[3,2048,128]{2,1,0:T(8,128)(2,1)S(1)}, bf16[3,2048,128]{2,1,0:T(8,128)(2,1)S(1)}, u32[]{:S(2)}, u32[]{:S(2)}) collective-permute-start(bf16[3,2048,128]{2,1,0:T(8,128)(2,1)S(1)} %copy-done), channel_id=1, source_target_pairs={{0,4},{4,8},{8,12},{12,16},{16,20},{20,24},{24,28},{1,5},{5,9},{9,... | collective-permute-start | bytes 4718600 | tf_op jit(solution)/shard_map/ppermute | solution.py:47
  90.0 1.8 slice.238.w_ref
  91.8 30.9 %ffn.1 = (bf16[2048,768]{1,0:T(8,128)(2,1)}, bf16[2048,768]{1,0:T(8,128)(2,1)}, bf16[2048,768]{1,0:T(8,128)(2,1)}, bf16[2048,768]{1,0:T(8,128)(2,1)}, bf16[3,204...) custom-call(bf16[512,768]{1,0:T(8,128)(2,1)} %refs_0_.3, bf16[512,768]{1,0:T(8,128)(2,1)} %copy-done.16, ...), custom_call_target="tpu_custom_call" | custom-call | flops 575000000 | bytes 1000 | tf_op jit(solution)/shard_map/ffn/pallas_call | solution.py:276
  122.8 3.4 %broadcast_select_fusion.1 = (bf16[4,1,96,1536]{3,2,1,0:T(8,128)(2,1)}, bf16[4,1,96,1536]{3,2,1,0:T(8,128)(2,1)}) fusion(pred[]{:T(512)S(6)} %eq.6, bf16[4,2,96,1536]{3,2,1,0:T(8,128)(2,1)} %bitcast.138), kind=kLoop, calls=%fused_computation.32 | loop fusion | flops 1179648 | bytes 4718593 | tf_op jit(solution)/shard_map/jit(_where)/select_n | solution.py:107
  126.2 8.0 %attn.2 = (bf16[192,1024]{1,0:T(8,128)(2,1)S(1)}, bf16[192,1024]{1,0:T(8,128)(2,1)S(1)}, bf16[3,1024,128]{2,1,0:T(8,128)(2,1)S(1)}, f32[3,2048,128]{2,1,0:T(8,128)S(1)}) custom-call(s32[1]{0:T(128)} %bitcast.refs_0_.place_ref, s32[8]{0:T(128)S(1)} %and_select_fusion.refs_1_, s32[1,2048]{1,0:T(1,128)S(1)} %add_subtract_fusion.refs_2_, ...), custom_call_target="tpu_custom_call" | custom-call | flops 115000000 | bytes 1000 | tf_op jit(solution)/shard_map/attn/pallas_call | solution.py:428
  137.4 16.9 %attn.3 = (bf16[192,2048]{1,0:T(8,128)(2,1)S(1)}, bf16[192,2048]{1,0:T(8,128)(2,1)S(1)}, bf16[3,1024,128]{2,1,0:T(8,128)(2,1)S(1)}, f32[3,1024,128]{2,1,0:T(8,128)S(1)}, f32[3,1024,128]{2,1,0:T(8,128)S(1)}) custom-call(s32[1]{0:T(128)} %bitcast.refs_0_.place_ref, s32[8]{0:T(128)S(1)} %and_select_fusion.refs_1_, s32[1,2048]{1,0:T(1,128)S(1)} %add_subtract_fusion.refs_2_, ...), custom_call_target="tpu_custom_call" | custom-call | flops 115000000 | bytes 1000 | tf_op jit(solution)/shard_map/attn/pallas_call | solution.py:428
  157.3 9.5 %mid.1 = (bf16[2048,768]{1,0:T(8,128)(2,1)}, bf16[768,384]{1,0:T(8,128)(2,1)}) custom-call(bf16[192,2048]{1,0:T(8,128)(2,1)} %copy-done.9, bf16[192,2048]{1,0:T(8,128)(2,1)} %copy-done.8, bf16[2048,768]{1,0:T(8,128)(2,1)} %get-tuple-element.70.mixer_ref, bf16[2048,768]{1,0:T(8,128)(2,1)} %get-tuple-element.71.g_ref, ...), custom_call_target="tpu_custom_call" | custom-call | flops 10350000128 | bytes 1000 | tf_op jit(solution)/shard_map/mid/pallas_call | solution.py:471
  172.5 14.1 %collective-permute-start.28 = (bf16[192,1536]{1,0:T(8,128)(2,1)}, bf16[192,1536]{1,0:T(8,128)(2,1)}, u32[]{:S(2)}, u32[]{:S(2)}) collective-permute-start(bf16[192,1536]{1,0:T(8,128)(2,1)} %bitcast.59), channel_id=1, source_target_pairs={{0,8},{4,12},{8,0},{12,4},{16,24},{20,28},{24,16},{28,20},{1,9},{5... | collective-permute-start | bytes 1769480 | tf_op jit(solution)/shard_map/ppermute | solution.py:41
  190.3 7.8 %post.2 = (bf16[2048,768]{1,0:T(8,128)(2,1)}, f32[768,384]{1,0:T(8,128)}, f32[8,768]{1,0:T(8,128)}) custom-call(s32[1]{0:T(128)} %bitcast.refs_0_.place_ref, f32[3,1024,128]{2,1,0:T(8,128)} %copy-done.7, bf16[3,1024,128]{2,1,0:T(8,128)(2,1)} %collective-permute-done.18.ahead_ref, bf16[192,2048]{1,0:T(8,128)(2,1)} %copy-done.8, ...), custom_call_target="tpu_custom_call" | custom-call | flops 9200000000 | bytes 1000 | tf_op jit(solution)/shard_map/post/pallas_call | solution.py:548
  198.1 2.3 collective-permute-done.19.ahead_ref
  200.4 8.4 %post.3 = (bf16[2048,768]{1,0:T(8,128)(2,1)}, bf16[768,768]{1,0:T(8,128)(2,1)}, f32[8,768]{1,0:T(8,128)}) custom-call(s32[1]{0:T(128)} %bitcast.refs_0_.place_ref, f32[3,1024,128]{2,1,0:T(8,128)} %copy-done.6, bf16[3,1024,128]{2,1,0:T(8,128)(2,1)} %collective-permute-done.19.ahead_ref, ...), custom_call_target="tpu_custom_call", output_to_operand_aliasing={{0}: (11, {})} | custom-call | flops 9200000000 | bytes 1000 | tf_op jit(solution)/shard_map/post/pallas_call | solution.py:548
  211.7 3.7 %collective-permute-start.23 = (bf16[400,768]{1,0:T(8,128)(2,1)S(1)}, bf16[400,768]{1,0:T(8,128)(2,1)S(1)}, u32[]{:S(2)}, u32[]{:S(2)}) collective-permute-start(bf16[400,768]{1,0:T(8,128)(2,1)S(1)} %pad_maximum_fusion.6), channel_id=1, source_target_pairs={{0,4},{4,0},{8,12},{12,8},{16,20},{20,16},{24,28},{28,24},{1,5},{5... | collective-permute-start | bytes 1843208 | tf_op jit(solution)/shard_map/ppermute | solution.py:41
  216.8 8.8 %collective-permute-start.29 = (bf16[96,1536]{1,0:T(8,128)(2,1)S(1)}, bf16[96,1536]{1,0:T(8,128)(2,1)S(1)}, u32[]{:S(2)}, u32[]{:S(2)}) collective-permute-start(bf16[96,1536]{1,0:T(8,128)(2,1)S(1)} %fusion.15), channel_id=1, source_target_pairs={{0,16},{4,20},{8,24},{12,28},{16,0},{20,4},{24,8},{28,12},{1,17},{... | collective-permute-start | bytes 884744 | tf_op jit(solution)/shard_map/ppermute | solution.py:41
  226.5 2.3 collective-permute-done.23
  229.2 5.4 %collective-permute-start.24 = (bf16[208,768]{1,0:T(8,128)(2,1)S(1)}, bf16[208,768]{1,0:T(8,128)(2,1)S(1)}, u32[]{:S(2)}, u32[]{:S(2)}) collective-permute-start(bf16[208,768]{1,0:T(8,128)(2,1)S(1)} %pad_maximum_fusion.10), channel_id=1, source_target_pairs={{0,8},{4,12},{8,0},{12,4},{16,24},{20,28},{24,16},{28,20},{1,9},{5... | collective-permute-start | bytes 958472 | tf_op jit(solution)/shard_map/ppermute | solution.py:41
  234.7 2.3 collective-permute-done.29
  237.0 7.4 %collective-permute-done.22 = bf16[512,768]{1,0:T(8,128)(2,1)S(1)} collective-permute-done((bf16[512,768]{1,0:T(8,128)(2,1)S(1)}, bf16[512,768]{1,0:T(8,128)(2,1)S(1)}, u32[]{:S(2)}, u32[]{:S(2)}) %collective-permute-start.22) | collective-permute-done | bytes 786464 | tf_op jit(solution)/shard_map/ppermute | solution.py:41
  244.8 1.9 collective-permute-start.25
  247.4 3.4 %fusion.7 = (f32[512,768]{1,0:T(8,128)}, f32[512,768]{1,0:T(8,128)}) fusion(bf16[512,768]{1,0:T(8,128)(2,1)S(1)} %copy-done.11, bf16[512,768]{1,0:T(8,128)(2,1)} %refs_4_, f32[512]{0:T(512)S(1)} %get-tuple-element.194, f32[512]{0:T(512)S(1)} %get-tuple-element.195, f32[512]{0:T(512)S(1)} %add_rsqrt_fusion, f32[512]{0:T(512)S(1)} %broadcast_multiply_fusion.2, ...), kind=kLoop, calls=%fused_computation.11 | loop fusion | flops 7471104 | bytes 11021312 | tf_op jit(solution)/shard_map/add | solution.py:640
  251.7 2.3 collective-permute-done.25
  257.9 2.0 collective-permute-done.27
  (207 shorter events, 49.8 us)
Async XLA Ops:
  0.6 36.5 %collective-permute-start.1 = (bf16[512,768]{1,0:T(8,128)(2,1)}, bf16[512,768]{1,0:T(8,128)(2,1)S(1)}, u32[]{:S(2)}, u32[]{:S(2)}) collective-permute-start(bf16[512,768]{1,0:T(8,128)(2,1)} %refs_0_.3), channel_id=1, source_target_pairs={{0,2},{1,3},{2,0},{3,1},{4,6},{5,7},{6,4},{7,5},{8,10},{9,11},{10,... | collective-permute-start | bytes 2359304 | tf_op jit(solution)/shard_map/ppermute | solution.py:41
  3.6 45.0 %collective-permute-start = (bf16[512,768]{1,0:T(8,128)(2,1)}, bf16[512,768]{1,0:T(8,128)(2,1)S(1)}, u32[]{:S(2)}, u32[]{:S(2)}) collective-permute-start(bf16[512,768]{1,0:T(8,128)(2,1)} %refs_0_.3), channel_id=1, source_target_pairs={{0,1},{1,0},{2,3},{3,2},{4,5},{5,4},{6,7},{7,6},{8,9},{9,8},{10,11... | collective-permute-start | bytes 2359304 | tf_op jit(solution)/shard_map/ppermute | solution.py:41
  5.0 9.3 %collective-permute-start.3 = (bf16[96,640]{1,0:T(8,128)(2,1)S(1)}, bf16[96,640]{1,0:T(8,128)(2,1)S(1)}, u32[]{:S(2)}, u32[]{:S(2)}) collective-permute-start(bf16[96,640]{1,0:T(8,128)(2,1)S(1)} %pad_maximum_fusion.16), channel_id=1, source_target_pairs={{0,16},{4,20},{8,24},{12,28},{16,0},{20,4},{24,8},{28,12},{1,17},{... | collective-permute-start | bytes 368648 | tf_op jit(solution)/shard_map/ppermute | solution.py:41
  14.5 12.3 %copy-start.19 = (bf16[768,96]{0,1:T(8,128)(2,1)S(1)}, bf16[768,96]{0,1:T(8,128)(2,1)}, u32[]{:S(2)}) copy-start(bf16[768,96]{0,1:T(8,128)(2,1)} %param.25) | copy-start | bytes 442372
  14.5 7.7 %collective-permute-start.4 = (bf16[192,640]{1,0:T(8,128)(2,1)S(1)}, bf16[192,640]{1,0:T(8,128)(2,1)S(1)}, u32[]{:S(2)}, u32[]{:S(2)}) collective-permute-start(bf16[192,640]{1,0:T(8,128)(2,1)S(1)} %bitcast.154), channel_id=1, source_target_pairs={{0,8},{4,12},{8,0},{12,4},{16,24},{20,28},{24,16},{28,20},{1,9},{5... | collective-permute-start | bytes 737288 | tf_op jit(solution)/shard_map/ppermute | solution.py:41
  22.3 14.9 %collective-permute-start.5 = (bf16[384,640]{1,0:T(8,128)(2,1)S(1)}, bf16[384,640]{1,0:T(8,128)(2,1)S(1)}, u32[]{:S(2)}, u32[]{:S(2)}) collective-permute-start(bf16[384,640]{1,0:T(8,128)(2,1)S(1)} %bitcast.139), channel_id=1, source_target_pairs={{0,4},{4,0},{8,12},{12,8},{16,20},{20,16},{24,28},{28,24},{1,5},{5... | collective-permute-start | bytes 1474568 | tf_op jit(solution)/shard_map/ppermute | solution.py:41
  23.9 9.1 %collective-permute-start.6 = (bf16[96,768]{1,0:T(8,128)(2,1)S(1)}, bf16[96,768]{1,0:T(8,128)(2,1)S(1)}, u32[]{:S(2)}, u32[]{:S(2)}) collective-permute-start(bf16[96,768]{1,0:T(8,128)(2,1)S(1)} %copy-done.20), channel_id=1, source_target_pairs={{0,16},{4,20},{8,24},{12,28},{16,0},{20,4},{24,8},{28,12},{1,17},{... | collective-permute-start | bytes 442376 | tf_op jit(solution)/shard_map/ppermute | solution.py:41
  33.0 12.3 %collective-permute-start.9 = (bf16[192,768]{1,0:T(8,128)(2,1)S(1)}, bf16[192,768]{1,0:T(8,128)(2,1)S(1)}, u32[]{:S(2)}, u32[]{:S(2)}) collective-permute-start(bf16[192,768]{1,0:T(8,128)(2,1)S(1)} %bitcast.151), channel_id=1, source_target_pairs={{0,8},{4,12},{8,0},{12,4},{16,24},{20,28},{24,16},{28,20},{1,9},{5... | collective-permute-start | bytes 884744 | tf_op jit(solution)/shard_map/ppermute | solution.py:41
  33.8 14.1 %collective-permute-start.7 = (bf16[96,1024]{1,0:T(8,128)(2,1)S(1)}, bf16[96,1024]{1,0:T(8,128)(2,1)S(1)}, u32[]{:S(2)}, u32[]{:S(2)}) collective-permute-start(bf16[96,1024]{1,0:T(8,128)(2,1)S(1)} %pad_maximum_fusion.14), channel_id=1, source_target_pairs={{0,16},{4,20},{8,24},{12,28},{16,0},{20,4},{24,8},{28,12},{1,17},{... | collective-permute-start | bytes 589832 | tf_op jit(solution)/shard_map/ppermute | solution.py:41
  37.2 11.5 %collective-permute-start.2 = (bf16[512,768]{1,0:T(8,128)(2,1)S(1)}, bf16[512,768]{1,0:T(8,128)(2,1)S(1)}, u32[]{:S(2)}, u32[]{:S(2)}) collective-permute-start(bf16[512,768]{1,0:T(8,128)(2,1)S(1)} %collective-permute-done.1.refs_2_), channel_id=1, source_target_pairs={{0,1},{1,0},{2,3},{3,2},{4,5},{5,4},{6,7},{7,6},{8,9},{9,8},{10,11... | collective-permute-start | bytes 2359304 | tf_op jit(solution)/shard_map/ppermute | solution.py:41
  45.4 15.1 %collective-permute-start.10 = (bf16[384,768]{1,0:T(8,128)(2,1)S(1)}, bf16[384,768]{1,0:T(8,128)(2,1)S(1)}, u32[]{:S(2)}, u32[]{:S(2)}) collective-permute-start(bf16[384,768]{1,0:T(8,128)(2,1)S(1)} %bitcast.136), channel_id=1, source_target_pairs={{0,4},{4,0},{8,12},{12,8},{16,20},{20,16},{24,28},{28,24},{1,5},{5... | collective-permute-start | bytes 1769480 | tf_op jit(solution)/shard_map/ppermute | solution.py:41
  46.7 13.8 %copy-start.23 = (f32[1,768]{1,0:T(1,128)}, f32[1,768]{1,0:T(1,128)S(1)}, u32[]{:S(2)}) copy-start(f32[1,768]{1,0:T(1,128)S(1)} %stack.83.gain_ref) | copy-start | bytes 9220
  47.4 17.6 %collective-permute-start.11 = (bf16[512,768]{1,0:T(8,128)(2,1)}, bf16[512,768]{1,0:T(8,128)(2,1)}, u32[]{:S(2)}, u32[]{:S(2)}) collective-permute-start(bf16[512,768]{1,0:T(8,128)(2,1)} %refs_4_), channel_id=1, source_target_pairs={{0,2},{1,3},{2,0},{3,1},{4,6},{5,7},{6,4},{7,5},{8,10},{9,11},{10,... | collective-permute-start | bytes 2359304 | tf_op jit(solution)/shard_map/ppermute | solution.py:41
  48.0 13.9 %collective-permute-start.8 = (bf16[192,1024]{1,0:T(8,128)(2,1)S(1)}, bf16[192,1024]{1,0:T(8,128)(2,1)S(1)}, u32[]{:S(2)}, u32[]{:S(2)}) collective-permute-start(bf16[192,1024]{1,0:T(8,128)(2,1)S(1)} %bitcast.146), channel_id=1, source_target_pairs={{0,8},{4,12},{8,0},{12,4},{16,24},{20,28},{24,16},{28,20},{1,9},{5... | collective-permute-start | bytes 1179656 | tf_op jit(solution)/shard_map/ppermute | solution.py:41
  65.2 16.5 %collective-permute-start.12 = (bf16[384,1024]{1,0:T(8,128)(2,1)S(1)}, bf16[384,1024]{1,0:T(8,128)(2,1)S(1)}, u32[]{:S(2)}, u32[]{:S(2)}) collective-permute-start(bf16[384,1024]{1,0:T(8,128)(2,1)S(1)} %bitcast.135), channel_id=1, source_target_pairs={{0,4},{4,0},{8,12},{12,8},{16,20},{20,16},{24,28},{28,24},{1,5},{5... | collective-permute-start | bytes 2359304 | tf_op jit(solution)/shard_map/ppermute | solution.py:41
  66.9 24.9 %collective-permute-start.14 = (bf16[512,768]{1,0:T(8,128)(2,1)}, bf16[512,768]{1,0:T(8,128)(2,1)}, u32[]{:S(2)}, u32[]{:S(2)}) collective-permute-start(bf16[512,768]{1,0:T(8,128)(2,1)} %refs_4_), channel_id=1, source_target_pairs={{0,1},{1,0},{2,3},{3,2},{4,5},{5,4},{6,7},{7,6},{8,9},{9,8},{10,11... | collective-permute-start | bytes 2359304 | tf_op jit(solution)/shard_map/ppermute | solution.py:41
  67.0 24.8 %collective-permute-start.15 = (bf16[512,768]{1,0:T(8,128)(2,1)}, bf16[512,768]{1,0:T(8,128)(2,1)}, u32[]{:S(2)}, u32[]{:S(2)}) collective-permute-start(bf16[512,768]{1,0:T(8,128)(2,1)} %collective-permute-done.11.refs_6_), channel_id=1, source_target_pairs={{0,1},{1,0},{2,3},{3,2},{4,5},{5,4},{6,7},{7,6},{8,9},{9,8},{10,11... | collective-permute-start | bytes 2359304 | tf_op jit(solution)/shard_map/ppermute | solution.py:41
  83.9 42.3 %collective-permute-start.13 = (bf16[3,2048,128]{2,1,0:T(8,128)(2,1)S(1)}, bf16[3,2048,128]{2,1,0:T(8,128)(2,1)S(1)}, u32[]{:S(2)}, u32[]{:S(2)}) collective-permute-start(bf16[3,2048,128]{2,1,0:T(8,128)(2,1)S(1)} %copy-done), channel_id=1, source_target_pairs={{0,4},{4,8},{8,12},{12,16},{16,20},{20,24},{24,28},{1,5},{5,9},{9,... | collective-permute-start | bytes 4718600 | tf_op jit(solution)/shard_map/ppermute | solution.py:47
  126.2 43.7 %collective-permute-start.20 = (bf16[384,1536]{1,0:T(8,128)(2,1)}, bf16[384,1536]{1,0:T(8,128)(2,1)}, u32[]{:S(2)}, u32[]{:S(2)}) collective-permute-start(bf16[384,1536]{1,0:T(8,128)(2,1)} %bitcast.42), channel_id=1, source_target_pairs={{0,4},{4,0},{8,12},{12,8},{16,20},{20,16},{24,28},{28,24},{1,5},{5... | collective-permute-start | bytes 3538952 | tf_op jit(solution)/shard_map/ppermute | solution.py:41
  135.9 32.6 %collective-permute-start.18 = (bf16[3,1024,128]{2,1,0:T(8,128)(2,1)S(1)}, bf16[3,1024,128]{2,1,0:T(8,128)(2,1)}, u32[]{:S(2)}, u32[]{:S(2)}) collective-permute-start(bf16[3,1024,128]{2,1,0:T(8,128)(2,1)S(1)} %get-tuple-element.76), channel_id=1, source_target_pairs={{4,0},{8,4},{12,8},{16,12},{20,16},{24,20},{28,24},{5,1},{9,5},{13... | collective-permute-start | bytes 2359304 | tf_op jit(solution)/shard_map/ppermute | solution.py:47
  168.4 18.4 %collective-permute-start.16 = (bf16[1024,768]{1,0:T(8,128)(2,1)S(1)}, bf16[1024,768]{1,0:T(8,128)(2,1)S(1)}, u32[]{:S(2)}, u32[]{:S(2)}) collective-permute-start(bf16[1024,768]{1,0:T(8,128)(2,1)S(1)} %pad_maximum_fusion.1), channel_id=1, source_target_pairs={{0,1},{1,0},{2,3},{3,2},{4,5},{5,4},{6,7},{7,6},{8,9},{9,8},{10,11... | collective-permute-start | bytes 4718600 | tf_op jit(solution)/shard_map/ppermute | solution.py:41
  168.5 31.9 %collective-permute-start.19 = (bf16[3,1024,128]{2,1,0:T(8,128)(2,1)S(1)}, bf16[3,1024,128]{2,1,0:T(8,128)(2,1)}, u32[]{:S(2)}, u32[]{:S(2)}) collective-permute-start(bf16[3,1024,128]{2,1,0:T(8,128)(2,1)S(1)} %get-tuple-element.77), channel_id=1, source_target_pairs={{4,0},{8,4},{12,8},{16,12},{20,16},{24,20},{28,24},{5,1},{9,5},{13... | collective-permute-start | bytes 2359304 | tf_op jit(solution)/shard_map/ppermute | solution.py:47
  172.5 42.9 %collective-permute-start.28 = (bf16[192,1536]{1,0:T(8,128)(2,1)}, bf16[192,1536]{1,0:T(8,128)(2,1)}, u32[]{:S(2)}, u32[]{:S(2)}) collective-permute-start(bf16[192,1536]{1,0:T(8,128)(2,1)} %bitcast.59), channel_id=1, source_target_pairs={{0,8},{4,12},{8,0},{12,4},{16,24},{20,28},{24,16},{28,20},{1,9},{5... | collective-permute-start | bytes 1769480 | tf_op jit(solution)/shard_map/ppermute | solution.py:41
  189.7 39.1 %collective-permute-start.17 = (bf16[512,768]{1,0:T(8,128)(2,1)}, bf16[512,768]{1,0:T(8,128)(2,1)}, u32[]{:S(2)}, u32[]{:S(2)}) collective-permute-start(bf16[512,768]{1,0:T(8,128)(2,1)} %fusion.13), channel_id=1, source_target_pairs={{0,2},{1,3},{2,0},{3,1},{4,6},{5,7},{6,4},{7,5},{8,10},{9,11},{10,... | collective-permute-start | bytes 2359304 | tf_op jit(solution)/shard_map/ppermute | solution.py:41
  210.4 15.2 %collective-permute-start.21 = (bf16[1024,768]{1,0:T(8,128)(2,1)S(1)}, bf16[1024,768]{1,0:T(8,128)(2,1)S(1)}, u32[]{:S(2)}, u32[]{:S(2)}) collective-permute-start(bf16[1024,768]{1,0:T(8,128)(2,1)S(1)} %pad_maximum_fusion.2), channel_id=1, source_target_pairs={{0,1},{1,0},{2,3},{3,2},{4,5},{5,4},{6,7},{7,6},{8,9},{9,8},{10,11... | collective-permute-start | bytes 4718600 | tf_op jit(solution)/shard_map/ppermute | solution.py:41
  211.7 17.2 %collective-permute-start.23 = (bf16[400,768]{1,0:T(8,128)(2,1)S(1)}, bf16[400,768]{1,0:T(8,128)(2,1)S(1)}, u32[]{:S(2)}, u32[]{:S(2)}) collective-permute-start(bf16[400,768]{1,0:T(8,128)(2,1)S(1)} %pad_maximum_fusion.6), channel_id=1, source_target_pairs={{0,4},{4,0},{8,12},{12,8},{16,20},{20,16},{24,28},{28,24},{1,5},{5... | collective-permute-start | bytes 1843208 | tf_op jit(solution)/shard_map/ppermute | solution.py:41
  216.8 20.2 %collective-permute-start.29 = (bf16[96,1536]{1,0:T(8,128)(2,1)S(1)}, bf16[96,1536]{1,0:T(8,128)(2,1)S(1)}, u32[]{:S(2)}, u32[]{:S(2)}) collective-permute-start(bf16[96,1536]{1,0:T(8,128)(2,1)S(1)} %fusion.15), channel_id=1, source_target_pairs={{0,16},{4,20},{8,24},{12,28},{16,0},{20,4},{24,8},{28,12},{1,17},{... | collective-permute-start | bytes 884744 | tf_op jit(solution)/shard_map/ppermute | solution.py:41
  226.0 18.4 %collective-permute-start.22 = (bf16[512,768]{1,0:T(8,128)(2,1)S(1)}, bf16[512,768]{1,0:T(8,128)(2,1)S(1)}, u32[]{:S(2)}, u32[]{:S(2)}) collective-permute-start(bf16[512,768]{1,0:T(8,128)(2,1)S(1)} %fusion.11), channel_id=1, source_target_pairs={{0,2},{1,3},{2,0},{3,1},{4,6},{5,7},{6,4},{7,5},{8,10},{9,11},{10,... | collective-permute-start | bytes 2359304 | tf_op jit(solution)/shard_map/ppermute | solution.py:41
  229.2 15.3 %collective-permute-start.24 = (bf16[208,768]{1,0:T(8,128)(2,1)S(1)}, bf16[208,768]{1,0:T(8,128)(2,1)S(1)}, u32[]{:S(2)}, u32[]{:S(2)}) collective-permute-start(bf16[208,768]{1,0:T(8,128)(2,1)S(1)} %pad_maximum_fusion.10), channel_id=1, source_target_pairs={{0,8},{4,12},{8,0},{12,4},{16,24},{20,28},{24,16},{28,20},{1,9},{5... | collective-permute-start | bytes 958472 | tf_op jit(solution)/shard_map/ppermute | solution.py:41
  244.8 9.2 %collective-permute-start.25 = (bf16[112,768]{1,0:T(8,128)(2,1)S(1)}, bf16[112,768]{1,0:T(8,128)(2,1)S(1)}, u32[]{:S(2)}, u32[]{:S(2)}) collective-permute-start(bf16[112,768]{1,0:T(8,128)(2,1)S(1)} %pad_maximum_fusion.15), channel_id=1, source_target_pairs={{0,16},{4,20},{8,24},{12,28},{16,0},{20,4},{24,8},{28,12},{1,17},{... | collective-permute-start | bytes 516104 | tf_op jit(solution)/shard_map/ppermute | solution.py:41
  254.7 1.4 collective-permute-start.26
  256.1 3.9 %collective-permute-start.27 = (f32[8,768]{1,0:T(8,128)S(1)}, f32[8,768]{1,0:T(8,128)S(1)}, u32[]{:S(2)}, u32[]{:S(2)}) collective-permute-start(f32[8,768]{1,0:T(8,128)S(1)} %add.156), channel_id=1, source_target_pairs={{0,2},{1,3},{2,0},{3,1},{4,6},{5,7},{6,4},{7,5},{8,10},{9,11},{10,... | collective-permute-start | bytes 73736 | tf_op jit(solution)/shard_map/ppermute | solution.py:41
  (28 other events, 112.5 us)

commit v2 on v1

--- a/solution.py
+++ b/solution.py
@@ -19,6 +19,7 @@
 TR = 512
 FR = 512
 PR = 512
+MR = 512
 bf16 = jnp.bfloat16
 f32 = jnp.float32
 NN = (((1,), (0,)), ((), ()))
@@ -62,11 +63,11 @@
     return [own, near, far, diagonal]
 
 
-def scatter_core(blocks, rows):
-    back = jnp.concatenate([blocks[rows : 2 * rows], blocks[3 * rows :]], axis=0)
-    near = swap(back, "tensor", 1).astype(f32)
-    far = (blocks[2 * rows : 3 * rows].astype(f32) + near[rows:]).astype(bf16)
-    return blocks[:rows].astype(f32) + near[:rows], far
+def scatter_core(blocks):
+    rows = blocks.shape[0] // 4
+    near = swap(blocks[2 * rows :], "tensor", 1).astype(f32)
+    total = blocks[: 2 * rows].astype(f32) + near
+    return total[:rows], total[rows:].astype(bf16)
 
 
 def split(held, rows, left, bit):
@@ -99,23 +100,26 @@
     return first, lax.reduce_precision(sums - first, 8, 7)
 
 
-def scatter_step(held, rows, left, bit, gate=None, landed=None, sums=None):
+def halves(held, rows, left, bit):
     cols = held.shape[1]
     pairs = split(held, rows, left, bit)
     high = ((lax.axis_index("dp") >> bit) & 1) == 1
     send = jnp.where(high, pairs[:, 0], pairs[:, 1]).astype(bf16).reshape(-1, cols)
-    keep = jnp.where(high, pairs[:, 1], pairs[:, 0]).astype(f32).reshape(-1, cols)
+    keep = jnp.where(high, pairs[:, 1], pairs[:, 0]).reshape(-1, cols)
+    return send, keep
+
+
+def scatter_step(held, rows, left, bit, landed=None, sums=None):
+    send, keep = halves(held, rows, left, bit)
     count = send.shape[0]
     if sums is not None:
         first, second = two_parts(sums)
         send = jnp.concatenate([send, first.astype(bf16), second.astype(bf16)], axis=0)
-    if gate is not None:
-        send = after(send, gate)
     other = swap(send, "dp", 1 << bit)
     if landed is not None:
         other = after(other, landed)
     other = other.astype(f32)
-    held = keep + other[:count]
+    held = keep.astype(f32) + other[:count]
     if sums is None:
         return held
     return held, (first + second) + (other[count : count + 8] + other[count + 8 :])
@@ -219,9 +223,18 @@
     return (jnp.where(h >= 0, 1.0 - tail, tail), bell * (1.0 / math.sqrt(2.0 * math.pi)))
 
 
-def ffn_kernel(*refs, pieces, blk):
+def store_halves(total, high, chunk, send_ref, keep_ref):
+    count = total.shape[0] // chunk
+    low, top = (
+        jnp.concatenate([total[n * chunk : (n + 1) * chunk] for n in range(side, count, 2)], axis=0) for side in (0, 1)
+    )
+    send_ref[: total.shape[0] // 2] = jnp.where(high == 1, low, top).astype(bf16)
+    keep_ref[...] = jnp.where(high == 1, top, low).astype(bf16)
+
+
+def ffn_kernel(*refs, pieces, blk, chunk):
     hids, gs, refs = refs[:pieces], refs[pieces : 2 * pieces], refs[2 * pieces :]
-    gains_ref, up_ref, down_ref, bias_ref, normed_ref, g_ref, branch_ref, back_ref, do_ref, grad_ref, sums_ref, acc_ref = refs
+    gains_ref, up_ref, down_ref, qkv_ref, bias_ref, high_ref, normed_ref, g_ref, branch_ref, back_ref, do_ref, send_ref, keep_ref, sums_ref, acc_ref = refs
     heads = do_ref.shape[0]
     F = bias_ref.shape[1]
     step = pl.program_id(0)
@@ -256,40 +269,43 @@
 
     @pl.when(step == pl.num_programs(0) - 1)
     def _():
-        grad_ref[...] = acc_ref[...].astype(bf16)
-
-    do = mm(g, down_ref[:, F:])
+        store_halves(acc_ref[...], high_ref[0], chunk, send_ref, keep_ref)
+
+    do = jnp.concatenate([mm(g, qkv_ref[...]), mm(g, down_ref[:, F:])], axis=1)
     lane = lax.broadcasted_iota(jnp.int32, (FR, 128), 1)
     for h in range(heads):
-        at = (h // 2) * 128
-        x = do[:, at : at + 128]
-        if h % 2 == 0:
+        at = HD * (h + 1)
+        x = do[:, at // 128 * 128 : at // 128 * 128 + 128]
+        if at % 128 == 0:
             x = pltpu.roll(x, HD, 1)
         do_ref[h] = jnp.where(lane < HD, 0.0, x).astype(bf16)
 
 
-def ffn(hids, gs, gains, up, down, bias, heads):
+def ffn(hids, gs, gains, up, down, qkv, bias, high, heads, chunk):
     blk, D = gs[0].shape
     T = blk * len(gs)
     F = bias.shape[1]
     rows = rows_spec(D, FR)
     return pl.pallas_call(
-        functools.partial(ffn_kernel, pieces=len(gs), blk=blk),
+        functools.partial(ffn_kernel, pieces=len(gs), blk=blk, chunk=chunk),
         grid=(T // FR,),
         in_specs=piece_specs(len(gs), blk, D, FR) * 2
-        + [whole_spec(array.shape) for array in (gains, up, down, bias)],
-        out_specs=[rows] * 4 + [heads_spec(heads, 128, FR), whole_spec((D, 2 * F)), whole_spec((8, D))],
+        + [whole_spec(gains.shape), whole_spec(up.shape), whole_spec(down.shape)]
+        + [pl.BlockSpec((D, 128), lambda i: (0, qkv.shape[1] // 128 - 1)), whole_spec(bias.shape)]
+        + [pl.BlockSpec(memory_space=pltpu.SMEM)],
+        out_specs=[rows] * 4 + [heads_spec(heads, 128, FR)] + [whole_spec((D // 2, 2 * F))] * 2 + [whole_spec((8, D))],
         out_shape=[jax.ShapeDtypeStruct((T, D), bf16)] * 4
         + [
             jax.ShapeDtypeStruct((heads, T, 128), bf16),
-            jax.ShapeDtypeStruct((D, 2 * F), bf16),
+            jax.ShapeDtypeStruct((D // 2, 2 * F), bf16),
+            jax.ShapeDtypeStruct((D // 2, 2 * F), bf16),
             jax.ShapeDtypeStruct((8, D), f32),
         ],
         scratch_shapes=[pltpu.VMEM((D, 2 * F), f32)],
         compiler_params=pltpu.CompilerParams(vmem_limit_bytes=VMEM_LIMIT),
         cost_estimate=cost(0.5),
         name="ffn",
-    )(*hids, *gs, gains, up, down, bias)
+    )(*hids, *gs, gains, up, down, qkv, bias, high)
 
 
 def attn_kernel(*refs, T, blk, heads, late):
@@ -445,12 +461,14 @@
     )(place, first, start, tail, kv, q, do, cos, sin, *early)
 
 
-def mid_kernel(o_ref, dq_ref, mixer_ref, g_ref, branch_ref, w_ref, out_ref, grad_ref, acc_ref):
+def mid_kernel(o_ref, dq_ref, mixer_ref, g_ref, branch_ref, qkv_ref, down_ref, out_ref, grad_ref, acc_ref):
     W = o_ref.shape[0]
+    pad = qkv_ref.shape[1] - HD
     step = pl.program_id(0)
     o = o_ref[...]
-    rows = o.astype(f32).T.astype(bf16)
-    out_ref[...] = (mm(rows, w_ref[:, :W], NT) + branch_ref[...].astype(f32)).astype(bf16)
+    rows = jnp.concatenate([jnp.zeros((pad, o.shape[1]), f32), o.astype(f32)], axis=0).T.astype(bf16)
+    out = mm(rows[:, : pad + HD], qkv_ref[...], NT) + mm(rows[:, pad + HD :], down_ref[...], NT)
+    out_ref[...] = (out + branch_ref[...].astype(f32)).astype(bf16)
 
     @pl.when(step == 0)
     def _():
@@ -464,33 +482,39 @@
         grad_ref[...] = acc_ref[...].T.astype(bf16)
 
 
-def mid(o, dq, mixer, g, branch, w):
+def mid(o, dq, mixer, g, branch, qkv, down):
     T, D = mixer.shape
     W = o.shape[0]
-    cols = pl.BlockSpec((W, TR), lambda i: (0, i))
+    cols = pl.BlockSpec((W, MR), lambda i: (0, i))
+    rows = rows_spec(D, MR)
+    rest = W - HD
     return pl.pallas_call(
         mid_kernel,
-        grid=(T // TR,),
-        in_specs=[cols, cols, rows_spec(D), rows_spec(D), rows_spec(D), whole_spec(w.shape)],
-        out_specs=[rows_spec(D), whole_spec((D, 2 * W))],
+        grid=(T // MR,),
+        in_specs=[
+            cols, cols, rows, rows, rows,
+            pl.BlockSpec((D, 128), lambda i: (0, qkv.shape[1] // 128 - 1)),
+            pl.BlockSpec((D, rest), lambda i: (0, down.shape[1] // rest - 1)),
+        ],
+        out_specs=[pl.BlockSpec((MR, D), lambda i: (i // 2 + i % 2 * 2, 0)), whole_spec((D, 2 * W))],
         out_shape=[jax.ShapeDtypeStruct((T, D), bf16), jax.ShapeDtypeStruct((D, 2 * W), bf16)],
         scratch_shapes=[pltpu.VMEM((2 * W, D), f32)],
         compiler_params=pltpu.CompilerParams(vmem_limit_bytes=VMEM_LIMIT),
-        cost_estimate=cost(9),
+        cost_estimate=cost(0.1),
         name="mid",
-    )(o, dq, mixer, g, branch, w)
-
-
-def post_kernel(place_ref, dkv_ref, ahead_ref, dq_ref, cos_ref, sin_ref, normed_ref, mixer_ref, back_ref, gain_ref, w_ref, *refs):
+    )(o, dq, mixer, g, branch, qkv, down)
+
+
+def post_kernel(place_ref, dkv_ref, ahead_ref, dq_ref, cos_ref, sin_ref, normed_ref, mixer_ref, back_ref, gain_ref, w_ref, *refs, chunk):
     heads = dkv_ref.shape[0]
     W = heads * HD
     step = pl.program_id(0)
-    if len(refs) == 8:
-        _, acc_in, sums_in, mid_ref, *refs = refs
+    late = chunk is not None
+    if late:
+        _, acc_in, sums_in, mid_ref, hat_ref, send_ref, keep_ref, sums_ref, acc_ref = refs
     else:
-        acc_in = mid_ref = None
-        sums_in, *refs = refs
-    hat_ref, grad_ref, sums_ref, acc_ref = refs
+        acc_in = None
+        sums_in, hat_ref, grad_ref, sums_ref, acc_ref = refs
 
     @pl.when(step == 0)
     def _():
@@ -512,12 +536,18 @@
 
     @pl.when(step == pl.num_programs(0) - 1)
     def _():
-        grad_ref[:, : 2 * W] = acc_ref[...].astype(grad_ref.dtype)
-        if mid_ref is not None:
-            grad_ref[:, 2 * W :] = mid_ref[...]
-
-
-def post(part, place, dkv, ahead, dq, cos, sin, normed, mixer, back, gain, w, early=()):
+        if late:
+            total = jnp.concatenate([acc_ref[...], mid_ref[...].astype(f32)], axis=1)
+            store_halves(total, place_ref[1], chunk, send_ref, keep_ref)
+            one = sums_ref[...].astype(bf16).astype(f32)
+            two = (sums_ref[...] - one).astype(bf16).astype(f32)
+            sums_ref[...] = one + two
+            send_ref[total.shape[0] // 2 :] = jnp.concatenate([one, two], axis=0).astype(bf16)
+        else:
+            grad_ref[...] = acc_ref[...]
+
+
+def post(part, place, dkv, ahead, dq, cos, sin, normed, mixer, back, gain, w, early=(), chunk=None):
     T, D = mixer.shape
     heads = dkv.shape[0]
     W = heads * HD
@@ -543,27 +573,77 @@
     specs = [half, half, cols(W), cols(8), cols(8), rows(at), rows(at), rows(at), fixed(gain.shape), fixed(w.shape)]
     if late:
         specs += [pl.BlockSpec(memory_space=pl.ANY), fixed((D, 2 * W)), fixed((8, D)), fixed((D, 2 * W))]
+        grads = [fixed((D // 2 + 16, 4 * W)), fixed((D // 2, 4 * W))]
+        shapes = [jax.ShapeDtypeStruct((D // 2 + 16, 4 * W), bf16), jax.ShapeDtypeStruct((D // 2, 4 * W), bf16)]
     else:
         specs += [fixed((8, D))]
+        grads = [fixed((D, 2 * W))]
+        shapes = [jax.ShapeDtypeStruct((D, 2 * W), f32)]
     return pl.pallas_call(
-        post_kernel,
+        functools.partial(post_kernel, chunk=chunk),
         grid_spec=pltpu.PrefetchScalarGridSpec(
             num_scalar_prefetch=1,
             grid=(per,),
             in_specs=specs,
-            out_specs=[rows(at), fixed((D, (4 if late else 2) * W)), fixed((8, D))],
+            out_specs=[rows(lambda i, place: at(i, place) // 2 + at(i, place) % 2 * 2)] + grads + [fixed((8, D))],
             scratch_shapes=[pltpu.VMEM((D, 2 * W), f32)],
         ),
         out_shape=[
             jax.ShapeDtypeStruct((T, D), bf16),
-            jax.ShapeDtypeStruct((D, 4 * W), bf16) if late else jax.ShapeDtypeStruct((D, 2 * W), f32),
+            *shapes,
             jax.ShapeDtypeStruct((8, D), f32),
         ],
         input_output_aliases={11: 0} if late else {},
         compiler_params=pltpu.CompilerParams(vmem_limit_bytes=VMEM_LIMIT),
-        cost_estimate=cost(8),
+        cost_estimate=cost(8 if late else 0.1),
         name="post",
     )(place, dkv, ahead, dq, cos, sin, normed, mixer, back, gain, w, *early)
+
+
+def mix_finish_kernel(keep_ref, other_ref, own_ref, triple_ref, out_ref, sums_ref):
+    rows = keep_ref.shape[0]
+    W = out_ref.shape[0]
+    other = other_ref[...].astype(f32)
+    total = keep_ref[...] + other[:rows]
+    sums_ref[...] = own_ref[...] + (other[rows : rows + 8] + other[rows + 8 :])
+    triple_ref[:, 0, :] = total[:, 2 * W : 3 * W]
+    for n in range(2):
+        triple_ref[:, 1 + n, :] = jnp.concatenate(
+            [total[:, at + n * HD : at + (n + 1) * HD] for at in range(0, 2 * W, 2 * HD)], axis=1
+        )
+    out_ref[...] = total[:, 3 * W :].T
+
+
+def mix_finish(keep, other, own, W):
+    rows = keep.shape[0]
+    return pl.pallas_call(
+        mix_finish_kernel,
+        out_shape=[
+            jax.ShapeDtypeStruct((rows, 3, W), f32),
+            jax.ShapeDtypeStruct((W, rows), f32),
+            jax.ShapeDtypeStruct(own.shape, f32),
+        ],
+        cost_estimate=cost(0.1),
+        name="mix_finish",
+    )(keep, other, own)
+
+
+def ffn_finish_kernel(keep_ref, other_ref, up_ref, down_ref):
+    F = up_ref.shape[1]
+    total = keep_ref[...] + other_ref[...].astype(f32)
+    up_ref[...] = total[:, :F]
+    down_ref[...] = total[:, F:].T
+
+
+def ffn_finish(keep, other):
+    rows, cols = keep.shape
+    F = cols // 2
+    return pl.pallas_call(
+        ffn_finish_kernel,
+        out_shape=[jax.ShapeDtypeStruct((rows, F), f32), jax.ShapeDtypeStruct((F, rows), f32)],
+        cost_estimate=cost(0.1),
+        name="ffn_finish",
+    )(keep, other)
 
 
 def shards(
@@ -584,8 +664,8 @@
     q_w, k_w, v_w = (triple_weight[:, i].reshape(chunk, heads, HD) for i in range(3))
     kv_w = jnp.concatenate([k_w, v_w], axis=2).reshape(chunk, 2 * W)
     pad = (-W) % 128
-    no_cols = jnp.zeros((chunk, pad), bf16)
-    qkv_w, qkv_parts = gather_dp(jnp.concatenate([kv_w, q_w.reshape(chunk, W), no_cols], axis=1), down_order)
+    out_own = output_weight.T
+    qkv_w, qkv_parts = gather_dp(jnp.concatenate([kv_w, q_w.reshape(chunk, W), out_own[:, :pad]], axis=1), down_order)
     hids = gather_tensor(hidden_in)
     gs = gather_tensor(after(out_grad, hids[2]))
 
@@ -602,50 +682,69 @@
     v_bias = pair_bias[1].reshape(heads, HD)
     kv_bias = jnp.concatenate([jnp.zeros_like(v_bias), v_bias], axis=1).reshape(2 * W)
     bias = jnp.concatenate([kv_bias, pair_bias[0], jnp.zeros((pad,), f32)])[None]
+    high = (lax.axis_index("dp") & 1).astype(jnp.int32)
+    spots = jnp.stack([t, high])
     mixer_in, kv, q = pre(hids, gains, qkv_w, bias, cos, sin, heads)
-    up_w, up_parts = gather_dp(up_weight, down_order, [qkv_parts[-2]] + [None] * (bits - 2) + [qkv_w, kv])
-    down_own = jnp.concatenate([down_weight.T, output_weight.T, no_cols], axis=1)
-    down_w, _ = gather_dp(down_own, down_order, [up_parts[0]] + [None] * (bits - 2) + [(kv, up_w, gs[2])])
+    feed_gains, feed_bias = gains[2:], up_bias[None]
+    early_ops = (feed_gains, feed_bias, first, start)
+    up_w, up_parts = gather_dp(up_weight, down_order, [qkv_parts[-2]] + [None] * (bits - 2) + [qkv_w, (kv, early_ops)])
+    down_own = jnp.concatenate([down_weight.T, out_own[:, pad:]], axis=1)
+    down_w, _ = gather_dp(down_own, down_order, [up_parts[0]] + [None] * (bits - 2) + [(kv, up_w)])
     tail = shift(after(kv, down_w), "dp", 1)
-    normed, g, branch, back, do, ffn_grad, ffn_sums = ffn(hids, gs, gains[2:], up_w, down_w, up_bias[None], heads)
-    spots = t[None]
+    normed, g, branch, back, do, ffn_send, ffn_keep, ffn_sums = ffn(
+        hids, gs, feed_gains, up_w, down_w, qkv_w, feed_bias, high[None], heads, chunk
+    )
     attn_args = (spots, first, start, tail, kv, q, do, cos, sin, blk)
     *early, dtail_low, carry = attention(*attn_args)
     ahead_low = shift(dtail_low, "dp", -1)
     ffn_order = down_order[::-1]
+    ffn_other = swap(after(ffn_send, tail), "dp", 1 << ffn_order[0])
     o, dq, dtail_high, dkv_low, dkv_high = attention(*attn_args, early=(carry, *early))
-    ahead_high = shift(after(dtail_high, ahead_low), "dp", -1)
-    ffn_first = scatter_step(ffn_grad, chunk, ffn_order, ffn_order[0], tail, o)
+    ahead_high = shift(after(dtail_high, ahead_low, ffn_other), "dp", -1)
     post_args = (dq, cos, sin, normed, mixer_in, back, mixer_gain[None], qkv_w)
-    branch, mid_grad = mid(o, dq, mixer_in, g, branch, down_w[:, F:])
-    branch_own, branch_far = scatter_core(branch, blk)
-    branch_across = swap(branch_far, "tensor", 2)
+    ffn_first = ffn_keep.astype(f32) + ffn_other.astype(f32)
+    ffn_send, ffn_keep = halves(ffn_first, chunk, ffn_order[1:], ffn_order[1])
+    ffn_other = swap(ffn_send, "dp", 1 << ffn_order[1])
+    early = post(0, spots, dkv_low, after(ahead_low, ffn_first), *post_args, early=(ffn_sums,))
+    branch, mid_grad = mid(after(o, early[2]), dq, mixer_in, g, branch, qkv_w, down_w)
+    hat, mix_send, mix_keep, sums = post(
+        1, spots, dkv_high, ahead_high, *post_args, early=(*early, mid_grad), chunk=chunk
+    )
+    mix_order = ffn_order
+    hat, mix_send, mix_keep, sums, ffn_other = lax.optimization_barrier((hat, mix_send, mix_keep, sums, ffn_other))
+    mix_other = swap(mix_send, "dp", 1 << mix_order[0])
+    hat_own, far = scatter_core(hat)
+    landed_far = swap(far, "tensor", 2)
+    branch_own, branch_far = scatter_core(branch)
+    branch_across = swap(after(branch_far, landed_far), "tensor", 2)
+    ffn_grads = ffn_keep.astype(f32) + after(ffn_other, far).astype(f32)
+    for n in range(2, bits):
+        ffn_send, ffn_keep = halves(ffn_grads, chunk, ffn_order[n:], ffn_order[n])
+        ffn_other = swap(ffn_send, "dp", 1 << ffn_order[n])
+        ffn_grads = ffn_keep.astype(f32) + ffn_other.astype(f32)
+    mix_other = after(mix_other, far, branch_far, ffn_other).astype(f32)
+    mix_grads = mix_keep.astype(f32) + mix_other[: mix_keep.shape[0]]
+    sums = sums + (mix_other[-16:-8] + mix_other[-8:])
+    for n in range(1, bits - 1):
+        mix_grads, sums = scatter_step(mix_grads, chunk, mix_order[n:], mix_order[n], landed_far if n == 1 else None, sums)
+    mix_send, mix_keep = halves(mix_grads, chunk, mix_order[-1:], mix_order[-1])
+    one, two = two_parts(sums)
+    mix_send = jnp.concatenate([mix_send, one.astype(bf16), two.astype(bf16)], axis=0)
+    mix_other = swap(mix_send, "dp", 1 << mix_order[-1])
+    ffn_other = after(ffn_other, mix_send)
+    up_grad, down_grad = ffn_finish(ffn_keep, ffn_other)
+    grad_hat = hat_own + after(landed_far, mix_send).astype(f32)
+    mix_other = after(mix_other, up_grad, grad_hat)
+    triple_grad, out_grad_t, sums = mix_finish(mix_keep, mix_other, one + two, W)
     result = hidden_in.astype(f32) + branch_own + branch_across.astype(f32) + out_bias
-    early = post(0, spots, dkv_low, after(ahead_low, ffn_first, branch_far), *post_args, early=(ffn_sums,))
-    hat, mix_grad, sums = post(1, spots, dkv_high, ahead_high, *post_args, early=(*early, mid_grad))
-    hat_own, hat_far = scatter_core(hat, blk)
-    hat_across = swap(hat_far, "tensor", 2)
-    grad_hat = hat_own + hat_across.astype(f32)
-    mix_order = down_order[::-1]
-    mix_grads = mix_grad
-    for n, bit in enumerate(mix_order):
-        landed = [(hat_far, branch_across), hat_across][n] if n < 2 else None
-        mix_grads, sums = scatter_step(mix_grads, chunk, mix_order[n:], bit, None, landed, sums)
-    ffn_grads = scatter_step(ffn_first, chunk, ffn_order[1:], ffn_order[1], None, mid_grad)
-    for n in range(2, bits):
-        ffn_grads = scatter_step(ffn_grads, chunk, ffn_order[n:], ffn_order[n], None, hat_across)
     own, inv_std = normalize(hidden_in.astype(f32))
     first_mean = jnp.mean(grad_hat, axis=-1, keepdims=True)
     second_mean = jnp.mean(grad_hat * own, axis=-1, keepdims=True)
     grad_hidden = out_grad.astype(f32) + inv_std * (grad_hat - first_mean - own * second_mean)
     norm_sums = sums + swap(sums, "tensor", 1)
-    norm_sums = norm_sums + swap(norm_sums, "tensor", 2)
+    norm_sums = norm_sums + swap(after(norm_sums, branch_across), "tensor", 2)
     head_sums = sums[2, : 2 * W].reshape(heads, 2, HD)[:, 1].reshape(W)
     pair_grad = jnp.stack([sums[2, 2 * W : 3 * W], head_sums])
-    kv_grads = mix_grads[:, : 2 * W].reshape(chunk, heads, 2, HD)
-    triple_grad = jnp.stack(
-        [mix_grads[:, 2 * W : 3 * W], kv_grads[:, :, 0].reshape(chunk, W), kv_grads[:, :, 1].reshape(chunk, W)], axis=1
-    )
     return (
         result,
         grad_hidden,
@@ -655,10 +754,10 @@
         norm_sums[4],
         triple_grad,
         pair_grad,
-        mix_grads[:, 3 * W :].T,
-        ffn_grads[:, :F],
+        out_grad_t,
+        up_grad,
         sums[5],
-        ffn_grads[:, F:].T,
+        down_grad,
         norm_sums[6],
     )
 

time: 262 us -> 258 us (0.985)
  starting transfers between devices: 61.1 us -> 41.2 us
  Pallas kernels: 92.3 us -> 105 us
  waiting for transfers between devices: 59 us -> 65.1 us
  other arithmetic: 20 us -> 14.6 us
  local copies, waits for them, and re-layouts: 26.6 us -> 30.7 us
    ppermute x27, starting transfers between devices: 54.5 us -> 35.7 us  [swap(): return lax.ppermute(value, axis, [(i, i ^ mask) for i in range(count)])]
    pallas_call x2, Pallas kernels: 24.9 us -> 32.5 us  [attention(): pl.pallas_call(functools.partial(attn_kernel, T=T, blk=blk, heads=heads,...]
    pallas_call x4 -> x6, Pallas kernels: 56.7 us -> 61.9 us  [the longest x1 30.3 us: ffn(): pl.pallas_call(functools.partial(ffn_kernel, pieces=len(gs), blk=blk, chu...]
    ppermute x3, waiting for transfers between devices: 2.27 us -> 6.85 us  [shift(): return lax.ppermute(value, axis, route)]
    another operation x4, local copies, waits for them, and re-layouts: 0.02 us -> 2.76 us  [shards(): gains = jnp.stack([mixer_gain, mixer_shift, feed_gain, feed_shift])]
    unnamed x64 -> x67, local copies, waits for them, and re-layouts: 10.9 us -> 13.2 us
  transfers between devices with their start and end apart: 30 -> 30, of which waited for: 12 -> 14; matrix products, arithmetic and copies ran while one was open for 13% -> 13% of each run, Pallas kernels for 35% -> 41%
where the time goes in v2:
time: 258 us
  Pallas kernels  105 us (41%)
  waiting for transfers between devices  65.1 us (25%)
  starting transfers between devices  41.2 us (16%)
  local copies, waits for them, and re-layouts  30.7 us (12%)
  other arithmetic  14.6 us (6%)
    ppermute x27, waiting for transfers between devices, swap(): return lax.ppermute(value, axis, [(i, i ^ mask) for i in range(count)])  58.3 us
    ppermute x27, starting transfers between devices, swap(): return lax.ppermute(value, axis, [(i, i ^ mask) for i in range(count)])  35.7 us
    pallas_call x2, Pallas kernels, attention(): pl.pallas_call(functools.partial(attn_kernel, T=T, blk=blk, heads=heads,...  32.5 us
    pallas_call x1, Pallas kernels, ffn(): pl.pallas_call(functools.partial(ffn_kernel, pieces=len(gs), blk=blk, chu...  30.3 us
    pallas_call x2, Pallas kernels, post(): pl.pallas_call(functools.partial(post_kernel, chunk=chunk), grid_spec=plt...  17.8 us
    unnamed x67, local copies, waits for them, and re-layouts  13.2 us
    pallas_call x1, Pallas kernels, pre(): pl.pallas_call(functools.partial(pre_kernel, pieces=len(hids), blk=blk),...  10.7 us
    pallas_call x1, Pallas kernels, mid(): pl.pallas_call(mid_kernel, grid=(T // MR,), in_specs=[cols, cols, rows, r...  9.66 us
  transfers between devices with their start and end apart: 30, of which 14 were waited for; matrix products, arithmetic and copies ran while one was open for 13% of the time, Pallas kernels for 41%

profile of v2, /device:TPU:0, one launch (start us, length us, event | category | flops | bytes accessed | tf_op | source)
XLA Modules:
  0.0 258.1 jit_solution(9291445906349694931)
XLA Ops:
  1.2 2.6 collective-permute-start.1
  6.0 2.6 %collective-permute-start.3 = (bf16[96,640]{1,0:T(8,128)(2,1)S(1)}, bf16[96,640]{1,0:T(8,128)(2,1)S(1)}, u32[]{:S(2)}, u32[]{:S(2)}) collective-permute-start(bf16[96,640]{1,0:T(8,128)(2,1)S(1)} %pad_maximum_fusion.12), channel_id=1, source_target_pairs={{0,16},{4,20},{8,24},{12,28},{16,0},{20,4},{24,8},{28,12},{1,17},{... | collective-permute-start | bytes 368648 | tf_op jit(solution)/shard_map/ppermute | solution.py:42
  17.2 6.1 %collective-permute-done.4 = bf16[192,640]{1,0:T(8,128)(2,1)S(1)} collective-permute-done((bf16[192,640]{1,0:T(8,128)(2,1)S(1)}, bf16[192,640]{1,0:T(8,128)(2,1)S(1)}, u32[]{:S(2)}, u32[]{:S(2)}) %collective-permute-start.4) | collective-permute-done | bytes 245792 | tf_op jit(solution)/shard_map/ppermute | solution.py:42
  25.0 2.1 collective-permute-start.6
  29.3 4.3 %collective-permute-done.6 = bf16[96,768]{1,0:T(8,128)(2,1)S(1)} collective-permute-done((bf16[96,768]{1,0:T(8,128)(2,1)S(1)}, bf16[96,768]{1,0:T(8,128)(2,1)S(1)}, u32[]{:S(2)}, u32[]{:S(2)}) %collective-permute-start.6) | collective-permute-done | bytes 147488 | tf_op jit(solution)/shard_map/ppermute | solution.py:42
  34.4 3.4 %collective-permute-start.7 = (bf16[96,896]{1,0:T(8,128)(2,1)S(1)}, bf16[96,896]{1,0:T(8,128)(2,1)S(1)}, u32[]{:S(2)}, u32[]{:S(2)}) collective-permute-start(bf16[96,896]{1,0:T(8,128)(2,1)S(1)} %pad_maximum_fusion.10), channel_id=1, source_target_pairs={{0,16},{4,20},{8,24},{12,28},{16,0},{20,4},{24,8},{28,12},{1,17},{... | collective-permute-start | bytes 516104 | tf_op jit(solution)/shard_map/ppermute | solution.py:42
  39.8 5.5 %collective-permute-done.9 = bf16[192,768]{1,0:T(8,128)(2,1)S(1)} collective-permute-done((bf16[192,768]{1,0:T(8,128)(2,1)S(1)}, bf16[192,768]{1,0:T(8,128)(2,1)S(1)}, u32[]{:S(2)}, u32[]{:S(2)}) %collective-permute-start.9) | collective-permute-done | bytes 294944 | tf_op jit(solution)/shard_map/ppermute | solution.py:42
  46.1 2.6 %collective-permute-start.8 = (bf16[192,896]{1,0:T(8,128)(2,1)S(1)}, bf16[192,896]{1,0:T(8,128)(2,1)S(1)}, u32[]{:S(2)}, u32[]{:S(2)}) collective-permute-start(bf16[192,896]{1,0:T(8,128)(2,1)S(1)} %bitcast.105), channel_id=1, source_target_pairs={{0,8},{4,12},{8,0},{12,4},{16,24},{20,28},{24,16},{28,20},{1,9},{5... | collective-permute-start | bytes 1032200 | tf_op jit(solution)/shard_map/ppermute | solution.py:42
  49.9 10.7 %pre.1 = (bf16[2048,768]{1,0:T(8,128)(2,1)}, bf16[3,2048,128]{2,1,0:T(8,128)(2,1)}, bf16[3,2048,128]{2,1,0:T(8,128)(2,1)}) custom-call(bf16[512,768]{1,0:T(8,128)(2,1)} %refs_0_.3, bf16[512,768]{1,0:T(8,128)(2,1)} %copy-done.13, bf16[512,768]{1,0:T(8,128)(2,1)} %copy-done.14, bf16[512,768]{1,0:T(8,128)(2,1)} %copy-done.15, ...), custom_call_target="tpu_custom_call" | custom-call | flops 575000000 | bytes 1000 | tf_op jit(solution)/shard_map/pre/pallas_call | solution.py:199
  63.2 15.4 %collective-permute-done.11 = bf16[384,896]{1,0:T(8,128)(2,1)S(1)} collective-permute-done((bf16[384,896]{1,0:T(8,128)(2,1)S(1)}, bf16[384,896]{1,0:T(8,128)(2,1)S(1)}, u32[]{:S(2)}, u32[]{:S(2)}) %collective-permute-start.11) | collective-permute-done | bytes 688160 | tf_op jit(solution)/shard_map/ppermute | solution.py:42
  80.8 2.7 %collective-permute-start.12 = (bf16[3,2048,128]{2,1,0:T(8,128)(2,1)S(1)}, bf16[3,2048,128]{2,1,0:T(8,128)(2,1)S(1)}, u32[]{:S(2)}, u32[]{:S(2)}) collective-permute-start(bf16[3,2048,128]{2,1,0:T(8,128)(2,1)S(1)} %copy-done), channel_id=1, source_target_pairs={{0,4},{4,8},{8,12},{12,16},{16,20},{20,24},{24,28},{1,5},{5,9},{9,... | collective-permute-start | bytes 4718600 | tf_op jit(solution)/shard_map/ppermute | solution.py:48
  84.1 2.1 collective-permute-done.13.refs_5_
  87.3 30.3 %ffn.1 = (bf16[2048,768]{1,0:T(8,128)(2,1)}, bf16[2048,768]{1,0:T(8,128)(2,1)}, bf16[2048,768]{1,0:T(8,128)(2,1)}, bf16[2048,768]{1,0:T(8,128)(2,1)}, bf16[3,204...) custom-call(bf16[512,768]{1,0:T(8,128)(2,1)} %refs_0_.3, ...), custom_call_target="tpu_custom_call" | custom-call | flops 575000000 | bytes 1000 | tf_op jit(solution)/shard_map/ffn/pallas_call | solution.py:289
  120.3 9.5 %attn.2 = (bf16[192,1024]{1,0:T(8,128)(2,1)S(1)}, bf16[192,1024]{1,0:T(8,128)(2,1)S(1)}, bf16[3,1024,128]{2,1,0:T(8,128)(2,1)S(1)}, f32[3,2048,128]{2,1,0:T(8,128)S(1)}) custom-call(s32[2]{0:T(128)S(1)} %pad_add_fusion.refs_0_.place_ref, s32[8]{0:T(128)S(1)} %and_select_fusion.refs_1_, s32[1,2048]{1,0:T(1,128)S(1)} %add_subtract_fusion.refs_2_, ...), custom_call_target="tpu_custom_call" | custom-call | flops 115000000 | bytes 1000 | tf_op jit(solution)/shard_map/attn/pallas_call | solution.py:444
  129.8 1.6 copy-done.3
  132.8 23.1 %attn.3 = (bf16[192,2048]{1,0:T(8,128)(2,1)S(1)}, bf16[192,2048]{1,0:T(8,128)(2,1)S(1)}, bf16[3,1024,128]{2,1,0:T(8,128)(2,1)S(1)}, f32[3,1024,128]{2,1,0:T(8,128)S(1)}, f32[3,1024,128]{2,1,0:T(8,128)S(1)}) custom-call(s32[2]{0:T(128)S(1)} %pad_add_fusion.refs_0_.place_ref, s32[8]{0:T(128)S(1)} %and_select_fusion.refs_1_, ...), custom_call_target="tpu_custom_call" | custom-call | flops 115000000 | bytes 1000 | tf_op jit(solution)/shard_map/attn/pallas_call | solution.py:444
  155.9 6.8 %collective-permute-done.16.ahead_ref = bf16[3,1024,128]{2,1,0:T(8,128)(2,1)S(1)} collective-permute-done((bf16[3,1024,128]{2,1,0:T(8,128)(2,1)S(1)}, bf16[3,1024,128]{2,1,0:T(8,128)(2,1)S(1)}, u32[]{:S(2)}, u32[]{:S(2)}) %collective-permute-start.16) | collective-permute-done | bytes 786464 | tf_op jit(solution)/shard_map/ppermute | solution.py:48
  164.7 8.6 %post.2 = (bf16[2048,768]{1,0:T(8,128)(2,1)}, f32[768,384]{1,0:T(8,128)}, f32[8,768]{1,0:T(8,128)}) custom-call(s32[2]{0:T(128)} %copy-done.9, f32[3,1024,128]{2,1,0:T(8,128)} %copy-done.7, bf16[3,1024,128]{2,1,0:T(8,128)(2,1)} %copy-done.19, bf16[192,2048]{1,0:T(8,128)(2,1)} %copy-done.4, f32[8,2048]{1,0:T(8,128)} %get-tuple-element.206.refs_7_.cos_ref, ...), custom_call_target="tpu_custom_call" | custom-call | flops 115000000 | bytes 1000 | tf_op jit(solution)/shard_map/post/pallas_call | solution.py:582
  173.4 3.3 %collective-permute-start.20 = (bf16[192,1536]{1,0:T(8,128)(2,1)S(1)}, bf16[192,1536]{1,0:T(8,128)(2,1)S(1)}, u32[]{:S(2)}, u32[]{:S(2)}) collective-permute-start(bf16[192,1536]{1,0:T(8,128)(2,1)S(1)} %bitcast.101), channel_id=1, source_target_pairs={{0,8},{4,12},{8,0},{12,4},{16,24},{20,28},{24,16},{28,20},{1,9},{5... | collective-permute-start | bytes 1769480 | tf_op jit(solution)/shard_map/ppermute | solution.py:42
  176.7 9.7 %mid.1 = (bf16[2048,768]{1,0:T(8,128)(2,1)}, bf16[768,384]{1,0:T(8,128)(2,1)}) custom-call(bf16[192,2048]{1,0:T(8,128)(2,1)} %copy-done.8, bf16[192,2048]{1,0:T(8,128)(2,1)} %copy-done.4, bf16[2048,768]{1,0:T(8,128)(2,1)} %get-tuple-element.93.mixer_ref, bf16[2048,768]{1,0:T(8,128)(2,1)} %get-tuple-element.98.g_ref, ...), custom_call_target="tpu_custom_call" | custom-call | flops 115000000 | bytes 1000 | tf_op jit(solution)/shard_map/mid/pallas_call | solution.py:491
  187.2 9.2 %post.3 = (bf16[2048,768]{1,0:T(8,128)(2,1)}, bf16[400,768]{1,0:T(8,128)(2,1)}, bf16[384,768]{1,0:T(8,128)(2,1)}, f32[8,768]{1,0:T(8,128)}) custom-call(s32[2]{0:T(128)} %copy-done.9, f32[3,1024,128]{2,1,0:T(8,128)} %copy-done.10, bf16[3,1024,128]{2,1,0:T(8,128)(2,1)} %copy-done.29, bf16[192,2048]{1,0:T(8,128)(2,1)} %copy-done.4, ...), custom_call_target="tpu_custom_call", output_to_operand_aliasing={{0}: (11, {})} | custom-call | flops 9200000000 | bytes 1000 | tf_op jit(solution)/shard_map/post/pallas_call | solution.py:582
  196.7 1.7 slice.144
  202.4 7.6 %collective-permute-start.25 = (bf16[96,1536]{1,0:T(8,128)(2,1)S(1)}, bf16[96,1536]{1,0:T(8,128)(2,1)S(1)}, u32[]{:S(2)}, u32[]{:S(2)}) collective-permute-start(bf16[96,1536]{1,0:T(8,128)(2,1)S(1)} %fusion.11), channel_id=1, source_target_pairs={{0,16},{4,20},{8,24},{12,28},{16,0},{20,4},{24,8},{28,12},{1,17},{... | collective-permute-start | bytes 884744 | tf_op jit(solution)/shard_map/ppermute | solution.py:42
  211.9 4.4 %collective-permute-done.24 = bf16[400,768]{1,0:T(8,128)(2,1)S(1)} collective-permute-done((bf16[400,768]{1,0:T(8,128)(2,1)S(1)}, bf16[400,768]{1,0:T(8,128)(2,1)S(1)}, u32[]{:S(2)}, u32[]{:S(2)}) %collective-permute-start.24) | collective-permute-done | bytes 614432 | tf_op jit(solution)/shard_map/ppermute | solution.py:42
  216.3 6.4 %collective-permute-done.25.other_ref = bf16[96,1536]{1,0:T(8,128)(2,1)S(1)} collective-permute-done((bf16[96,1536]{1,0:T(8,128)(2,1)S(1)}, bf16[96,1536]{1,0:T(8,128)(2,1)S(1)}, u32[]{:S(2)}, u32[]{:S(2)}) %collective-permute-start.25) | collective-permute-done | bytes 294944 | tf_op jit(solution)/shard_map/ppermute | solution.py:42
  224.5 8.5 %collective-permute-done.26 = bf16[208,768]{1,0:T(8,128)(2,1)S(1)} collective-permute-done((bf16[208,768]{1,0:T(8,128)(2,1)S(1)}, bf16[208,768]{1,0:T(8,128)(2,1)S(1)}, u32[]{:S(2)}, u32[]{:S(2)}) %collective-permute-start.26) | collective-permute-done | bytes 319520 | tf_op jit(solution)/shard_map/ppermute | solution.py:42
  236.6 2.2 ffn_finish.1
  238.8 1.9 copy.51
  240.6 3.4 %collective-permute-done.27.other_ref = bf16[112,768]{1,0:T(8,128)(2,1)S(1)} collective-permute-done((bf16[112,768]{1,0:T(8,128)(2,1)S(1)}, bf16[112,768]{1,0:T(8,128)(2,1)S(1)}, u32[]{:S(2)}, u32[]{:S(2)}) %collective-permute-start.27) | collective-permute-done | bytes 172064 | tf_op jit(solution)/shard_map/ppermute | solution.py:42
  244.7 2.0 mix_finish.1
  250.2 1.8 copy.50
  253.5 4.0 %fusion.7 = (f32[512,768]{1,0:T(8,128)}, f32[512,768]{1,0:T(8,128)}) fusion(bf16[512,768]{1,0:T(8,128)(2,1)S(1)} %copy-done.11, f32[512,768]{1,0:T(8,128)S(1)} %get-tuple-element.177, bf16[512,768]{1,0:T(8,128)(2,1)} %refs_4_, f32[512]{0:T(512)S(1)} %get-tuple-element.213, f32[512]{0:T(512)S(1)} %get-tuple-element.214, f32[512]{0:T(512)S(1)} %add_rsqrt_fusion, ...), kind=kLoop, calls=%fused_computation.13 | loop fusion | flops 5111808 | bytes 8662016 | tf_op jit(solution)/shard_map/add | solution.py:743
  (197 shorter events, 50.9 us)
Async XLA Ops:
  0.6 48.0 %collective-permute-start = (bf16[512,768]{1,0:T(8,128)(2,1)}, bf16[512,768]{1,0:T(8,128)(2,1)S(1)}, u32[]{:S(2)}, u32[]{:S(2)}) collective-permute-start(bf16[512,768]{1,0:T(8,128)(2,1)} %refs_0_.3), channel_id=1, source_target_pairs={{0,1},{1,0},{2,3},{3,2},{4,5},{5,4},{6,7},{7,6},{8,9},{9,8},{10,11... | collective-permute-start | bytes 2359304 | tf_op jit(solution)/shard_map/ppermute | solution.py:42
  1.2 36.6 %collective-permute-start.1 = (bf16[512,768]{1,0:T(8,128)(2,1)}, bf16[512,768]{1,0:T(8,128)(2,1)S(1)}, u32[]{:S(2)}, u32[]{:S(2)}) collective-permute-start(bf16[512,768]{1,0:T(8,128)(2,1)} %refs_0_.3), channel_id=1, source_target_pairs={{0,2},{1,3},{2,0},{3,1},{4,6},{5,7},{6,4},{7,5},{8,10},{9,11},{10,... | collective-permute-start | bytes 2359304 | tf_op jit(solution)/shard_map/ppermute | solution.py:42
  6.0 9.3 %collective-permute-start.3 = (bf16[96,640]{1,0:T(8,128)(2,1)S(1)}, bf16[96,640]{1,0:T(8,128)(2,1)S(1)}, u32[]{:S(2)}, u32[]{:S(2)}) collective-permute-start(bf16[96,640]{1,0:T(8,128)(2,1)S(1)} %pad_maximum_fusion.12), channel_id=1, source_target_pairs={{0,16},{4,20},{8,24},{12,28},{16,0},{20,4},{24,8},{28,12},{1,17},{... | collective-permute-start | bytes 368648 | tf_op jit(solution)/shard_map/ppermute | solution.py:42
  15.5 7.8 %collective-permute-start.4 = (bf16[192,640]{1,0:T(8,128)(2,1)S(1)}, bf16[192,640]{1,0:T(8,128)(2,1)S(1)}, u32[]{:S(2)}, u32[]{:S(2)}) collective-permute-start(bf16[192,640]{1,0:T(8,128)(2,1)S(1)} %bitcast.109), channel_id=1, source_target_pairs={{0,8},{4,12},{8,0},{12,4},{16,24},{20,28},{24,16},{28,20},{1,9},{5... | collective-permute-start | bytes 737288 | tf_op jit(solution)/shard_map/ppermute | solution.py:42
  23.5 14.3 %collective-permute-start.5 = (bf16[384,640]{1,0:T(8,128)(2,1)S(1)}, bf16[384,640]{1,0:T(8,128)(2,1)S(1)}, u32[]{:S(2)}, u32[]{:S(2)}) collective-permute-start(bf16[384,640]{1,0:T(8,128)(2,1)S(1)} %bitcast.97), channel_id=1, source_target_pairs={{0,4},{4,0},{8,12},{12,8},{16,20},{20,16},{24,28},{28,24},{1,5},{5... | collective-permute-start | bytes 1474568 | tf_op jit(solution)/shard_map/ppermute | solution.py:42
  25.0 8.5 %collective-permute-start.6 = (bf16[96,768]{1,0:T(8,128)(2,1)S(1)}, bf16[96,768]{1,0:T(8,128)(2,1)S(1)}, u32[]{:S(2)}, u32[]{:S(2)}) collective-permute-start(bf16[96,768]{1,0:T(8,128)(2,1)S(1)} %copy-done.24), channel_id=1, source_target_pairs={{0,16},{4,20},{8,24},{12,28},{16,0},{20,4},{24,8},{28,12},{1,17},{... | collective-permute-start | bytes 442376 | tf_op jit(solution)/shard_map/ppermute | solution.py:42
  33.7 11.6 %collective-permute-start.9 = (bf16[192,768]{1,0:T(8,128)(2,1)S(1)}, bf16[192,768]{1,0:T(8,128)(2,1)S(1)}, u32[]{:S(2)}, u32[]{:S(2)}) collective-permute-start(bf16[192,768]{1,0:T(8,128)(2,1)S(1)} %bitcast.106), channel_id=1, source_target_pairs={{0,8},{4,12},{8,0},{12,4},{16,24},{20,28},{24,16},{28,20},{1,9},{5... | collective-permute-start | bytes 884744 | tf_op jit(solution)/shard_map/ppermute | solution.py:42
  34.4 11.6 %collective-permute-start.7 = (bf16[96,896]{1,0:T(8,128)(2,1)S(1)}, bf16[96,896]{1,0:T(8,128)(2,1)S(1)}, u32[]{:S(2)}, u32[]{:S(2)}) collective-permute-start(bf16[96,896]{1,0:T(8,128)(2,1)S(1)} %pad_maximum_fusion.10), channel_id=1, source_target_pairs={{0,16},{4,20},{8,24},{12,28},{16,0},{20,4},{24,8},{28,12},{1,17},{... | collective-permute-start | bytes 516104 | tf_op jit(solution)/shard_map/ppermute | solution.py:42
  37.8 10.9 %collective-permute-start.2 = (bf16[512,768]{1,0:T(8,128)(2,1)S(1)}, bf16[512,768]{1,0:T(8,128)(2,1)S(1)}, u32[]{:S(2)}, u32[]{:S(2)}) collective-permute-start(bf16[512,768]{1,0:T(8,128)(2,1)S(1)} %collective-permute-done.1.refs_2_), channel_id=1, source_target_pairs={{0,1},{1,0},{2,3},{3,2},{4,5},{5,4},{6,7},{7,6},{8,9},{9,8},{10,11... | collective-permute-start | bytes 2359304 | tf_op jit(solution)/shard_map/ppermute | solution.py:42
  45.4 15.2 %collective-permute-start.10 = (bf16[384,768]{1,0:T(8,128)(2,1)S(1)}, bf16[384,768]{1,0:T(8,128)(2,1)S(1)}, u32[]{:S(2)}, u32[]{:S(2)}) collective-permute-start(bf16[384,768]{1,0:T(8,128)(2,1)S(1)} %bitcast.96), channel_id=1, source_target_pairs={{0,4},{4,0},{8,12},{12,8},{16,20},{20,16},{24,28},{28,24},{1,5},{5... | collective-permute-start | bytes 1769480 | tf_op jit(solution)/shard_map/ppermute | solution.py:42
  46.1 15.9 %collective-permute-start.8 = (bf16[192,896]{1,0:T(8,128)(2,1)S(1)}, bf16[192,896]{1,0:T(8,128)(2,1)S(1)}, u32[]{:S(2)}, u32[]{:S(2)}) collective-permute-start(bf16[192,896]{1,0:T(8,128)(2,1)S(1)} %bitcast.105), channel_id=1, source_target_pairs={{0,8},{4,12},{8,0},{12,4},{16,24},{20,28},{24,16},{28,20},{1,9},{5... | collective-permute-start | bytes 1032200 | tf_op jit(solution)/shard_map/ppermute | solution.py:42
  62.1 16.5 %collective-permute-start.11 = (bf16[384,896]{1,0:T(8,128)(2,1)S(1)}, bf16[384,896]{1,0:T(8,128)(2,1)S(1)}, u32[]{:S(2)}, u32[]{:S(2)}) collective-permute-start(bf16[384,896]{1,0:T(8,128)(2,1)S(1)} %bitcast.95), channel_id=1, source_target_pairs={{0,4},{4,0},{8,12},{12,8},{16,20},{20,16},{24,28},{28,24},{1,5},{5... | collective-permute-start | bytes 2064392 | tf_op jit(solution)/shard_map/ppermute | solution.py:42
  62.7 20.9 %collective-permute-start.14 = (bf16[512,768]{1,0:T(8,128)(2,1)}, bf16[512,768]{1,0:T(8,128)(2,1)}, u32[]{:S(2)}, u32[]{:S(2)}) collective-permute-start(bf16[512,768]{1,0:T(8,128)(2,1)} %refs_4_), channel_id=1, source_target_pairs={{0,2},{1,3},{2,0},{3,1},{4,6},{5,7},{6,4},{7,5},{8,10},{9,11},{10,... | collective-permute-start | bytes 2359304 | tf_op jit(solution)/shard_map/ppermute | solution.py:42
  80.8 36.8 %collective-permute-start.12 = (bf16[3,2048,128]{2,1,0:T(8,128)(2,1)S(1)}, bf16[3,2048,128]{2,1,0:T(8,128)(2,1)S(1)}, u32[]{:S(2)}, u32[]{:S(2)}) collective-permute-start(bf16[3,2048,128]{2,1,0:T(8,128)(2,1)S(1)} %copy-done), channel_id=1, source_target_pairs={{0,4},{4,8},{8,12},{12,16},{16,20},{20,24},{24,28},{1,5},{5,9},{9,... | collective-permute-start | bytes 4718600 | tf_op jit(solution)/shard_map/ppermute | solution.py:48
  83.5 2.7 %collective-permute-start.13 = (bf16[512,768]{1,0:T(8,128)(2,1)}, bf16[512,768]{1,0:T(8,128)(2,1)}, u32[]{:S(2)}, u32[]{:S(2)}) collective-permute-start(bf16[512,768]{1,0:T(8,128)(2,1)} %refs_4_), channel_id=1, source_target_pairs={{0,1},{1,0},{2,3},{3,2},{4,5},{5,4},{6,7},{7,6},{8,9},{9,8},{10,11... | collective-permute-start | bytes 2359304 | tf_op jit(solution)/shard_map/ppermute | solution.py:42
  83.6 3.7 %collective-permute-start.15 = (bf16[512,768]{1,0:T(8,128)(2,1)}, bf16[512,768]{1,0:T(8,128)(2,1)}, u32[]{:S(2)}, u32[]{:S(2)}) collective-permute-start(bf16[512,768]{1,0:T(8,128)(2,1)} %collective-permute-done.14.refs_6_), channel_id=1, source_target_pairs={{0,1},{1,0},{2,3},{3,2},{4,5},{5,4},{6,7},{7,6},{8,9},{9,8},{10,11... | collective-permute-start | bytes 2359304 | tf_op jit(solution)/shard_map/ppermute | solution.py:42
  87.3 31.6 %copy-start.5 = (f32[8,2048]{1,0:T(8,128)S(1)}, f32[8,2048]{1,0:T(8,128)}, u32[]{:S(2)}) copy-start(f32[8,2048]{1,0:T(8,128)} %get-tuple-element.205.refs_8_.sin_ref) | copy-start | bytes 196612
  87.3 31.6 %copy-start.6 = (f32[8,2048]{1,0:T(8,128)S(1)}, f32[8,2048]{1,0:T(8,128)}, u32[]{:S(2)}) copy-start(f32[8,2048]{1,0:T(8,128)} %get-tuple-element.206.refs_7_.cos_ref) | copy-start | bytes 196612
  117.6 45.1 %collective-permute-start.17 = (bf16[384,1536]{1,0:T(8,128)(2,1)}, bf16[384,1536]{1,0:T(8,128)(2,1)S(1)}, u32[]{:S(2)}, u32[]{:S(2)}) collective-permute-start(bf16[384,1536]{1,0:T(8,128)(2,1)} %get-tuple-element.89), channel_id=1, source_target_pairs={{0,4},{4,0},{8,12},{12,8},{16,20},{20,16},{24,28},{28,24},{1,5},{5... | collective-permute-start | bytes 3538952 | tf_op jit(solution)/shard_map/ppermute | solution.py:42
  131.5 31.3 %collective-permute-start.16 = (bf16[3,1024,128]{2,1,0:T(8,128)(2,1)S(1)}, bf16[3,1024,128]{2,1,0:T(8,128)(2,1)S(1)}, u32[]{:S(2)}, u32[]{:S(2)}) collective-permute-start(bf16[3,1024,128]{2,1,0:T(8,128)(2,1)S(1)} %get-tuple-element.86), channel_id=1, source_target_pairs={{4,0},{8,4},{12,8},{16,12},{20,16},{24,20},{28,24},{5,1},{9,5},{13... | collective-permute-start | bytes 2359304 | tf_op jit(solution)/shard_map/ppermute | solution.py:48
  162.8 23.6 %collective-permute-start.19 = (bf16[3,1024,128]{2,1,0:T(8,128)(2,1)S(1)}, bf16[3,1024,128]{2,1,0:T(8,128)(2,1)S(1)}, u32[]{:S(2)}, u32[]{:S(2)}) collective-permute-start(bf16[3,1024,128]{2,1,0:T(8,128)(2,1)S(1)} %get-tuple-element.103), channel_id=1, source_target_pairs={{4,0},{8,4},{12,8},{16,12},{20,16},{24,20},{28,24},{5,1},{9,5},{13... | collective-permute-start | bytes 2359304 | tf_op jit(solution)/shard_map/ppermute | solution.py:48
  173.4 23.3 %collective-permute-start.20 = (bf16[192,1536]{1,0:T(8,128)(2,1)S(1)}, bf16[192,1536]{1,0:T(8,128)(2,1)S(1)}, u32[]{:S(2)}, u32[]{:S(2)}) collective-permute-start(bf16[192,1536]{1,0:T(8,128)(2,1)S(1)} %bitcast.101), channel_id=1, source_target_pairs={{0,8},{4,12},{8,0},{12,4},{16,24},{20,28},{24,16},{28,20},{1,9},{5... | collective-permute-start | bytes 1769480 | tf_op jit(solution)/shard_map/ppermute | solution.py:42
  198.3 3.5 %collective-permute-start.21 = (bf16[1024,768]{1,0:T(8,128)(2,1)S(1)}, bf16[1024,768]{1,0:T(8,128)(2,1)S(1)}, u32[]{:S(2)}, u32[]{:S(2)}) collective-permute-start(bf16[1024,768]{1,0:T(8,128)(2,1)S(1)} %slice.144), channel_id=1, source_target_pairs={{0,1},{1,0},{2,3},{3,2},{4,5},{5,4},{6,7},{7,6},{8,9},{9,8},{10,11... | collective-permute-start | bytes 4718600 | tf_op jit(solution)/shard_map/ppermute | solution.py:42
  199.4 10.6 %collective-permute-start.18 = (bf16[1024,768]{1,0:T(8,128)(2,1)S(1)}, bf16[1024,768]{1,0:T(8,128)(2,1)S(1)}, u32[]{:S(2)}, u32[]{:S(2)}) collective-permute-start(bf16[1024,768]{1,0:T(8,128)(2,1)S(1)} %slice.138), channel_id=1, source_target_pairs={{0,1},{1,0},{2,3},{3,2},{4,5},{5,4},{6,7},{7,6},{8,9},{9,8},{10,11... | collective-permute-start | bytes 4718600 | tf_op jit(solution)/shard_map/ppermute | solution.py:42
  200.3 16.0 %collective-permute-start.24 = (bf16[400,768]{1,0:T(8,128)(2,1)S(1)}, bf16[400,768]{1,0:T(8,128)(2,1)S(1)}, u32[]{:S(2)}, u32[]{:S(2)}) collective-permute-start(bf16[400,768]{1,0:T(8,128)(2,1)S(1)} %copy-done.30), channel_id=1, source_target_pairs={{0,4},{4,0},{8,12},{12,8},{16,20},{20,16},{24,28},{28,24},{1,5},{5... | collective-permute-start | bytes 1843208 | tf_op jit(solution)/shard_map/ppermute | solution.py:42
  202.4 20.3 %collective-permute-start.25 = (bf16[96,1536]{1,0:T(8,128)(2,1)S(1)}, bf16[96,1536]{1,0:T(8,128)(2,1)S(1)}, u32[]{:S(2)}, u32[]{:S(2)}) collective-permute-start(bf16[96,1536]{1,0:T(8,128)(2,1)S(1)} %fusion.11), channel_id=1, source_target_pairs={{0,16},{4,20},{8,24},{12,28},{16,0},{20,4},{24,8},{28,12},{1,17},{... | collective-permute-start | bytes 884744 | tf_op jit(solution)/shard_map/ppermute | solution.py:42
  211.3 21.7 %collective-permute-start.22 = (bf16[512,768]{1,0:T(8,128)(2,1)S(1)}, bf16[512,768]{1,0:T(8,128)(2,1)S(1)}, u32[]{:S(2)}, u32[]{:S(2)}) collective-permute-start(bf16[512,768]{1,0:T(8,128)(2,1)S(1)} %slice.244), channel_id=1, source_target_pairs={{0,2},{1,3},{2,0},{3,1},{4,6},{5,7},{6,4},{7,5},{8,10},{9,11},{10,... | collective-permute-start | bytes 2359304 | tf_op jit(solution)/shard_map/ppermute | solution.py:42
  223.5 9.6 %collective-permute-start.26 = (bf16[208,768]{1,0:T(8,128)(2,1)S(1)}, bf16[208,768]{1,0:T(8,128)(2,1)S(1)}, u32[]{:S(2)}, u32[]{:S(2)}) collective-permute-start(bf16[208,768]{1,0:T(8,128)(2,1)S(1)} %pad_maximum_fusion.7), channel_id=1, source_target_pairs={{0,8},{4,12},{8,0},{12,4},{16,24},{20,28},{24,16},{28,20},{1,9},{5... | collective-permute-start | bytes 958472 | tf_op jit(solution)/shard_map/ppermute | solution.py:42
  233.9 10.2 %collective-permute-start.27 = (bf16[112,768]{1,0:T(8,128)(2,1)S(1)}, bf16[112,768]{1,0:T(8,128)(2,1)S(1)}, u32[]{:S(2)}, u32[]{:S(2)}) collective-permute-start(bf16[112,768]{1,0:T(8,128)(2,1)S(1)} %pad_maximum_fusion.11), channel_id=1, source_target_pairs={{0,16},{4,20},{8,24},{12,28},{16,0},{20,4},{24,8},{28,12},{1,17},{... | collective-permute-start | bytes 516104 | tf_op jit(solution)/shard_map/ppermute | solution.py:42
  234.6 18.3 %collective-permute-start.23 = (bf16[512,768]{1,0:T(8,128)(2,1)}, bf16[512,768]{1,0:T(8,128)(2,1)S(1)}, u32[]{:S(2)}, u32[]{:S(2)}) collective-permute-start(bf16[512,768]{1,0:T(8,128)(2,1)} %slice.245), channel_id=1, source_target_pairs={{0,2},{1,3},{2,0},{3,1},{4,6},{5,7},{6,4},{7,5},{8,10},{9,11},{10,... | collective-permute-start | bytes 2359304 | tf_op jit(solution)/shard_map/ppermute | solution.py:42
  246.7 5.3 %collective-permute-start.28 = (f32[8,768]{1,0:T(8,128)}, f32[8,768]{1,0:T(8,128)S(1)}, u32[]{:S(2)}, u32[]{:S(2)}) collective-permute-start(f32[8,768]{1,0:T(8,128)} %get-tuple-element.124), channel_id=1, source_target_pairs={{0,1},{1,0},{2,3},{3,2},{4,5},{5,4},{6,7},{7,6},{8,9},{9,8},{10,11... | collective-permute-start | bytes 73736 | tf_op jit(solution)/shard_map/ppermute | solution.py:42
  252.9 4.5 %collective-permute-start.29 = (f32[8,768]{1,0:T(8,128)S(1)}, f32[8,768]{1,0:T(8,128)S(1)}, u32[]{:S(2)}, u32[]{:S(2)}) collective-permute-start(f32[8,768]{1,0:T(8,128)S(1)} %add.131), channel_id=1, source_target_pairs={{0,2},{1,3},{2,0},{3,1},{4,6},{5,7},{6,4},{7,5},{8,10},{9,11},{10,... | collective-permute-start | bytes 73736 | tf_op jit(solution)/shard_map/ppermute | solution.py:42
  (29 other events, 231.6 us)

commit v3 on v2

--- a/solution.py
+++ b/solution.py
@@ -18,8 +18,8 @@
 NK = 2
 TR = 512
 FR = 512
-PR = 512
-MR = 512
+PR = 1024
+MR = 1024
 bf16 = jnp.bfloat16
 f32 = jnp.float32
 NN = (((1,), (0,)), ((), ()))
@@ -63,10 +63,10 @@
     return [own, near, far, diagonal]
 
 
-def scatter_core(blocks):
-    rows = blocks.shape[0] // 4
-    near = swap(blocks[2 * rows :], "tensor", 1).astype(f32)
-    total = blocks[: 2 * rows].astype(f32) + near
+def scatter_core(kept, sent):
+    near = swap(sent, "tensor", 1).astype(f32)
+    total = kept.astype(f32) + near
+    rows = kept.shape[0] // 2
     return total[:rows], total[rows:].astype(bf16)
 
 
@@ -89,7 +89,7 @@
         high = ((me >> bit) & 1) == 1
         above = 1 << sum(b > bit for b in done)
         one, two = held.reshape(above, -1, cols), other.reshape(above, -1, cols)
-        held = jnp.stack([jnp.where(high, two, one), jnp.where(high, one, two)], axis=1).reshape(-1, cols)
+        held = jnp.concatenate([jnp.where(high, two, one), jnp.where(high, one, two)], axis=1).reshape(-1, cols)
         done.append(bit)
         parts.append(held)
     return held, parts
@@ -461,14 +461,15 @@
     )(place, first, start, tail, kv, q, do, cos, sin, *early)
 
 
-def mid_kernel(o_ref, dq_ref, mixer_ref, g_ref, branch_ref, qkv_ref, down_ref, out_ref, grad_ref, acc_ref):
+def mid_kernel(o_ref, dq_ref, mixer_ref, g_ref, branch_ref, qkv_ref, down_ref, kept_ref, sent_ref, grad_ref, acc_ref):
     W = o_ref.shape[0]
     pad = qkv_ref.shape[1] - HD
     step = pl.program_id(0)
     o = o_ref[...]
     rows = jnp.concatenate([jnp.zeros((pad, o.shape[1]), f32), o.astype(f32)], axis=0).T.astype(bf16)
     out = mm(rows[:, : pad + HD], qkv_ref[...], NT) + mm(rows[:, pad + HD :], down_ref[...], NT)
-    out_ref[...] = (out + branch_ref[...].astype(f32)).astype(bf16)
+    out = (out + branch_ref[...].astype(f32)).astype(bf16)
+    kept_ref[...], sent_ref[...] = out[: MR // 2], out[MR // 2 :]
 
     @pl.when(step == 0)
     def _():
@@ -496,8 +497,8 @@
             pl.BlockSpec((D, 128), lambda i: (0, qkv.shape[1] // 128 - 1)),
             pl.BlockSpec((D, rest), lambda i: (0, down.shape[1] // rest - 1)),
         ],
-        out_specs=[pl.BlockSpec((MR, D), lambda i: (i // 2 + i % 2 * 2, 0)), whole_spec((D, 2 * W))],
-        out_shape=[jax.ShapeDtypeStruct((T, D), bf16), jax.ShapeDtypeStruct((D, 2 * W), bf16)],
+        out_specs=[rows_spec(D, MR // 2)] * 2 + [whole_spec((D, 2 * W))],
+        out_shape=[jax.ShapeDtypeStruct((T // 2, D), bf16)] * 2 + [jax.ShapeDtypeStruct((D, 2 * W), bf16)],
         scratch_shapes=[pltpu.VMEM((2 * W, D), f32)],
         compiler_params=pltpu.CompilerParams(vmem_limit_bytes=VMEM_LIMIT),
         cost_estimate=cost(0.1),
@@ -511,10 +512,10 @@
     step = pl.program_id(0)
     late = chunk is not None
     if late:
-        _, acc_in, sums_in, mid_ref, hat_ref, send_ref, keep_ref, sums_ref, acc_ref = refs
+        _, _, acc_in, sums_in, mid_ref, kept_ref, sent_ref, send_ref, keep_ref, sums_ref, acc_ref = refs
     else:
         acc_in = None
-        sums_in, hat_ref, grad_ref, sums_ref, acc_ref = refs
+        sums_in, kept_ref, sent_ref, grad_ref, sums_ref, acc_ref = refs
 
     @pl.when(step == 0)
     def _():
@@ -528,7 +529,8 @@
     acc_ref[...] += mm(mixer_ref[...], kv, TN)
     dq = dq_ref[...].astype(f32).T.astype(bf16)
     part = mm(kv, w_ref[:, : 2 * W], NT) + mm(dq, w_ref[:, 2 * W : 3 * W], NT)
-    hat_ref[...] = (part * gain_ref[...] + back_ref[...].astype(f32)).astype(bf16)
+    hat = (part * gain_ref[...] + back_ref[...].astype(f32)).astype(bf16)
+    kept_ref[...], sent_ref[...] = hat[: PR // 2], hat[PR // 2 :]
     sums_ref[0:1] += jnp.sum(part * normed_ref[...].astype(f32), axis=0, keepdims=True)
     sums_ref[1:2] += jnp.sum(part, axis=0, keepdims=True)
     sums_ref[2:3, : 2 * W] += jnp.sum(kv.astype(f32), axis=0, keepdims=True)
@@ -572,7 +574,7 @@
     late = len(early) > 1
     specs = [half, half, cols(W), cols(8), cols(8), rows(at), rows(at), rows(at), fixed(gain.shape), fixed(w.shape)]
     if late:
-        specs += [pl.BlockSpec(memory_space=pl.ANY), fixed((D, 2 * W)), fixed((8, D)), fixed((D, 2 * W))]
+        specs += [pl.BlockSpec(memory_space=pl.ANY)] * 2 + [fixed((D, 2 * W)), fixed((8, D)), fixed((D, 2 * W))]
         grads = [fixed((D // 2 + 16, 4 * W)), fixed((D // 2, 4 * W))]
         shapes = [jax.ShapeDtypeStruct((D // 2 + 16, 4 * W), bf16), jax.ShapeDtypeStruct((D // 2, 4 * W), bf16)]
     else:
@@ -585,15 +587,16 @@
             num_scalar_prefetch=1,
             grid=(per,),
             in_specs=specs,
-            out_specs=[rows(lambda i, place: at(i, place) // 2 + at(i, place) % 2 * 2)] + grads + [fixed((8, D))],
+            out_specs=[pl.BlockSpec((PR // 2, D), lambda i, place: (at(i, place), 0))] * 2 + grads + [fixed((8, D))],
             scratch_shapes=[pltpu.VMEM((D, 2 * W), f32)],
         ),
         out_shape=[
-            jax.ShapeDtypeStruct((T, D), bf16),
+            jax.ShapeDtypeStruct((T // 2, D), bf16),
+            jax.ShapeDtypeStruct((T // 2, D), bf16),
             *shapes,
             jax.ShapeDtypeStruct((8, D), f32),
         ],
-        input_output_aliases={11: 0} if late else {},
+        input_output_aliases={11: 0, 12: 1} if late else {},
         compiler_params=pltpu.CompilerParams(vmem_limit_bytes=VMEM_LIMIT),
         cost_estimate=cost(8 if late else 0.1),
         name="post",
@@ -606,9 +609,9 @@
     other = other_ref[...].astype(f32)
     total = keep_ref[...] + other[:rows]
     sums_ref[...] = own_ref[...] + (other[rows : rows + 8] + other[rows + 8 :])
-    triple_ref[:, 0, :] = total[:, 2 * W : 3 * W]
+    triple_ref[0] = total[:, 2 * W : 3 * W]
     for n in range(2):
-        triple_ref[:, 1 + n, :] = jnp.concatenate(
+        triple_ref[1 + n] = jnp.concatenate(
             [total[:, at + n * HD : at + (n + 1) * HD] for at in range(0, 2 * W, 2 * HD)], axis=1
         )
     out_ref[...] = total[:, 3 * W :].T
@@ -619,7 +622,7 @@
     return pl.pallas_call(
         mix_finish_kernel,
         out_shape=[
-            jax.ShapeDtypeStruct((rows, 3, W), f32),
+            jax.ShapeDtypeStruct((3, rows, W), f32),
             jax.ShapeDtypeStruct((W, rows), f32),
             jax.ShapeDtypeStruct(own.shape, f32),
         ],
@@ -632,7 +635,7 @@
     F = up_ref.shape[1]
     total = keep_ref[...] + other_ref[...].astype(f32)
     up_ref[...] = total[:, :F]
-    down_ref[...] = total[:, F:].T
+    down_ref[...] = total[:, F:]
 
 
 def ffn_finish(keep, other):
@@ -640,7 +643,7 @@
     F = cols // 2
     return pl.pallas_call(
         ffn_finish_kernel,
-        out_shape=[jax.ShapeDtypeStruct((rows, F), f32), jax.ShapeDtypeStruct((F, rows), f32)],
+        out_shape=[jax.ShapeDtypeStruct((rows, F), f32)] * 2,
         cost_estimate=cost(0.1),
         name="ffn_finish",
     )(keep, other)
@@ -665,7 +668,9 @@
     kv_w = jnp.concatenate([k_w, v_w], axis=2).reshape(chunk, 2 * W)
     pad = (-W) % 128
     out_own = output_weight.T
-    qkv_w, qkv_parts = gather_dp(jnp.concatenate([kv_w, q_w.reshape(chunk, W), out_own[:, :pad]], axis=1), down_order)
+    up_w, up_parts = gather_dp(up_weight, down_order)
+    qkv_own = jnp.concatenate([kv_w, q_w.reshape(chunk, W), out_own[:, :pad]], axis=1)
+    qkv_w, qkv_parts = gather_dp(qkv_own, down_order, [up_parts[0]])
     hids = gather_tensor(hidden_in)
     gs = gather_tensor(after(out_grad, hids[2]))
 
@@ -687,9 +692,8 @@
     mixer_in, kv, q = pre(hids, gains, qkv_w, bias, cos, sin, heads)
     feed_gains, feed_bias = gains[2:], up_bias[None]
     early_ops = (feed_gains, feed_bias, first, start)
-    up_w, up_parts = gather_dp(up_weight, down_order, [qkv_parts[-2]] + [None] * (bits - 2) + [qkv_w, (kv, early_ops)])
     down_own = jnp.concatenate([down_weight.T, out_own[:, pad:]], axis=1)
-    down_w, _ = gather_dp(down_own, down_order, [up_parts[0]] + [None] * (bits - 2) + [(kv, up_w)])
+    down_w, _ = gather_dp(down_own, down_order, [qkv_parts[-2]] + [None] * (bits - 2) + [(gs[2], up_w, early_ops)])
     tail = shift(after(kv, down_w), "dp", 1)
     normed, g, branch, back, do, ffn_send, ffn_keep, ffn_sums = ffn(
         hids, gs, feed_gains, up_w, down_w, qkv_w, feed_bias, high[None], heads, chunk
@@ -706,23 +710,23 @@
     ffn_send, ffn_keep = halves(ffn_first, chunk, ffn_order[1:], ffn_order[1])
     ffn_other = swap(ffn_send, "dp", 1 << ffn_order[1])
     early = post(0, spots, dkv_low, after(ahead_low, ffn_first), *post_args, early=(ffn_sums,))
-    branch, mid_grad = mid(after(o, early[2]), dq, mixer_in, g, branch, qkv_w, down_w)
-    hat, mix_send, mix_keep, sums = post(
+    *branch, mid_grad = mid(after(o, early[3]), dq, mixer_in, g, branch, qkv_w, down_w)
+    *hat, mix_send, mix_keep, sums = post(
         1, spots, dkv_high, ahead_high, *post_args, early=(*early, mid_grad), chunk=chunk
     )
     mix_order = ffn_order
-    hat, mix_send, mix_keep, sums, ffn_other = lax.optimization_barrier((hat, mix_send, mix_keep, sums, ffn_other))
+    *hat, mix_send, mix_keep, sums, ffn_other = lax.optimization_barrier((*hat, mix_send, mix_keep, sums, ffn_other))
     mix_other = swap(mix_send, "dp", 1 << mix_order[0])
-    hat_own, far = scatter_core(hat)
+    hat_own, far = scatter_core(*hat)
     landed_far = swap(far, "tensor", 2)
-    branch_own, branch_far = scatter_core(branch)
+    branch_own, branch_far = scatter_core(*branch)
     branch_across = swap(after(branch_far, landed_far), "tensor", 2)
     ffn_grads = ffn_keep.astype(f32) + after(ffn_other, far).astype(f32)
     for n in range(2, bits):
         ffn_send, ffn_keep = halves(ffn_grads, chunk, ffn_order[n:], ffn_order[n])
         ffn_other = swap(ffn_send, "dp", 1 << ffn_order[n])
         ffn_grads = ffn_keep.astype(f32) + ffn_other.astype(f32)
-    mix_other = after(mix_other, far, branch_far, ffn_other).astype(f32)
+    mix_other = after(mix_other, far, branch_far, ffn_send).astype(f32)
     mix_grads = mix_keep.astype(f32) + mix_other[: mix_keep.shape[0]]
     sums = sums + (mix_other[-16:-8] + mix_other[-8:])
     for n in range(1, bits - 1):
@@ -734,15 +738,15 @@
     ffn_other = after(ffn_other, mix_send)
     up_grad, down_grad = ffn_finish(ffn_keep, ffn_other)
     grad_hat = hat_own + after(landed_far, mix_send).astype(f32)
-    mix_other = after(mix_other, up_grad, grad_hat)
-    triple_grad, out_grad_t, sums = mix_finish(mix_keep, mix_other, one + two, W)
-    result = hidden_in.astype(f32) + branch_own + branch_across.astype(f32) + out_bias
     own, inv_std = normalize(hidden_in.astype(f32))
     first_mean = jnp.mean(grad_hat, axis=-1, keepdims=True)
     second_mean = jnp.mean(grad_hat * own, axis=-1, keepdims=True)
     grad_hidden = out_grad.astype(f32) + inv_std * (grad_hat - first_mean - own * second_mean)
+    mix_other = after(mix_other, up_grad, grad_hidden)
+    triple_grad, out_grad_t, sums = mix_finish(mix_keep, mix_other, one + two, W)
+    result = hidden_in.astype(f32) + branch_own + after(branch_across, sums).astype(f32) + out_bias
     norm_sums = sums + swap(sums, "tensor", 1)
-    norm_sums = norm_sums + swap(after(norm_sums, branch_across), "tensor", 2)
+    norm_sums = norm_sums + swap(norm_sums, "tensor", 2)
     head_sums = sums[2, : 2 * W].reshape(heads, 2, HD)[:, 1].reshape(W)
     pair_grad = jnp.stack([sums[2, 2 * W : 3 * W], head_sums])
     return (
@@ -752,12 +756,12 @@
         norm_sums[1],
         norm_sums[3],
         norm_sums[4],
-        triple_grad,
+        jnp.transpose(triple_grad, (1, 0, 2)),
         pair_grad,
         out_grad_t,
         up_grad,
         sums[5],
-        down_grad,
+        down_grad.T,
         norm_sums[6],
     )
 

time: 258 us -> 249 us (0.965); the launches traced: 258 us -> 245 us
  local copies, waits for them, and re-layouts: 30.7 us -> 20.9 us
  starting transfers between devices: 41.2 us -> 33.4 us
  Pallas kernels: 105 us -> 100 us
  other arithmetic: 14.6 us -> 19.3 us
  waiting for transfers between devices: 65.1 us -> 69.1 us
    ppermute x27, starting transfers between devices: 35.7 us -> 26.9 us  [swap(): return lax.ppermute(value, axis, [(i, i ^ mask) for i in range(count)])]
    pallas_call x2, Pallas kernels: 32.5 us -> 28 us  [attention(): pl.pallas_call(functools.partial(attn_kernel, T=T, blk=blk, heads=heads,...]
    ppermute x3, waiting for transfers between devices: 6.85 us -> 10.6 us  [shift(): return lax.ppermute(value, axis, route)]
    concatenate x0 -> x7, other arithmetic: none -> 3.58 us  [gather_dp(): jnp.concatenate([jnp.where(high, two, one), jnp.where(high, one, two)], a...]
    another operation x4 -> x0, local copies, waits for them, and re-layouts: 3.5 us -> none  [gather_dp(): jnp.stack([jnp.where(high, two, one), jnp.where(high, one, two)], axis=1)]
    add x3 -> x4, other arithmetic: 0.67 us -> 3.55 us  [the longest x1 2.81 us: shards(): hidden_in.astype(f32) + branch_own + after(branch_across, sums).astype(f32)]
  transfers between devices with their start and end apart: 30 -> 30, of which waited for: 14 -> 17; matrix products, arithmetic and copies ran while one was open for 13% -> 11% of each run, Pallas kernels for 41% -> 41%
where the time goes in v3:
time: 249 us; the launch traced here: 245 us
  Pallas kernels  100 us (40%)
  waiting for transfers between devices  69.1 us (28%)
  starting transfers between devices  33.4 us (13%)
  local copies, waits for them, and re-layouts  20.9 us (8%)
  other arithmetic  19.3 us (8%)
    ppermute x27, waiting for transfers between devices, swap(): return lax.ppermute(value, axis, [(i, i ^ mask) for i in range(count)])  58.5 us
    pallas_call x1, Pallas kernels, ffn(): pl.pallas_call(functools.partial(ffn_kernel, pieces=len(gs), blk=blk, chu...  30.3 us
    pallas_call x2, Pallas kernels, attention(): pl.pallas_call(functools.partial(attn_kernel, T=T, blk=blk, heads=heads,...  28 us
    ppermute x27, starting transfers between devices, swap(): return lax.ppermute(value, axis, [(i, i ^ mask) for i in range(count)])  26.9 us
    pallas_call x2, Pallas kernels, post(): pl.pallas_call(functools.partial(post_kernel, chunk=chunk), grid_spec=plt...  18.4 us
    unnamed x67, local copies, waits for them, and re-layouts  11 us
    pallas_call x1, Pallas kernels, pre(): pl.pallas_call(functools.partial(pre_kernel, pieces=len(hids), blk=blk),...  10.7 us
    ppermute x3, waiting for transfers between devices, shift(): return lax.ppermute(value, axis, route)  10.6 us
  transfers between devices with their start and end apart: 30, of which 17 were waited for; matrix products, arithmetic and copies ran while one was open for 11% of the time, Pallas kernels for 41%

profile of v3, /device:TPU:0, one launch (start us, length us, event | category | flops | bytes accessed | tf_op | source)
XLA Modules:
  0.0 244.6 jit_solution(6087256606579619427)
XLA Ops:
  0.7 3.0 %collective-permute-start.1 = (bf16[512,768]{1,0:T(8,128)(2,1)}, bf16[512,768]{1,0:T(8,128)(2,1)S(1)}, u32[]{:S(2)}, u32[]{:S(2)}) collective-permute-start(bf16[512,768]{1,0:T(8,128)(2,1)} %refs_0_.3), channel_id=1, source_target_pairs={{0,2},{1,3},{2,0},{3,1},{4,6},{5,7},{6,4},{7,5},{8,10},{9,11},{10,... | collective-permute-start | bytes 2359304 | tf_op jit(solution)/shard_map/ppermute | solution.py:42
  3.7 2.6 %collective-permute-start.3 = (bf16[96,768]{1,0:T(8,128)(2,1)}, bf16[96,768]{1,0:T(8,128)(2,1)S(1)}, u32[]{:S(2)}, u32[]{:S(2)}) collective-permute-start(bf16[96,768]{1,0:T(8,128)(2,1)} %param.23), channel_id=1, source_target_pairs={{0,16},{4,20},{8,24},{12,28},{16,0},{20,4},{24,8},{28,12},{1,17},{... | collective-permute-start | bytes 442376 | tf_op jit(solution)/shard_map/ppermute | solution.py:42
  16.0 4.1 %collective-permute-start.10 = (bf16[192,768]{1,0:T(8,128)(2,1)S(1)}, bf16[192,768]{1,0:T(8,128)(2,1)S(1)}, u32[]{:S(2)}, u32[]{:S(2)}) collective-permute-start(bf16[192,768]{1,0:T(8,128)(2,1)S(1)} %get-tuple-element.161), channel_id=1, source_target_pairs={{0,8},{4,12},{8,0},{12,4},{16,24},{20,28},{24,16},{28,20},{1,9},{5... | collective-permute-start | bytes 884744 | tf_op jit(solution)/shard_map/ppermute | solution.py:42
  20.1 2.9 %collective-permute-done.4 = bf16[96,640]{1,0:T(8,128)(2,1)S(1)} collective-permute-done((bf16[96,640]{1,0:T(8,128)(2,1)S(1)}, bf16[96,640]{1,0:T(8,128)(2,1)S(1)}, u32[]{:S(2)}, u32[]{:S(2)}) %collective-permute-start.4) | collective-permute-done | bytes 122912 | tf_op jit(solution)/shard_map/ppermute | solution.py:42
  23.1 5.8 %collective-permute-done.10 = bf16[192,768]{1,0:T(8,128)(2,1)S(1)} collective-permute-done((bf16[192,768]{1,0:T(8,128)(2,1)S(1)}, bf16[192,768]{1,0:T(8,128)(2,1)S(1)}, u32[]{:S(2)}, u32[]{:S(2)}) %collective-permute-start.10) | collective-permute-done | bytes 294944 | tf_op jit(solution)/shard_map/ppermute | solution.py:42
  29.0 1.6 collective-permute-start.11
  30.6 3.0 %collective-permute-done.5 = bf16[192,640]{1,0:T(8,128)(2,1)S(1)} collective-permute-done((bf16[192,640]{1,0:T(8,128)(2,1)S(1)}, bf16[192,640]{1,0:T(8,128)(2,1)S(1)}, u32[]{:S(2)}, u32[]{:S(2)}) %collective-permute-start.5) | collective-permute-done | bytes 245792 | tf_op jit(solution)/shard_map/ppermute | solution.py:42
  33.9 1.6 collective-permute-start.6
  36.0 8.0 %collective-permute-done.7 = bf16[96,896]{1,0:T(8,128)(2,1)S(1)} collective-permute-done((bf16[96,896]{1,0:T(8,128)(2,1)S(1)}, bf16[96,896]{1,0:T(8,128)(2,1)S(1)}, u32[]{:S(2)}, u32[]{:S(2)}) %collective-permute-start.7) | collective-permute-done | bytes 172064 | tf_op jit(solution)/shard_map/ppermute | solution.py:42
  46.6 7.6 %collective-permute-done.8 = bf16[192,896]{1,0:T(8,128)(2,1)S(1)} collective-permute-done((bf16[192,896]{1,0:T(8,128)(2,1)S(1)}, bf16[192,896]{1,0:T(8,128)(2,1)S(1)}, u32[]{:S(2)}, u32[]{:S(2)}) %collective-permute-start.8) | collective-permute-done | bytes 344096 | tf_op jit(solution)/shard_map/ppermute | solution.py:42
  59.6 10.7 %pre.1 = (bf16[2048,768]{1,0:T(8,128)(2,1)}, bf16[3,2048,128]{2,1,0:T(8,128)(2,1)}, bf16[3,2048,128]{2,1,0:T(8,128)(2,1)}) custom-call(bf16[512,768]{1,0:T(8,128)(2,1)} %refs_0_.3, bf16[512,768]{1,0:T(8,128)(2,1)} %copy-done.14, bf16[512,768]{1,0:T(8,128)(2,1)} %copy-done.13, bf16[512,768]{1,0:T(8,128)(2,1)} %copy-done.15, ...), custom_call_target="tpu_custom_call" | custom-call | flops 575000000 | bytes 1000 | tf_op jit(solution)/shard_map/pre/pallas_call | solution.py:199
  73.1 3.7 %collective-permute-start.13 = (bf16[3,2048,128]{2,1,0:T(8,128)(2,1)S(1)}, bf16[3,2048,128]{2,1,0:T(8,128)(2,1)S(1)}, u32[]{:S(2)}, u32[]{:S(2)}) collective-permute-start(bf16[3,2048,128]{2,1,0:T(8,128)(2,1)S(1)} %copy-done), channel_id=1, source_target_pairs={{0,4},{4,8},{8,12},{12,16},{16,20},{20,24},{24,28},{1,5},{5,9},{9,... | collective-permute-start | bytes 4718600 | tf_op jit(solution)/shard_map/ppermute | solution.py:48
  77.4 2.1 collective-permute-done.14.refs_5_
  80.6 30.3 %ffn.1 = (bf16[2048,768]{1,0:T(8,128)(2,1)}, bf16[2048,768]{1,0:T(8,128)(2,1)}, bf16[2048,768]{1,0:T(8,128)(2,1)}, bf16[2048,768]{1,0:T(8,128)(2,1)}, bf16[3,204...) custom-call(bf16[512,768]{1,0:T(8,128)(2,1)} %refs_0_.3, ...), custom_call_target="tpu_custom_call" | custom-call | flops 575000000 | bytes 1000 | tf_op jit(solution)/shard_map/ffn/pallas_call | solution.py:289
  110.9 2.2 collective-permute-start.17
  114.6 9.5 %attn.2 = (bf16[192,1024]{1,0:T(8,128)(2,1)S(1)}, bf16[192,1024]{1,0:T(8,128)(2,1)S(1)}, bf16[3,1024,128]{2,1,0:T(8,128)(2,1)S(1)}, f32[3,2048,128]{2,1,0:T(8,128)S(1)}) custom-call(s32[2]{0:T(128)S(1)} %pad_add_fusion.refs_0_.place_ref, s32[8]{0:T(128)S(1)} %and_select_fusion.refs_1_, s32[1,2048]{1,0:T(1,128)S(1)} %add_subtract_fusion.refs_2_, ...), custom_call_target="tpu_custom_call" | custom-call | flops 115000000 | bytes 1000 | tf_op jit(solution)/shard_map/attn/pallas_call | solution.py:444
  124.1 1.7 copy-done.3
  127.3 18.5 %attn.3 = (bf16[192,2048]{1,0:T(8,128)(2,1)S(1)}, bf16[192,2048]{1,0:T(8,128)(2,1)S(1)}, bf16[3,1024,128]{2,1,0:T(8,128)(2,1)S(1)}, f32[3,1024,128]{2,1,0:T(8,128)S(1)}, f32[3,1024,128]{2,1,0:T(8,128)S(1)}) custom-call(s32[2]{0:T(128)S(1)} %pad_add_fusion.refs_0_.place_ref, s32[8]{0:T(128)S(1)} %and_select_fusion.refs_1_, ...), custom_call_target="tpu_custom_call" | custom-call | flops 115000000 | bytes 1000 | tf_op jit(solution)/shard_map/attn/pallas_call | solution.py:444
  145.8 10.6 %collective-permute-done.16.ahead_ref = bf16[3,1024,128]{2,1,0:T(8,128)(2,1)S(1)} collective-permute-done((bf16[3,1024,128]{2,1,0:T(8,128)(2,1)S(1)}, bf16[3,1024,128]{2,1,0:T(8,128)(2,1)S(1)}, u32[]{:S(2)}, u32[]{:S(2)}) %collective-permute-start.16) | collective-permute-done | bytes 786464 | tf_op jit(solution)/shard_map/ppermute | solution.py:48
  158.1 9.0 %post.2 = (bf16[1024,768]{1,0:T(8,128)(2,1)}, bf16[1024,768]{1,0:T(8,128)(2,1)}, f32[768,384]{1,0:T(8,128)}, f32[8,768]{1,0:T(8,128)}) custom-call(s32[2]{0:T(128)} %copy-done.9, f32[3,1024,128]{2,1,0:T(8,128)} %copy-done.7, bf16[3,1024,128]{2,1,0:T(8,128)(2,1)} %copy-done.19, bf16[192,2048]{1,0:T(8,128)(2,1)} %copy-done.4, ...), custom_call_target="tpu_custom_call" | custom-call | flops 115000000 | bytes 1000 | tf_op jit(solution)/shard_map/post/pallas_call | solution.py:584
  167.2 3.9 %collective-permute-start.20 = (bf16[192,1536]{1,0:T(8,128)(2,1)S(1)}, bf16[192,1536]{1,0:T(8,128)(2,1)S(1)}, u32[]{:S(2)}, u32[]{:S(2)}) collective-permute-start(bf16[192,1536]{1,0:T(8,128)(2,1)S(1)} %bitcast.112), channel_id=1, source_target_pairs={{0,8},{4,12},{8,0},{12,4},{16,24},{20,28},{24,16},{28,20},{1,9},{5... | collective-permute-start | bytes 1769480 | tf_op jit(solution)/shard_map/ppermute | solution.py:42
  171.1 9.2 %mid.1 = (bf16[1024,768]{1,0:T(8,128)(2,1)}, bf16[1024,768]{1,0:T(8,128)(2,1)}, bf16[768,384]{1,0:T(8,128)(2,1)}) custom-call(bf16[192,2048]{1,0:T(8,128)(2,1)} %copy-done.8, bf16[192,2048]{1,0:T(8,128)(2,1)} %copy-done.4, bf16[2048,768]{1,0:T(8,128)(2,1)} %get-tuple-element.93.mixer_ref, bf16[2048,768]{1,0:T(8,128)(2,1)} %get-tuple-element.98.g_ref, ...), custom_call_target="tpu_custom_call" | custom-call | flops 115000000 | bytes 1000 | tf_op jit(solution)/shard_map/mid/pallas_call | solution.py:492
  181.3 9.4 %post.3 = (bf16[1024,768]{1,0:T(8,128)(2,1)}, bf16[1024,768]{1,0:T(8,128)(2,1)}, bf16[400,768]{1,0:T(8,128)(2,1)}, bf16[384,768]{1,0:T(8,128)(2,1)}, f32[8,768]{1,0:T(8,128)}) custom-call(s32[2]{0:T(128)} %copy-done.9, f32[3,1024,128]{2,1,0:T(8,128)} %copy-done.10, bf16[3,1024,128]{2,1,0:T(8,128)(2,1)} %copy-done.30, ...), custom_call_target="tpu_custom_call", output_to_operand_aliasing={{0}: (11, {}), {1}: (12, {})} | custom-call | flops 9200000000 | bytes 1000 | tf_op jit(solution)/shard_map/post/pallas_call | solution.py:584
  198.1 10.6 %collective-permute-done.24 = bf16[400,768]{1,0:T(8,128)(2,1)S(1)} collective-permute-done((bf16[400,768]{1,0:T(8,128)(2,1)S(1)}, bf16[400,768]{1,0:T(8,128)(2,1)S(1)}, u32[]{:S(2)}, u32[]{:S(2)}) %collective-permute-start.24) | collective-permute-done | bytes 614432 | tf_op jit(solution)/shard_map/ppermute | solution.py:42
  210.8 9.3 %collective-permute-done.25 = bf16[208,768]{1,0:T(8,128)(2,1)S(1)} collective-permute-done((bf16[208,768]{1,0:T(8,128)(2,1)S(1)}, bf16[208,768]{1,0:T(8,128)(2,1)S(1)}, u32[]{:S(2)}, u32[]{:S(2)}) %collective-permute-start.25) | collective-permute-done | bytes 319520 | tf_op jit(solution)/shard_map/ppermute | solution.py:42
  221.1 1.5 collective-permute-start.23
  223.2 2.9 %fusion.7 = f32[512,768]{1,0:T(8,128)} fusion(bf16[512,768]{1,0:T(8,128)(2,1)S(1)} %copy-done.11, bf16[512,768]{1,0:T(8,128)(2,1)} %refs_4_, f32[512]{0:T(512)S(1)} %get-tuple-element.181, f32[512]{0:T(512)S(1)} %get-tuple-element.182, f32[512]{0:T(512)S(1)} %add_rsqrt_fusion, f32[512]{0:T(512)S(1)} %broadcast_multiply_fusion.2, ...), kind=kLoop, calls=%fused_computation.13 | loop fusion | flops 4325376 | bytes 5513216 | tf_op jit(solution)/shard_map/add | solution.py:744
  226.2 2.0 ffn_finish.1
  228.9 2.1 collective-permute-done.26.other_ref
  231.0 1.9 mix_finish.1
  238.7 2.4 collective-permute-done.29
  241.8 2.8 %fusion.10 = f32[512,768]{1,0:T(8,128)} fusion(bf16[512,768]{1,0:T(8,128)(2,1)S(1)} %copy-done.11, f32[1024,768]{1,0:T(8,128)} %copy-done.12, bf16[512,768]{1,0:T(8,128)(2,1)S(1)} %collective-permute-done.23, f32[768]{0:T(1024)S(1)} %copy-done.29), kind=kLoop, calls=%fused_computation.16 | loop fusion | flops 1966080 | bytes 4721664 | tf_op jit(solution)/shard_map/add | solution.py:747
  (192 shorter events, 46.7 us)
Async XLA Ops:
  0.7 34.8 %collective-permute-start.1 = (bf16[512,768]{1,0:T(8,128)(2,1)}, bf16[512,768]{1,0:T(8,128)(2,1)S(1)}, u32[]{:S(2)}, u32[]{:S(2)}) collective-permute-start(bf16[512,768]{1,0:T(8,128)(2,1)} %refs_0_.3), channel_id=1, source_target_pairs={{0,2},{1,3},{2,0},{3,1},{4,6},{5,7},{6,4},{7,5},{8,10},{9,11},{10,... | collective-permute-start | bytes 2359304 | tf_op jit(solution)/shard_map/ppermute | solution.py:42
  3.7 54.7 %collective-permute-start = (bf16[512,768]{1,0:T(8,128)(2,1)}, bf16[512,768]{1,0:T(8,128)(2,1)S(1)}, u32[]{:S(2)}, u32[]{:S(2)}) collective-permute-start(bf16[512,768]{1,0:T(8,128)(2,1)} %refs_0_.3), channel_id=1, source_target_pairs={{0,1},{1,0},{2,3},{3,2},{4,5},{5,4},{6,7},{7,6},{8,9},{9,8},{10,11... | collective-permute-start | bytes 2359304 | tf_op jit(solution)/shard_map/ppermute | solution.py:42
  3.7 10.5 %collective-permute-start.3 = (bf16[96,768]{1,0:T(8,128)(2,1)}, bf16[96,768]{1,0:T(8,128)(2,1)S(1)}, u32[]{:S(2)}, u32[]{:S(2)}) collective-permute-start(bf16[96,768]{1,0:T(8,128)(2,1)} %param.23), channel_id=1, source_target_pairs={{0,16},{4,20},{8,24},{12,28},{16,0},{20,4},{24,8},{28,12},{1,17},{... | collective-permute-start | bytes 442376 | tf_op jit(solution)/shard_map/ppermute | solution.py:42
  14.3 8.7 %collective-permute-start.4 = (bf16[96,640]{1,0:T(8,128)(2,1)S(1)}, bf16[96,640]{1,0:T(8,128)(2,1)S(1)}, u32[]{:S(2)}, u32[]{:S(2)}) collective-permute-start(bf16[96,640]{1,0:T(8,128)(2,1)S(1)} %pad_maximum_fusion.12), channel_id=1, source_target_pairs={{0,16},{4,20},{8,24},{12,28},{16,0},{20,4},{24,8},{28,12},{1,17},{... | collective-permute-start | bytes 368648 | tf_op jit(solution)/shard_map/ppermute | solution.py:42
  15.9 40.7 %copy-start.24 = (f32[1,768]{1,0:T(1,128)}, f32[1,768]{1,0:T(1,128)S(1)}, u32[]{:S(2)}) copy-start(f32[1,768]{1,0:T(1,128)S(1)} %stack.32.gain_ref) | copy-start | bytes 9220
  16.0 13.0 %collective-permute-start.10 = (bf16[192,768]{1,0:T(8,128)(2,1)S(1)}, bf16[192,768]{1,0:T(8,128)(2,1)S(1)}, u32[]{:S(2)}, u32[]{:S(2)}) collective-permute-start(bf16[192,768]{1,0:T(8,128)(2,1)S(1)} %get-tuple-element.161), channel_id=1, source_target_pairs={{0,8},{4,12},{8,0},{12,4},{16,24},{20,28},{24,16},{28,20},{1,9},{5... | collective-permute-start | bytes 884744 | tf_op jit(solution)/shard_map/ppermute | solution.py:42
  23.0 10.6 %collective-permute-start.5 = (bf16[192,640]{1,0:T(8,128)(2,1)S(1)}, bf16[192,640]{1,0:T(8,128)(2,1)S(1)}, u32[]{:S(2)}, u32[]{:S(2)}) collective-permute-start(bf16[192,640]{1,0:T(8,128)(2,1)S(1)} %get-tuple-element.164), channel_id=1, source_target_pairs={{0,8},{4,12},{8,0},{12,4},{16,24},{20,28},{24,16},{28,20},{1,9},{5... | collective-permute-start | bytes 737288 | tf_op jit(solution)/shard_map/ppermute | solution.py:42
  29.0 16.3 %collective-permute-start.11 = (bf16[384,768]{1,0:T(8,128)(2,1)S(1)}, bf16[384,768]{1,0:T(8,128)(2,1)S(1)}, u32[]{:S(2)}, u32[]{:S(2)}) collective-permute-start(bf16[384,768]{1,0:T(8,128)(2,1)S(1)} %bitcast.102), channel_id=1, source_target_pairs={{0,4},{4,0},{8,12},{12,8},{16,20},{20,16},{24,28},{28,24},{1,5},{5... | collective-permute-start | bytes 1769480 | tf_op jit(solution)/shard_map/ppermute | solution.py:42
  33.7 10.3 %collective-permute-start.7 = (bf16[96,896]{1,0:T(8,128)(2,1)S(1)}, bf16[96,896]{1,0:T(8,128)(2,1)S(1)}, u32[]{:S(2)}, u32[]{:S(2)}) collective-permute-start(bf16[96,896]{1,0:T(8,128)(2,1)S(1)} %pad_maximum_fusion.10), channel_id=1, source_target_pairs={{0,16},{4,20},{8,24},{12,28},{16,0},{20,4},{24,8},{28,12},{1,17},{... | collective-permute-start | bytes 516104 | tf_op jit(solution)/shard_map/ppermute | solution.py:42
  33.9 23.3 %collective-permute-start.6 = (bf16[384,640]{1,0:T(8,128)(2,1)S(1)}, bf16[384,640]{1,0:T(8,128)(2,1)S(1)}, u32[]{:S(2)}, u32[]{:S(2)}) collective-permute-start(bf16[384,640]{1,0:T(8,128)(2,1)S(1)} %bitcast.104), channel_id=1, source_target_pairs={{0,4},{4,0},{8,12},{12,8},{16,20},{20,16},{24,28},{28,24},{1,5},{5... | collective-permute-start | bytes 1474568 | tf_op jit(solution)/shard_map/ppermute | solution.py:42
  35.5 19.2 %collective-permute-start.9 = (bf16[512,768]{1,0:T(8,128)(2,1)}, bf16[512,768]{1,0:T(8,128)(2,1)}, u32[]{:S(2)}, u32[]{:S(2)}) collective-permute-start(bf16[512,768]{1,0:T(8,128)(2,1)} %refs_4_), channel_id=1, source_target_pairs={{0,2},{1,3},{2,0},{3,1},{4,6},{5,7},{6,4},{7,5},{8,10},{9,11},{10,... | collective-permute-start | bytes 2359304 | tf_op jit(solution)/shard_map/ppermute | solution.py:42
  44.2 10.0 %collective-permute-start.8 = (bf16[192,896]{1,0:T(8,128)(2,1)S(1)}, bf16[192,896]{1,0:T(8,128)(2,1)S(1)}, u32[]{:S(2)}, u32[]{:S(2)}) collective-permute-start(bf16[192,896]{1,0:T(8,128)(2,1)S(1)} %get-tuple-element.156), channel_id=1, source_target_pairs={{0,8},{4,12},{8,0},{12,4},{16,24},{20,28},{24,16},{28,20},{1,9},{5... | collective-permute-start | bytes 1032200 | tf_op jit(solution)/shard_map/ppermute | solution.py:42
  45.4 13.0 %collective-permute-start.2 = (bf16[512,768]{1,0:T(8,128)(2,1)S(1)}, bf16[512,768]{1,0:T(8,128)(2,1)S(1)}, u32[]{:S(2)}, u32[]{:S(2)}) collective-permute-start(bf16[512,768]{1,0:T(8,128)(2,1)S(1)} %collective-permute-done.1.refs_2_), channel_id=1, source_target_pairs={{0,1},{1,0},{2,3},{3,2},{4,5},{5,4},{6,7},{7,6},{8,9},{9,8},{10,11... | collective-permute-start | bytes 2359304 | tf_op jit(solution)/shard_map/ppermute | solution.py:42
  54.9 16.2 %collective-permute-start.12 = (bf16[384,896]{1,0:T(8,128)(2,1)S(1)}, bf16[384,896]{1,0:T(8,128)(2,1)S(1)}, u32[]{:S(2)}, u32[]{:S(2)}) collective-permute-start(bf16[384,896]{1,0:T(8,128)(2,1)S(1)} %bitcast.100), channel_id=1, source_target_pairs={{0,4},{4,0},{8,12},{12,8},{16,20},{20,16},{24,28},{28,24},{1,5},{5... | collective-permute-start | bytes 2064392 | tf_op jit(solution)/shard_map/ppermute | solution.py:42
  73.1 37.8 %collective-permute-start.13 = (bf16[3,2048,128]{2,1,0:T(8,128)(2,1)S(1)}, bf16[3,2048,128]{2,1,0:T(8,128)(2,1)S(1)}, u32[]{:S(2)}, u32[]{:S(2)}) collective-permute-start(bf16[3,2048,128]{2,1,0:T(8,128)(2,1)S(1)} %copy-done), channel_id=1, source_target_pairs={{0,4},{4,8},{8,12},{12,16},{16,20},{20,24},{24,28},{1,5},{5,9},{9,... | collective-permute-start | bytes 4718600 | tf_op jit(solution)/shard_map/ppermute | solution.py:48
  76.8 2.7 %collective-permute-start.14 = (bf16[512,768]{1,0:T(8,128)(2,1)}, bf16[512,768]{1,0:T(8,128)(2,1)}, u32[]{:S(2)}, u32[]{:S(2)}) collective-permute-start(bf16[512,768]{1,0:T(8,128)(2,1)} %refs_4_), channel_id=1, source_target_pairs={{0,1},{1,0},{2,3},{3,2},{4,5},{5,4},{6,7},{7,6},{8,9},{9,8},{10,11... | collective-permute-start | bytes 2359304 | tf_op jit(solution)/shard_map/ppermute | solution.py:42
  76.9 3.7 %collective-permute-start.15 = (bf16[512,768]{1,0:T(8,128)(2,1)}, bf16[512,768]{1,0:T(8,128)(2,1)}, u32[]{:S(2)}, u32[]{:S(2)}) collective-permute-start(bf16[512,768]{1,0:T(8,128)(2,1)} %collective-permute-done.9.refs_6_), channel_id=1, source_target_pairs={{0,1},{1,0},{2,3},{3,2},{4,5},{5,4},{6,7},{7,6},{8,9},{9,8},{10,11... | collective-permute-start | bytes 2359304 | tf_op jit(solution)/shard_map/ppermute | solution.py:42
  80.6 32.5 %copy-start.6 = (f32[8,2048]{1,0:T(8,128)S(1)}, f32[8,2048]{1,0:T(8,128)}, u32[]{:S(2)}) copy-start(f32[8,2048]{1,0:T(8,128)} %get-tuple-element.174.refs_7_.cos_ref) | copy-start | bytes 196612
  110.9 45.5 %collective-permute-start.17 = (bf16[384,1536]{1,0:T(8,128)(2,1)}, bf16[384,1536]{1,0:T(8,128)(2,1)S(1)}, u32[]{:S(2)}, u32[]{:S(2)}) collective-permute-start(bf16[384,1536]{1,0:T(8,128)(2,1)} %get-tuple-element.89), channel_id=1, source_target_pairs={{0,4},{4,0},{8,12},{12,8},{16,20},{20,16},{24,28},{28,24},{1,5},{5... | collective-permute-start | bytes 3538952 | tf_op jit(solution)/shard_map/ppermute | solution.py:42
  125.7 30.7 %collective-permute-start.16 = (bf16[3,1024,128]{2,1,0:T(8,128)(2,1)S(1)}, bf16[3,1024,128]{2,1,0:T(8,128)(2,1)S(1)}, u32[]{:S(2)}, u32[]{:S(2)}) collective-permute-start(bf16[3,1024,128]{2,1,0:T(8,128)(2,1)S(1)} %get-tuple-element.86), channel_id=1, source_target_pairs={{4,0},{8,4},{12,8},{16,12},{20,16},{24,20},{28,24},{5,1},{9,5},{13... | collective-permute-start | bytes 2359304 | tf_op jit(solution)/shard_map/ppermute | solution.py:48
  156.4 24.0 %collective-permute-start.19 = (bf16[3,1024,128]{2,1,0:T(8,128)(2,1)S(1)}, bf16[3,1024,128]{2,1,0:T(8,128)(2,1)S(1)}, u32[]{:S(2)}, u32[]{:S(2)}) collective-permute-start(bf16[3,1024,128]{2,1,0:T(8,128)(2,1)S(1)} %get-tuple-element.104), channel_id=1, source_target_pairs={{4,0},{8,4},{12,8},{16,12},{20,16},{24,20},{28,24},{5,1},{9,5},{13... | collective-permute-start | bytes 2359304 | tf_op jit(solution)/shard_map/ppermute | solution.py:48
  167.2 23.7 %collective-permute-start.20 = (bf16[192,1536]{1,0:T(8,128)(2,1)S(1)}, bf16[192,1536]{1,0:T(8,128)(2,1)S(1)}, u32[]{:S(2)}, u32[]{:S(2)}) collective-permute-start(bf16[192,1536]{1,0:T(8,128)(2,1)S(1)} %bitcast.112), channel_id=1, source_target_pairs={{0,8},{4,12},{8,0},{12,4},{16,24},{20,28},{24,16},{28,20},{1,9},{5... | collective-permute-start | bytes 1769480 | tf_op jit(solution)/shard_map/ppermute | solution.py:42
  180.3 13.1 %collective-permute-start.18 = (bf16[1024,768]{1,0:T(8,128)(2,1)}, bf16[1024,768]{1,0:T(8,128)(2,1)S(1)}, u32[]{:S(2)}, u32[]{:S(2)}) collective-permute-start(bf16[1024,768]{1,0:T(8,128)(2,1)} %get-tuple-element.101), channel_id=1, source_target_pairs={{0,1},{1,0},{2,3},{3,2},{4,5},{5,4},{6,7},{7,6},{8,9},{9,8},{10,11... | collective-permute-start | bytes 4718600 | tf_op jit(solution)/shard_map/ppermute | solution.py:42
  190.9 4.6 %collective-permute-start.21 = (bf16[1024,768]{1,0:T(8,128)(2,1)}, bf16[1024,768]{1,0:T(8,128)(2,1)S(1)}, u32[]{:S(2)}, u32[]{:S(2)}) collective-permute-start(bf16[1024,768]{1,0:T(8,128)(2,1)} %get-tuple-element.115), channel_id=1, source_target_pairs={{0,1},{1,0},{2,3},{3,2},{4,5},{5,4},{6,7},{7,6},{8,9},{9,8},{10,11... | collective-permute-start | bytes 4718600 | tf_op jit(solution)/shard_map/ppermute | solution.py:42
  192.9 15.9 %collective-permute-start.24 = (bf16[400,768]{1,0:T(8,128)(2,1)S(1)}, bf16[400,768]{1,0:T(8,128)(2,1)S(1)}, u32[]{:S(2)}, u32[]{:S(2)}) collective-permute-start(bf16[400,768]{1,0:T(8,128)(2,1)S(1)} %copy-done.31), channel_id=1, source_target_pairs={{0,4},{4,0},{8,12},{12,8},{16,20},{20,16},{24,28},{28,24},{1,5},{5... | collective-permute-start | bytes 1843208 | tf_op jit(solution)/shard_map/ppermute | solution.py:42
  196.8 23.3 %collective-permute-start.22 = (bf16[512,768]{1,0:T(8,128)(2,1)S(1)}, bf16[512,768]{1,0:T(8,128)(2,1)S(1)}, u32[]{:S(2)}, u32[]{:S(2)}) collective-permute-start(bf16[512,768]{1,0:T(8,128)(2,1)S(1)} %slice.238), channel_id=1, source_target_pairs={{0,2},{1,3},{2,0},{3,1},{4,6},{5,7},{6,4},{7,5},{8,10},{9,11},{10,... | collective-permute-start | bytes 2359304 | tf_op jit(solution)/shard_map/ppermute | solution.py:42
  197.7 23.4 %collective-permute-start.27 = (bf16[96,1536]{1,0:T(8,128)(2,1)S(1)}, bf16[96,1536]{1,0:T(8,128)(2,1)S(1)}, u32[]{:S(2)}, u32[]{:S(2)}) collective-permute-start(bf16[96,1536]{1,0:T(8,128)(2,1)S(1)} %fusion.13), channel_id=1, source_target_pairs={{0,16},{4,20},{8,24},{12,28},{16,0},{20,4},{24,8},{28,12},{1,17},{... | collective-permute-start | bytes 884744 | tf_op jit(solution)/shard_map/ppermute | solution.py:42
  209.7 10.5 %collective-permute-start.25 = (bf16[208,768]{1,0:T(8,128)(2,1)S(1)}, bf16[208,768]{1,0:T(8,128)(2,1)S(1)}, u32[]{:S(2)}, u32[]{:S(2)}) collective-permute-start(bf16[208,768]{1,0:T(8,128)(2,1)S(1)} %pad_maximum_fusion.7), channel_id=1, source_target_pairs={{0,8},{4,12},{8,0},{12,4},{16,24},{20,28},{24,16},{28,20},{1,9},{5... | collective-permute-start | bytes 958472 | tf_op jit(solution)/shard_map/ppermute | solution.py:42
  220.9 10.0 %collective-permute-start.26 = (bf16[112,768]{1,0:T(8,128)(2,1)S(1)}, bf16[112,768]{1,0:T(8,128)(2,1)}, u32[]{:S(2)}, u32[]{:S(2)}) collective-permute-start(bf16[112,768]{1,0:T(8,128)(2,1)S(1)} %pad_maximum_fusion.11), channel_id=1, source_target_pairs={{0,16},{4,20},{8,24},{12,28},{16,0},{20,4},{24,8},{28,12},{1,17},{... | collective-permute-start | bytes 516104 | tf_op jit(solution)/shard_map/ppermute | solution.py:42
  221.1 20.7 %collective-permute-start.23 = (bf16[512,768]{1,0:T(8,128)(2,1)S(1)}, bf16[512,768]{1,0:T(8,128)(2,1)S(1)}, u32[]{:S(2)}, u32[]{:S(2)}) collective-permute-start(bf16[512,768]{1,0:T(8,128)(2,1)S(1)} %slice.239), channel_id=1, source_target_pairs={{0,2},{1,3},{2,0},{3,1},{4,6},{5,7},{6,4},{7,5},{8,10},{9,11},{10,... | collective-permute-start | bytes 2359304 | tf_op jit(solution)/shard_map/ppermute | solution.py:42
  232.9 3.0 %collective-permute-start.28 = (f32[8,768]{1,0:T(8,128)}, f32[8,768]{1,0:T(8,128)S(1)}, u32[]{:S(2)}, u32[]{:S(2)}) collective-permute-start(f32[8,768]{1,0:T(8,128)} %get-tuple-element.128), channel_id=1, source_target_pairs={{0,1},{1,0},{2,3},{3,2},{4,5},{5,4},{6,7},{7,6},{8,9},{9,8},{10,11... | collective-permute-start | bytes 73736 | tf_op jit(solution)/shard_map/ppermute | solution.py:42
  236.6 4.5 %collective-permute-start.29 = (f32[8,768]{1,0:T(8,128)S(1)}, f32[8,768]{1,0:T(8,128)S(1)}, u32[]{:S(2)}, u32[]{:S(2)}) collective-permute-start(f32[8,768]{1,0:T(8,128)S(1)} %add.131), channel_id=1, source_target_pairs={{0,2},{1,3},{2,0},{3,1},{4,6},{5,7},{6,4},{7,5},{8,10},{9,11},{10,... | collective-permute-start | bytes 73736 | tf_op jit(solution)/shard_map/ppermute | solution.py:42
  (30 other events, 287.8 us)

commit v4 on v3

--- a/solution.py
+++ b/solution.py
@@ -208,7 +208,7 @@
         ],
         out_specs=[rows_spec(D)] + [heads_spec(heads)] * 2,
         out_shape=[jax.ShapeDtypeStruct((T, D), bf16)] + [jax.ShapeDtypeStruct((heads, T, 128), bf16)] * 2,
-        compiler_params=pltpu.CompilerParams(vmem_limit_bytes=VMEM_LIMIT),
+        compiler_params=pltpu.CompilerParams(vmem_limit_bytes=40 * 2**20),
         cost_estimate=cost(0.5),
         name="pre",
     )(*hids, gains, w, bias, cos, sin)
@@ -455,7 +455,7 @@
             pltpu.VMEM((heads, 2 * TQ, 128), bf16),
         ],
         out_shape=[jax.ShapeDtypeStruct(*out) for out in outs],
-        compiler_params=pltpu.CompilerParams(vmem_limit_bytes=40 * 2**20),
+        compiler_params=pltpu.CompilerParams(vmem_limit_bytes=36 * 2**20),
         cost_estimate=cost(0.1),
         name="attn",
     )(place, first, start, tail, kv, q, do, cos, sin, *early)

time: 249 us -> 245 us (0.984); the launches traced: 245 us -> 244 us
  waiting for transfers between devices: 69.1 us -> 80.3 us
  Pallas kernels: 100 us -> 92.4 us
    ppermute x3, waiting for transfers between devices: 10.6 us -> 17.5 us  [shift(): return lax.ppermute(value, axis, route)]
    pallas_call x2, Pallas kernels: 28 us -> 22.8 us  [attention(): pl.pallas_call(functools.partial(attn_kernel, T=T, blk=blk, heads=heads,...]
    ppermute x27, waiting for transfers between devices: 58.5 us -> 62.8 us  [swap(): return lax.ppermute(value, axis, [(i, i ^ mask) for i in range(count)])]
    pallas_call x1, Pallas kernels: 10.7 us -> 7.67 us  [pre(): pl.pallas_call(functools.partial(pre_kernel, pieces=len(hids), blk=blk),...]
    unnamed x67 -> x75, local copies, waits for them, and re-layouts: 11 us -> 10.3 us
  transfers between devices with their start and end apart: 30 -> 30, of which waited for: 17 -> 17; matrix products, arithmetic and copies ran while one was open for 11% -> 10% of each run, Pallas kernels for 41% -> 38%
where the time goes in v4:
time: 245 us; the launch traced here: 244 us
  Pallas kernels  92.4 us (38%)
  waiting for transfers between devices  80.3 us (33%)
  starting transfers between devices  33.2 us (14%)
  local copies, waits for them, and re-layouts  19.7 us (8%)
  other arithmetic  17 us (7%)
    ppermute x27, waiting for transfers between devices, swap(): return lax.ppermute(value, axis, [(i, i ^ mask) for i in range(count)])  62.8 us
    pallas_call x1, Pallas kernels, ffn(): pl.pallas_call(functools.partial(ffn_kernel, pieces=len(gs), blk=blk, chu...  30.3 us
    ppermute x27, starting transfers between devices, swap(): return lax.ppermute(value, axis, [(i, i ^ mask) for i in range(count)])  26.7 us
    pallas_call x2, Pallas kernels, attention(): pl.pallas_call(functools.partial(attn_kernel, T=T, blk=blk, heads=heads,...  22.8 us
    pallas_call x2, Pallas kernels, post(): pl.pallas_call(functools.partial(post_kernel, chunk=chunk), grid_spec=plt...  18.5 us
    ppermute x3, waiting for transfers between devices, shift(): return lax.ppermute(value, axis, route)  17.5 us
    unnamed x75, local copies, waits for them, and re-layouts  10.3 us
    pallas_call x1, Pallas kernels, mid(): pl.pallas_call(mid_kernel, grid=(T // MR,), in_specs=[cols, cols, rows, r...  9.29 us
  transfers between devices with their start and end apart: 30, of which 17 were waited for; matrix products, arithmetic and copies ran while one was open for 10% of the time, Pallas kernels for 38%

profile of v4, /device:TPU:0, one launch (start us, length us, event | category | flops | bytes accessed | tf_op | source)
XLA Modules:
  0.0 244.0 jit_solution(2213910687550468914)
XLA Ops:
  0.7 3.0 %collective-permute-start.1 = (bf16[512,768]{1,0:T(8,128)(2,1)}, bf16[512,768]{1,0:T(8,128)(2,1)S(1)}, u32[]{:S(2)}, u32[]{:S(2)}) collective-permute-start(bf16[512,768]{1,0:T(8,128)(2,1)} %refs_0_.3), channel_id=1, source_target_pairs={{0,2},{1,3},{2,0},{3,1},{4,6},{5,7},{6,4},{7,5},{8,10},{9,11},{10,... | collective-permute-start | bytes 2359304 | tf_op jit(solution)/shard_map/ppermute | solution.py:42
  3.7 2.6 %collective-permute-start.3 = (bf16[96,768]{1,0:T(8,128)(2,1)}, bf16[96,768]{1,0:T(8,128)(2,1)S(1)}, u32[]{:S(2)}, u32[]{:S(2)}) collective-permute-start(bf16[96,768]{1,0:T(8,128)(2,1)} %param.23), channel_id=1, source_target_pairs={{0,16},{4,20},{8,24},{12,28},{16,0},{20,4},{24,8},{28,12},{1,17},{... | collective-permute-start | bytes 442376 | tf_op jit(solution)/shard_map/ppermute | solution.py:42
  12.7 1.6 collective-permute-done.3
  16.0 4.1 %collective-permute-start.10 = (bf16[192,768]{1,0:T(8,128)(2,1)S(1)}, bf16[192,768]{1,0:T(8,128)(2,1)S(1)}, u32[]{:S(2)}, u32[]{:S(2)}) collective-permute-start(bf16[192,768]{1,0:T(8,128)(2,1)S(1)} %get-tuple-element.161), channel_id=1, source_target_pairs={{0,8},{4,12},{8,0},{12,4},{16,24},{20,28},{24,16},{28,20},{1,9},{5... | collective-permute-start | bytes 884744 | tf_op jit(solution)/shard_map/ppermute | solution.py:42
  20.1 2.9 %collective-permute-done.4 = bf16[96,640]{1,0:T(8,128)(2,1)S(1)} collective-permute-done((bf16[96,640]{1,0:T(8,128)(2,1)S(1)}, bf16[96,640]{1,0:T(8,128)(2,1)S(1)}, u32[]{:S(2)}, u32[]{:S(2)}) %collective-permute-start.4) | collective-permute-done | bytes 122912 | tf_op jit(solution)/shard_map/ppermute | solution.py:42
  23.1 5.8 %collective-permute-done.10 = bf16[192,768]{1,0:T(8,128)(2,1)S(1)} collective-permute-done((bf16[192,768]{1,0:T(8,128)(2,1)S(1)}, bf16[192,768]{1,0:T(8,128)(2,1)S(1)}, u32[]{:S(2)}, u32[]{:S(2)}) %collective-permute-start.10) | collective-permute-done | bytes 294944 | tf_op jit(solution)/shard_map/ppermute | solution.py:42
  29.0 1.6 collective-permute-start.11
  30.6 3.0 %collective-permute-done.5 = bf16[192,640]{1,0:T(8,128)(2,1)S(1)} collective-permute-done((bf16[192,640]{1,0:T(8,128)(2,1)S(1)}, bf16[192,640]{1,0:T(8,128)(2,1)S(1)}, u32[]{:S(2)}, u32[]{:S(2)}) %collective-permute-start.5) | collective-permute-done | bytes 245792 | tf_op jit(solution)/shard_map/ppermute | solution.py:42
  33.9 1.6 collective-permute-start.6
  36.0 8.0 %collective-permute-done.7 = bf16[96,896]{1,0:T(8,128)(2,1)S(1)} collective-permute-done((bf16[96,896]{1,0:T(8,128)(2,1)S(1)}, bf16[96,896]{1,0:T(8,128)(2,1)S(1)}, u32[]{:S(2)}, u32[]{:S(2)}) %collective-permute-start.7) | collective-permute-done | bytes 172064 | tf_op jit(solution)/shard_map/ppermute | solution.py:42
  46.6 7.6 %collective-permute-done.8 = bf16[192,896]{1,0:T(8,128)(2,1)S(1)} collective-permute-done((bf16[192,896]{1,0:T(8,128)(2,1)S(1)}, bf16[192,896]{1,0:T(8,128)(2,1)S(1)}, u32[]{:S(2)}, u32[]{:S(2)}) %collective-permute-start.8) | collective-permute-done | bytes 344096 | tf_op jit(solution)/shard_map/ppermute | solution.py:42
  59.2 7.7 %pre.1 = (bf16[2048,768]{1,0:T(8,128)(2,1)S(1)}, bf16[3,2048,128]{2,1,0:T(8,128)(2,1)S(1)}, bf16[3,2048,128]{2,1,0:T(8,128)(2,1)S(1)}) custom-call(bf16[512,768]{1,0:T(8,128)(2,1)S(1)} %copy-done, bf16[512,768]{1,0:T(8,128)(2,1)S(1)} %copy-done.10, bf16[512,768]{1,0:T(8,128)(2,1)S(1)} %copy-done.8, bf16[512,768]{1,0:T(8,128)(2,1)S(1)} %collective-permute-done.2.refs_3_, ...), custom_call_target="tpu_custom_call" | custom-call | flops 575000000 | bytes 1000 | tf_op jit(solution)/shard_map/pre/pallas_call | solution.py:199
  66.9 4.2 %collective-permute-done.12 = bf16[384,896]{1,0:T(8,128)(2,1)S(1)} collective-permute-done((bf16[384,896]{1,0:T(8,128)(2,1)S(1)}, bf16[384,896]{1,0:T(8,128)(2,1)S(1)}, u32[]{:S(2)}, u32[]{:S(2)}) %collective-permute-start.12) | collective-permute-done | bytes 688160 | tf_op jit(solution)/shard_map/ppermute | solution.py:42
  72.4 3.7 %collective-permute-start.13 = (bf16[3,2048,128]{2,1,0:T(8,128)(2,1)S(1)}, bf16[3,2048,128]{2,1,0:T(8,128)(2,1)S(1)}, u32[]{:S(2)}, u32[]{:S(2)}) collective-permute-start(bf16[3,2048,128]{2,1,0:T(8,128)(2,1)S(1)} %get-tuple-element.78.refs_4_), channel_id=1, source_target_pairs={{0,4},{4,8},{8,12},{12,16},{16,20},{20,24},{24,28},{1,5},{5,9},{9,... | collective-permute-start | bytes 4718600 | tf_op jit(solution)/shard_map/ppermute | solution.py:48
  76.7 2.1 collective-permute-done.14.refs_5_
  79.9 30.3 %ffn.1 = (bf16[2048,768]{1,0:T(8,128)(2,1)}, bf16[2048,768]{1,0:T(8,128)(2,1)}, bf16[2048,768]{1,0:T(8,128)(2,1)}, bf16[2048,768]{1,0:T(8,128)(2,1)}, bf16[3,204...) custom-call(bf16[512,768]{1,0:T(8,128)(2,1)} %refs_0_.3, ...), custom_call_target="tpu_custom_call" | custom-call | flops 575000000 | bytes 1000 | tf_op jit(solution)/shard_map/ffn/pallas_call | solution.py:289
  110.2 2.2 collective-permute-start.17
  113.8 9.5 %attn.2 = (bf16[192,1024]{1,0:T(8,128)(2,1)S(1)}, bf16[192,1024]{1,0:T(8,128)(2,1)S(1)}, bf16[3,1024,128]{2,1,0:T(8,128)(2,1)S(1)}, f32[3,2048,128]{2,1,0:T(8,128)S(1)}) custom-call(s32[2]{0:T(128)S(1)} %pad_add_fusion.refs_0_.place_ref, s32[8]{0:T(128)S(1)} %and_select_fusion.refs_1_, s32[1,2048]{1,0:T(1,128)S(1)} %add_subtract_fusion.refs_2_, ...), custom_call_target="tpu_custom_call" | custom-call | flops 115000000 | bytes 1000 | tf_op jit(solution)/shard_map/attn/pallas_call | solution.py:444
  124.9 13.3 %attn.3 = (bf16[192,2048]{1,0:T(8,128)(2,1)S(1)}, bf16[192,2048]{1,0:T(8,128)(2,1)S(1)}, bf16[3,1024,128]{2,1,0:T(8,128)(2,1)}, f32[3,1024,128]{2,1,0:T(8,128)S(1)}, f32[3,1024,128]{2,1,0:T(8,128)S(1)}) custom-call(s32[2]{0:T(128)S(1)} %pad_add_fusion.refs_0_.place_ref, s32[8]{0:T(128)S(1)} %and_select_fusion.refs_1_, ...), custom_call_target="tpu_custom_call" | custom-call | flops 115000000 | bytes 1000 | tf_op jit(solution)/shard_map/attn/pallas_call | solution.py:444
  138.2 17.5 %collective-permute-done.16.ahead_ref = bf16[3,1024,128]{2,1,0:T(8,128)(2,1)S(1)} collective-permute-done((bf16[3,1024,128]{2,1,0:T(8,128)(2,1)S(1)}, bf16[3,1024,128]{2,1,0:T(8,128)(2,1)S(1)}, u32[]{:S(2)}, u32[]{:S(2)}) %collective-permute-start.16) | collective-permute-done | bytes 786464 | tf_op jit(solution)/shard_map/ppermute | solution.py:48
  157.4 9.1 %post.2 = (bf16[1024,768]{1,0:T(8,128)(2,1)}, bf16[1024,768]{1,0:T(8,128)(2,1)}, f32[768,384]{1,0:T(8,128)}, f32[8,768]{1,0:T(8,128)}) custom-call(s32[2]{0:T(128)} %copy-done.17, f32[3,1024,128]{2,1,0:T(8,128)} %copy-done.15, bf16[3,1024,128]{2,1,0:T(8,128)(2,1)} %copy-done.23, bf16[192,2048]{1,0:T(8,128)(2,1)} %copy-done.12, f32[8,2048]{1,0:T(8,128)} %copy-done.14, ...), custom_call_target="tpu_custom_call" | custom-call | flops 115000000 | bytes 1000 | tf_op jit(solution)/shard_map/post/pallas_call | solution.py:584
  166.6 3.9 %collective-permute-start.20 = (bf16[192,1536]{1,0:T(8,128)(2,1)S(1)}, bf16[192,1536]{1,0:T(8,128)(2,1)S(1)}, u32[]{:S(2)}, u32[]{:S(2)}) collective-permute-start(bf16[192,1536]{1,0:T(8,128)(2,1)S(1)} %bitcast.112), channel_id=1, source_target_pairs={{0,8},{4,12},{8,0},{12,4},{16,24},{20,28},{24,16},{28,20},{1,9},{5... | collective-permute-start | bytes 1769480 | tf_op jit(solution)/shard_map/ppermute | solution.py:42
  170.4 9.3 %mid.1 = (bf16[1024,768]{1,0:T(8,128)(2,1)}, bf16[1024,768]{1,0:T(8,128)(2,1)}, bf16[768,384]{1,0:T(8,128)(2,1)}) custom-call(bf16[192,2048]{1,0:T(8,128)(2,1)} %copy-done.16, bf16[192,2048]{1,0:T(8,128)(2,1)} %copy-done.12, bf16[2048,768]{1,0:T(8,128)(2,1)} %copy-done.3, bf16[2048,768]{1,0:T(8,128)(2,1)} %get-tuple-element.98.g_ref, ...), custom_call_target="tpu_custom_call" | custom-call | flops 115000000 | bytes 1000 | tf_op jit(solution)/shard_map/mid/pallas_call | solution.py:492
  180.7 9.4 %post.3 = (bf16[1024,768]{1,0:T(8,128)(2,1)}, bf16[1024,768]{1,0:T(8,128)(2,1)}, bf16[400,768]{1,0:T(8,128)(2,1)}, bf16[384,768]{1,0:T(8,128)(2,1)}, f32[8,768]{1,0:T(8,128)}) custom-call(s32[2]{0:T(128)} %copy-done.17, f32[3,1024,128]{2,1,0:T(8,128)} %copy-done.18, ...), custom_call_target="tpu_custom_call", output_to_operand_aliasing={{0}: (11, {}), {1}: (12, {})} | custom-call | flops 9200000000 | bytes 1000 | tf_op jit(solution)/shard_map/post/pallas_call | solution.py:584
  197.3 10.9 %collective-permute-done.24 = bf16[400,768]{1,0:T(8,128)(2,1)S(1)} collective-permute-done((bf16[400,768]{1,0:T(8,128)(2,1)S(1)}, bf16[400,768]{1,0:T(8,128)(2,1)S(1)}, u32[]{:S(2)}, u32[]{:S(2)}) %collective-permute-start.24) | collective-permute-done | bytes 614432 | tf_op jit(solution)/shard_map/ppermute | solution.py:42
  210.3 9.3 %collective-permute-done.25 = bf16[208,768]{1,0:T(8,128)(2,1)S(1)} collective-permute-done((bf16[208,768]{1,0:T(8,128)(2,1)S(1)}, bf16[208,768]{1,0:T(8,128)(2,1)S(1)}, u32[]{:S(2)}, u32[]{:S(2)}) %collective-permute-start.25) | collective-permute-done | bytes 319520 | tf_op jit(solution)/shard_map/ppermute | solution.py:42
  222.7 2.9 %fusion.7 = f32[512,768]{1,0:T(8,128)} fusion(bf16[512,768]{1,0:T(8,128)(2,1)S(1)} %copy-done.1, bf16[512,768]{1,0:T(8,128)(2,1)} %refs_4_, f32[512]{0:T(512)S(1)} %get-tuple-element.181, f32[512]{0:T(512)S(1)} %get-tuple-element.182, f32[512]{0:T(512)S(1)} %add_rsqrt_fusion, f32[512]{0:T(512)S(1)} %broadcast_multiply_fusion.2, ...), kind=kLoop, calls=%fused_computation.13 | loop fusion | flops 4325376 | bytes 5513216 | tf_op jit(solution)/shard_map/add | solution.py:744
  225.6 2.0 ffn_finish.1
  228.4 2.1 collective-permute-done.26.other_ref
  230.4 1.9 mix_finish.1
  238.2 2.4 collective-permute-done.29
  241.2 2.8 %fusion.10 = f32[512,768]{1,0:T(8,128)} fusion(bf16[512,768]{1,0:T(8,128)(2,1)S(1)} %copy-done.1, f32[1024,768]{1,0:T(8,128)} %copy-done.19, bf16[512,768]{1,0:T(8,128)(2,1)S(1)} %collective-permute-done.23, f32[768]{0:T(1024)S(1)} %copy-done.33), kind=kLoop, calls=%fused_computation.16 | loop fusion | flops 1966080 | bytes 4721664 | tf_op jit(solution)/shard_map/add | solution.py:747
  (200 shorter events, 44.5 us)
Async XLA Ops:
  0.7 34.8 %collective-permute-start.1 = (bf16[512,768]{1,0:T(8,128)(2,1)}, bf16[512,768]{1,0:T(8,128)(2,1)S(1)}, u32[]{:S(2)}, u32[]{:S(2)}) collective-permute-start(bf16[512,768]{1,0:T(8,128)(2,1)} %refs_0_.3), channel_id=1, source_target_pairs={{0,2},{1,3},{2,0},{3,1},{4,6},{5,7},{6,4},{7,5},{8,10},{9,11},{10,... | collective-permute-start | bytes 2359304 | tf_op jit(solution)/shard_map/ppermute | solution.py:42
  3.7 52.6 %collective-permute-start = (bf16[512,768]{1,0:T(8,128)(2,1)}, bf16[512,768]{1,0:T(8,128)(2,1)S(1)}, u32[]{:S(2)}, u32[]{:S(2)}) collective-permute-start(bf16[512,768]{1,0:T(8,128)(2,1)} %refs_0_.3), channel_id=1, source_target_pairs={{0,1},{1,0},{2,3},{3,2},{4,5},{5,4},{6,7},{7,6},{8,9},{9,8},{10,11... | collective-permute-start | bytes 2359304 | tf_op jit(solution)/shard_map/ppermute | solution.py:42
  3.7 10.5 %collective-permute-start.3 = (bf16[96,768]{1,0:T(8,128)(2,1)}, bf16[96,768]{1,0:T(8,128)(2,1)S(1)}, u32[]{:S(2)}, u32[]{:S(2)}) collective-permute-start(bf16[96,768]{1,0:T(8,128)(2,1)} %param.23), channel_id=1, source_target_pairs={{0,16},{4,20},{8,24},{12,28},{16,0},{20,4},{24,8},{28,12},{1,17},{... | collective-permute-start | bytes 442376 | tf_op jit(solution)/shard_map/ppermute | solution.py:42
  10.8 114.0 %copy-start.13 = (f32[8,2048]{1,0:T(8,128)}, f32[8,2048]{1,0:T(8,128)S(1)}, u32[]{:S(2)}) copy-start(f32[8,2048]{1,0:T(8,128)S(1)} %get-tuple-element.173.refs_8_.sin_ref) | copy-start | bytes 196612
  10.8 114.0 %copy-start.14 = (f32[8,2048]{1,0:T(8,128)}, f32[8,2048]{1,0:T(8,128)S(1)}, u32[]{:S(2)}) copy-start(f32[8,2048]{1,0:T(8,128)S(1)} %get-tuple-element.174.refs_7_.cos_ref) | copy-start | bytes 196612
  14.3 8.7 %collective-permute-start.4 = (bf16[96,640]{1,0:T(8,128)(2,1)S(1)}, bf16[96,640]{1,0:T(8,128)(2,1)S(1)}, u32[]{:S(2)}, u32[]{:S(2)}) collective-permute-start(bf16[96,640]{1,0:T(8,128)(2,1)S(1)} %pad_maximum_fusion.12), channel_id=1, source_target_pairs={{0,16},{4,20},{8,24},{12,28},{16,0},{20,4},{24,8},{28,12},{1,17},{... | collective-permute-start | bytes 368648 | tf_op jit(solution)/shard_map/ppermute | solution.py:42
  16.0 13.0 %collective-permute-start.10 = (bf16[192,768]{1,0:T(8,128)(2,1)S(1)}, bf16[192,768]{1,0:T(8,128)(2,1)S(1)}, u32[]{:S(2)}, u32[]{:S(2)}) collective-permute-start(bf16[192,768]{1,0:T(8,128)(2,1)S(1)} %get-tuple-element.161), channel_id=1, source_target_pairs={{0,8},{4,12},{8,0},{12,4},{16,24},{20,28},{24,16},{28,20},{1,9},{5... | collective-permute-start | bytes 884744 | tf_op jit(solution)/shard_map/ppermute | solution.py:42
  23.0 10.6 %collective-permute-start.5 = (bf16[192,640]{1,0:T(8,128)(2,1)S(1)}, bf16[192,640]{1,0:T(8,128)(2,1)S(1)}, u32[]{:S(2)}, u32[]{:S(2)}) collective-permute-start(bf16[192,640]{1,0:T(8,128)(2,1)S(1)} %get-tuple-element.164), channel_id=1, source_target_pairs={{0,8},{4,12},{8,0},{12,4},{16,24},{20,28},{24,16},{28,20},{1,9},{5... | collective-permute-start | bytes 737288 | tf_op jit(solution)/shard_map/ppermute | solution.py:42
  29.0 16.3 %collective-permute-start.11 = (bf16[384,768]{1,0:T(8,128)(2,1)S(1)}, bf16[384,768]{1,0:T(8,128)(2,1)S(1)}, u32[]{:S(2)}, u32[]{:S(2)}) collective-permute-start(bf16[384,768]{1,0:T(8,128)(2,1)S(1)} %bitcast.102), channel_id=1, source_target_pairs={{0,4},{4,0},{8,12},{12,8},{16,20},{20,16},{24,28},{28,24},{1,5},{5... | collective-permute-start | bytes 1769480 | tf_op jit(solution)/shard_map/ppermute | solution.py:42
  33.7 10.3 %collective-permute-start.7 = (bf16[96,896]{1,0:T(8,128)(2,1)S(1)}, bf16[96,896]{1,0:T(8,128)(2,1)S(1)}, u32[]{:S(2)}, u32[]{:S(2)}) collective-permute-start(bf16[96,896]{1,0:T(8,128)(2,1)S(1)} %pad_maximum_fusion.10), channel_id=1, source_target_pairs={{0,16},{4,20},{8,24},{12,28},{16,0},{20,4},{24,8},{28,12},{1,17},{... | collective-permute-start | bytes 516104 | tf_op jit(solution)/shard_map/ppermute | solution.py:42
  33.9 22.2 %collective-permute-start.6 = (bf16[384,640]{1,0:T(8,128)(2,1)S(1)}, bf16[384,640]{1,0:T(8,128)(2,1)S(1)}, u32[]{:S(2)}, u32[]{:S(2)}) collective-permute-start(bf16[384,640]{1,0:T(8,128)(2,1)S(1)} %bitcast.104), channel_id=1, source_target_pairs={{0,4},{4,0},{8,12},{12,8},{16,20},{20,16},{24,28},{28,24},{1,5},{5... | collective-permute-start | bytes 1474568 | tf_op jit(solution)/shard_map/ppermute | solution.py:42
  35.5 19.2 %collective-permute-start.9 = (bf16[512,768]{1,0:T(8,128)(2,1)}, bf16[512,768]{1,0:T(8,128)(2,1)}, u32[]{:S(2)}, u32[]{:S(2)}) collective-permute-start(bf16[512,768]{1,0:T(8,128)(2,1)} %refs_4_), channel_id=1, source_target_pairs={{0,2},{1,3},{2,0},{3,1},{4,6},{5,7},{6,4},{7,5},{8,10},{9,11},{10,... | collective-permute-start | bytes 2359304 | tf_op jit(solution)/shard_map/ppermute | solution.py:42
  44.2 10.0 %collective-permute-start.8 = (bf16[192,896]{1,0:T(8,128)(2,1)S(1)}, bf16[192,896]{1,0:T(8,128)(2,1)S(1)}, u32[]{:S(2)}, u32[]{:S(2)}) collective-permute-start(bf16[192,896]{1,0:T(8,128)(2,1)S(1)} %get-tuple-element.156), channel_id=1, source_target_pairs={{0,8},{4,12},{8,0},{12,4},{16,24},{20,28},{24,16},{28,20},{1,9},{5... | collective-permute-start | bytes 1032200 | tf_op jit(solution)/shard_map/ppermute | solution.py:42
  45.4 11.8 %collective-permute-start.2 = (bf16[512,768]{1,0:T(8,128)(2,1)S(1)}, bf16[512,768]{1,0:T(8,128)(2,1)S(1)}, u32[]{:S(2)}, u32[]{:S(2)}) collective-permute-start(bf16[512,768]{1,0:T(8,128)(2,1)S(1)} %collective-permute-done.1.refs_2_), channel_id=1, source_target_pairs={{0,1},{1,0},{2,3},{3,2},{4,5},{5,4},{6,7},{7,6},{8,9},{9,8},{10,11... | collective-permute-start | bytes 2359304 | tf_op jit(solution)/shard_map/ppermute | solution.py:42
  54.9 16.2 %collective-permute-start.12 = (bf16[384,896]{1,0:T(8,128)(2,1)S(1)}, bf16[384,896]{1,0:T(8,128)(2,1)S(1)}, u32[]{:S(2)}, u32[]{:S(2)}) collective-permute-start(bf16[384,896]{1,0:T(8,128)(2,1)S(1)} %bitcast.100), channel_id=1, source_target_pairs={{0,4},{4,0},{8,12},{12,8},{16,20},{20,16},{24,28},{28,24},{1,5},{5... | collective-permute-start | bytes 2064392 | tf_op jit(solution)/shard_map/ppermute | solution.py:42
  72.4 37.8 %collective-permute-start.13 = (bf16[3,2048,128]{2,1,0:T(8,128)(2,1)S(1)}, bf16[3,2048,128]{2,1,0:T(8,128)(2,1)S(1)}, u32[]{:S(2)}, u32[]{:S(2)}) collective-permute-start(bf16[3,2048,128]{2,1,0:T(8,128)(2,1)S(1)} %get-tuple-element.78.refs_4_), channel_id=1, source_target_pairs={{0,4},{4,8},{8,12},{12,16},{16,20},{20,24},{24,28},{1,5},{5,9},{9,... | collective-permute-start | bytes 4718600 | tf_op jit(solution)/shard_map/ppermute | solution.py:48
  76.1 2.7 %collective-permute-start.14 = (bf16[512,768]{1,0:T(8,128)(2,1)}, bf16[512,768]{1,0:T(8,128)(2,1)}, u32[]{:S(2)}, u32[]{:S(2)}) collective-permute-start(bf16[512,768]{1,0:T(8,128)(2,1)} %refs_4_), channel_id=1, source_target_pairs={{0,1},{1,0},{2,3},{3,2},{4,5},{5,4},{6,7},{7,6},{8,9},{9,8},{10,11... | collective-permute-start | bytes 2359304 | tf_op jit(solution)/shard_map/ppermute | solution.py:42
  76.2 3.7 %collective-permute-start.15 = (bf16[512,768]{1,0:T(8,128)(2,1)}, bf16[512,768]{1,0:T(8,128)(2,1)}, u32[]{:S(2)}, u32[]{:S(2)}) collective-permute-start(bf16[512,768]{1,0:T(8,128)(2,1)} %collective-permute-done.9.refs_6_), channel_id=1, source_target_pairs={{0,1},{1,0},{2,3},{3,2},{4,5},{5,4},{6,7},{7,6},{8,9},{9,8},{10,11... | collective-permute-start | bytes 2359304 | tf_op jit(solution)/shard_map/ppermute | solution.py:42
  110.2 45.5 %collective-permute-start.17 = (bf16[384,1536]{1,0:T(8,128)(2,1)}, bf16[384,1536]{1,0:T(8,128)(2,1)S(1)}, u32[]{:S(2)}, u32[]{:S(2)}) collective-permute-start(bf16[384,1536]{1,0:T(8,128)(2,1)} %get-tuple-element.89), channel_id=1, source_target_pairs={{0,4},{4,0},{8,12},{12,8},{16,20},{20,16},{24,28},{28,24},{1,5},{5... | collective-permute-start | bytes 3538952 | tf_op jit(solution)/shard_map/ppermute | solution.py:42
  123.3 32.4 %collective-permute-start.16 = (bf16[3,1024,128]{2,1,0:T(8,128)(2,1)S(1)}, bf16[3,1024,128]{2,1,0:T(8,128)(2,1)S(1)}, u32[]{:S(2)}, u32[]{:S(2)}) collective-permute-start(bf16[3,1024,128]{2,1,0:T(8,128)(2,1)S(1)} %get-tuple-element.86), channel_id=1, source_target_pairs={{4,0},{8,4},{12,8},{16,12},{20,16},{24,20},{28,24},{5,1},{9,5},{13... | collective-permute-start | bytes 2359304 | tf_op jit(solution)/shard_map/ppermute | solution.py:48
  155.7 24.1 %collective-permute-start.19 = (bf16[3,1024,128]{2,1,0:T(8,128)(2,1)}, bf16[3,1024,128]{2,1,0:T(8,128)(2,1)S(1)}, u32[]{:S(2)}, u32[]{:S(2)}) collective-permute-start(bf16[3,1024,128]{2,1,0:T(8,128)(2,1)} %get-tuple-element.104), channel_id=1, source_target_pairs={{4,0},{8,4},{12,8},{16,12},{20,16},{24,20},{28,24},{5,1},{9,5},{13... | collective-permute-start | bytes 2359304 | tf_op jit(solution)/shard_map/ppermute | solution.py:48
  166.6 23.8 %collective-permute-start.20 = (bf16[192,1536]{1,0:T(8,128)(2,1)S(1)}, bf16[192,1536]{1,0:T(8,128)(2,1)S(1)}, u32[]{:S(2)}, u32[]{:S(2)}) collective-permute-start(bf16[192,1536]{1,0:T(8,128)(2,1)S(1)} %bitcast.112), channel_id=1, source_target_pairs={{0,8},{4,12},{8,0},{12,4},{16,24},{20,28},{24,16},{28,20},{1,9},{5... | collective-permute-start | bytes 1769480 | tf_op jit(solution)/shard_map/ppermute | solution.py:42
  179.7 13.2 %collective-permute-start.18 = (bf16[1024,768]{1,0:T(8,128)(2,1)}, bf16[1024,768]{1,0:T(8,128)(2,1)S(1)}, u32[]{:S(2)}, u32[]{:S(2)}) collective-permute-start(bf16[1024,768]{1,0:T(8,128)(2,1)} %get-tuple-element.101), channel_id=1, source_target_pairs={{0,1},{1,0},{2,3},{3,2},{4,5},{5,4},{6,7},{7,6},{8,9},{9,8},{10,11... | collective-permute-start | bytes 4718600 | tf_op jit(solution)/shard_map/ppermute | solution.py:42
  190.3 4.7 %collective-permute-start.21 = (bf16[1024,768]{1,0:T(8,128)(2,1)}, bf16[1024,768]{1,0:T(8,128)(2,1)S(1)}, u32[]{:S(2)}, u32[]{:S(2)}) collective-permute-start(bf16[1024,768]{1,0:T(8,128)(2,1)} %get-tuple-element.115), channel_id=1, source_target_pairs={{0,1},{1,0},{2,3},{3,2},{4,5},{5,4},{6,7},{7,6},{8,9},{9,8},{10,11... | collective-permute-start | bytes 4718600 | tf_op jit(solution)/shard_map/ppermute | solution.py:42
  192.4 15.9 %collective-permute-start.24 = (bf16[400,768]{1,0:T(8,128)(2,1)S(1)}, bf16[400,768]{1,0:T(8,128)(2,1)S(1)}, u32[]{:S(2)}, u32[]{:S(2)}) collective-permute-start(bf16[400,768]{1,0:T(8,128)(2,1)S(1)} %copy-done.35), channel_id=1, source_target_pairs={{0,4},{4,0},{8,12},{12,8},{16,20},{20,16},{24,28},{28,24},{1,5},{5... | collective-permute-start | bytes 1843208 | tf_op jit(solution)/shard_map/ppermute | solution.py:42
  196.3 23.3 %collective-permute-start.22 = (bf16[512,768]{1,0:T(8,128)(2,1)S(1)}, bf16[512,768]{1,0:T(8,128)(2,1)S(1)}, u32[]{:S(2)}, u32[]{:S(2)}) collective-permute-start(bf16[512,768]{1,0:T(8,128)(2,1)S(1)} %slice.238), channel_id=1, source_target_pairs={{0,2},{1,3},{2,0},{3,1},{4,6},{5,7},{6,4},{7,5},{8,10},{9,11},{10,... | collective-permute-start | bytes 2359304 | tf_op jit(solution)/shard_map/ppermute | solution.py:42
  197.2 23.3 %collective-permute-start.27 = (bf16[96,1536]{1,0:T(8,128)(2,1)S(1)}, bf16[96,1536]{1,0:T(8,128)(2,1)S(1)}, u32[]{:S(2)}, u32[]{:S(2)}) collective-permute-start(bf16[96,1536]{1,0:T(8,128)(2,1)S(1)} %fusion.13), channel_id=1, source_target_pairs={{0,16},{4,20},{8,24},{12,28},{16,0},{20,4},{24,8},{28,12},{1,17},{... | collective-permute-start | bytes 884744 | tf_op jit(solution)/shard_map/ppermute | solution.py:42
  209.1 10.5 %collective-permute-start.25 = (bf16[208,768]{1,0:T(8,128)(2,1)S(1)}, bf16[208,768]{1,0:T(8,128)(2,1)S(1)}, u32[]{:S(2)}, u32[]{:S(2)}) collective-permute-start(bf16[208,768]{1,0:T(8,128)(2,1)S(1)} %pad_maximum_fusion.7), channel_id=1, source_target_pairs={{0,8},{4,12},{8,0},{12,4},{16,24},{20,28},{24,16},{28,20},{1,9},{5... | collective-permute-start | bytes 958472 | tf_op jit(solution)/shard_map/ppermute | solution.py:42
  220.4 10.0 %collective-permute-start.26 = (bf16[112,768]{1,0:T(8,128)(2,1)S(1)}, bf16[112,768]{1,0:T(8,128)(2,1)}, u32[]{:S(2)}, u32[]{:S(2)}) collective-permute-start(bf16[112,768]{1,0:T(8,128)(2,1)S(1)} %pad_maximum_fusion.11), channel_id=1, source_target_pairs={{0,16},{4,20},{8,24},{12,28},{16,0},{20,4},{24,8},{28,12},{1,17},{... | collective-permute-start | bytes 516104 | tf_op jit(solution)/shard_map/ppermute | solution.py:42
  220.5 20.7 %collective-permute-start.23 = (bf16[512,768]{1,0:T(8,128)(2,1)S(1)}, bf16[512,768]{1,0:T(8,128)(2,1)S(1)}, u32[]{:S(2)}, u32[]{:S(2)}) collective-permute-start(bf16[512,768]{1,0:T(8,128)(2,1)S(1)} %slice.239), channel_id=1, source_target_pairs={{0,2},{1,3},{2,0},{3,1},{4,6},{5,7},{6,4},{7,5},{8,10},{9,11},{10,... | collective-permute-start | bytes 2359304 | tf_op jit(solution)/shard_map/ppermute | solution.py:42
  232.4 3.0 %collective-permute-start.28 = (f32[8,768]{1,0:T(8,128)}, f32[8,768]{1,0:T(8,128)S(1)}, u32[]{:S(2)}, u32[]{:S(2)}) collective-permute-start(f32[8,768]{1,0:T(8,128)} %get-tuple-element.128), channel_id=1, source_target_pairs={{0,1},{1,0},{2,3},{3,2},{4,5},{5,4},{6,7},{7,6},{8,9},{9,8},{10,11... | collective-permute-start | bytes 73736 | tf_op jit(solution)/shard_map/ppermute | solution.py:42
  236.1 4.5 %collective-permute-start.29 = (f32[8,768]{1,0:T(8,128)S(1)}, f32[8,768]{1,0:T(8,128)S(1)}, u32[]{:S(2)}, u32[]{:S(2)}) collective-permute-start(f32[8,768]{1,0:T(8,128)S(1)} %add.131), channel_id=1, source_target_pairs={{0,2},{1,3},{2,0},{3,1},{4,6},{5,7},{6,4},{7,5},{8,10},{9,11},{10,... | collective-permute-start | bytes 73736 | tf_op jit(solution)/shard_map/ppermute | solution.py:42
  (34 other events, 353.4 us)

commit v5 on v4

--- a/solution.py
+++ b/solution.py
@@ -15,7 +15,7 @@
 NEG = -1e30
 TQ = 256
 TK = 256
-NK = 2
+NK = 4
 TR = 512
 FR = 512
 PR = 1024

time: 245 us -> 245 us (level)
  transfers between devices with their start and end apart: 30 -> 30, of which waited for: 17 -> 17; matrix products, arithmetic and copies ran while one was open for 10% -> 10% of each run, Pallas kernels for 38% -> 39%
where the time goes in v5:
time: 245 us; the launch traced here: 244 us
  Pallas kernels  94.5 us (39%)
  waiting for transfers between devices  78.2 us (32%)
  starting transfers between devices  33.2 us (14%)
  local copies, waits for them, and re-layouts  19.7 us (8%)
  other arithmetic  17 us (7%)
    ppermute x27, waiting for transfers between devices, swap(): return lax.ppermute(value, axis, [(i, i ^ mask) for i in range(count)])  62.8 us
    pallas_call x1, Pallas kernels, ffn(): pl.pallas_call(functools.partial(ffn_kernel, pieces=len(gs), blk=blk, chu...  30.3 us
    ppermute x27, starting transfers between devices, swap(): return lax.ppermute(value, axis, [(i, i ^ mask) for i in range(count)])  26.7 us
    pallas_call x2, Pallas kernels, attention(): pl.pallas_call(functools.partial(attn_kernel, T=T, blk=blk, heads=heads,...  24.9 us
    pallas_call x2, Pallas kernels, post(): pl.pallas_call(functools.partial(post_kernel, chunk=chunk), grid_spec=plt...  18.5 us
    ppermute x3, waiting for transfers between devices, shift(): return lax.ppermute(value, axis, route)  15.4 us
    unnamed x75, local copies, waits for them, and re-layouts  10.3 us
    pallas_call x1, Pallas kernels, mid(): pl.pallas_call(mid_kernel, grid=(T // MR,), in_specs=[cols, cols, rows, r...  9.29 us
  transfers between devices with their start and end apart: 30, of which 17 were waited for; matrix products, arithmetic and copies ran while one was open for 10% of the time, Pallas kernels for 39%

profile of v5, /device:TPU:0, one launch (start us, length us, event | category | flops | bytes accessed | tf_op | source)
XLA Modules:
  0.0 244.0 jit_solution(18176823731891815237)
XLA Ops:
  0.7 3.0 %collective-permute-start.1 = (bf16[512,768]{1,0:T(8,128)(2,1)}, bf16[512,768]{1,0:T(8,128)(2,1)S(1)}, u32[]{:S(2)}, u32[]{:S(2)}) collective-permute-start(bf16[512,768]{1,0:T(8,128)(2,1)} %refs_0_.3), channel_id=1, source_target_pairs={{0,2},{1,3},{2,0},{3,1},{4,6},{5,7},{6,4},{7,5},{8,10},{9,11},{10,... | collective-permute-start | bytes 2359304 | tf_op jit(solution)/shard_map/ppermute | solution.py:42
  3.7 2.6 %collective-permute-start.3 = (bf16[96,768]{1,0:T(8,128)(2,1)}, bf16[96,768]{1,0:T(8,128)(2,1)S(1)}, u32[]{:S(2)}, u32[]{:S(2)}) collective-permute-start(bf16[96,768]{1,0:T(8,128)(2,1)} %param.23), channel_id=1, source_target_pairs={{0,16},{4,20},{8,24},{12,28},{16,0},{20,4},{24,8},{28,12},{1,17},{... | collective-permute-start | bytes 442376 | tf_op jit(solution)/shard_map/ppermute | solution.py:42
  12.7 1.6 collective-permute-done.3
  16.0 4.1 %collective-permute-start.10 = (bf16[192,768]{1,0:T(8,128)(2,1)S(1)}, bf16[192,768]{1,0:T(8,128)(2,1)S(1)}, u32[]{:S(2)}, u32[]{:S(2)}) collective-permute-start(bf16[192,768]{1,0:T(8,128)(2,1)S(1)} %get-tuple-element.161), channel_id=1, source_target_pairs={{0,8},{4,12},{8,0},{12,4},{16,24},{20,28},{24,16},{28,20},{1,9},{5... | collective-permute-start | bytes 884744 | tf_op jit(solution)/shard_map/ppermute | solution.py:42
  20.1 2.9 %collective-permute-done.4 = bf16[96,640]{1,0:T(8,128)(2,1)S(1)} collective-permute-done((bf16[96,640]{1,0:T(8,128)(2,1)S(1)}, bf16[96,640]{1,0:T(8,128)(2,1)S(1)}, u32[]{:S(2)}, u32[]{:S(2)}) %collective-permute-start.4) | collective-permute-done | bytes 122912 | tf_op jit(solution)/shard_map/ppermute | solution.py:42
  23.1 5.8 %collective-permute-done.10 = bf16[192,768]{1,0:T(8,128)(2,1)S(1)} collective-permute-done((bf16[192,768]{1,0:T(8,128)(2,1)S(1)}, bf16[192,768]{1,0:T(8,128)(2,1)S(1)}, u32[]{:S(2)}, u32[]{:S(2)}) %collective-permute-start.10) | collective-permute-done | bytes 294944 | tf_op jit(solution)/shard_map/ppermute | solution.py:42
  29.0 1.6 collective-permute-start.11
  30.6 3.0 %collective-permute-done.5 = bf16[192,640]{1,0:T(8,128)(2,1)S(1)} collective-permute-done((bf16[192,640]{1,0:T(8,128)(2,1)S(1)}, bf16[192,640]{1,0:T(8,128)(2,1)S(1)}, u32[]{:S(2)}, u32[]{:S(2)}) %collective-permute-start.5) | collective-permute-done | bytes 245792 | tf_op jit(solution)/shard_map/ppermute | solution.py:42
  33.9 1.6 collective-permute-start.6
  36.0 8.0 %collective-permute-done.7 = bf16[96,896]{1,0:T(8,128)(2,1)S(1)} collective-permute-done((bf16[96,896]{1,0:T(8,128)(2,1)S(1)}, bf16[96,896]{1,0:T(8,128)(2,1)S(1)}, u32[]{:S(2)}, u32[]{:S(2)}) %collective-permute-start.7) | collective-permute-done | bytes 172064 | tf_op jit(solution)/shard_map/ppermute | solution.py:42
  46.6 7.6 %collective-permute-done.8 = bf16[192,896]{1,0:T(8,128)(2,1)S(1)} collective-permute-done((bf16[192,896]{1,0:T(8,128)(2,1)S(1)}, bf16[192,896]{1,0:T(8,128)(2,1)S(1)}, u32[]{:S(2)}, u32[]{:S(2)}) %collective-permute-start.8) | collective-permute-done | bytes 344096 | tf_op jit(solution)/shard_map/ppermute | solution.py:42
  59.2 7.7 %pre.1 = (bf16[2048,768]{1,0:T(8,128)(2,1)S(1)}, bf16[3,2048,128]{2,1,0:T(8,128)(2,1)S(1)}, bf16[3,2048,128]{2,1,0:T(8,128)(2,1)S(1)}) custom-call(bf16[512,768]{1,0:T(8,128)(2,1)S(1)} %copy-done, bf16[512,768]{1,0:T(8,128)(2,1)S(1)} %copy-done.10, bf16[512,768]{1,0:T(8,128)(2,1)S(1)} %copy-done.8, bf16[512,768]{1,0:T(8,128)(2,1)S(1)} %collective-permute-done.2.refs_3_, ...), custom_call_target="tpu_custom_call" | custom-call | flops 575000000 | bytes 1000 | tf_op jit(solution)/shard_map/pre/pallas_call | solution.py:199
  66.9 4.2 %collective-permute-done.12 = bf16[384,896]{1,0:T(8,128)(2,1)S(1)} collective-permute-done((bf16[384,896]{1,0:T(8,128)(2,1)S(1)}, bf16[384,896]{1,0:T(8,128)(2,1)S(1)}, u32[]{:S(2)}, u32[]{:S(2)}) %collective-permute-start.12) | collective-permute-done | bytes 688160 | tf_op jit(solution)/shard_map/ppermute | solution.py:42
  72.4 3.7 %collective-permute-start.13 = (bf16[3,2048,128]{2,1,0:T(8,128)(2,1)S(1)}, bf16[3,2048,128]{2,1,0:T(8,128)(2,1)S(1)}, u32[]{:S(2)}, u32[]{:S(2)}) collective-permute-start(bf16[3,2048,128]{2,1,0:T(8,128)(2,1)S(1)} %get-tuple-element.78.refs_4_), channel_id=1, source_target_pairs={{0,4},{4,8},{8,12},{12,16},{16,20},{20,24},{24,28},{1,5},{5,9},{9,... | collective-permute-start | bytes 4718600 | tf_op jit(solution)/shard_map/ppermute | solution.py:48
  76.7 2.1 collective-permute-done.14.refs_5_
  79.9 30.3 %ffn.1 = (bf16[2048,768]{1,0:T(8,128)(2,1)}, bf16[2048,768]{1,0:T(8,128)(2,1)}, bf16[2048,768]{1,0:T(8,128)(2,1)}, bf16[2048,768]{1,0:T(8,128)(2,1)}, bf16[3,204...) custom-call(bf16[512,768]{1,0:T(8,128)(2,1)} %refs_0_.3, ...), custom_call_target="tpu_custom_call" | custom-call | flops 575000000 | bytes 1000 | tf_op jit(solution)/shard_map/ffn/pallas_call | solution.py:289
  110.2 2.2 collective-permute-start.17
  113.8 8.7 %attn.2 = (bf16[192,1024]{1,0:T(8,128)(2,1)S(1)}, bf16[192,1024]{1,0:T(8,128)(2,1)S(1)}, bf16[3,1024,128]{2,1,0:T(8,128)(2,1)S(1)}, f32[3,2048,128]{2,1,0:T(8,128)S(1)}) custom-call(s32[2]{0:T(128)S(1)} %pad_add_fusion.refs_0_.place_ref, s32[8]{0:T(128)S(1)} %and_select_fusion.refs_1_, s32[1,2048]{1,0:T(1,128)S(1)} %add_subtract_fusion.refs_2_, ...), custom_call_target="tpu_custom_call" | custom-call | flops 115000000 | bytes 1000 | tf_op jit(solution)/shard_map/attn/pallas_call | solution.py:444
  124.1 16.2 %attn.3 = (bf16[192,2048]{1,0:T(8,128)(2,1)S(1)}, bf16[192,2048]{1,0:T(8,128)(2,1)S(1)}, bf16[3,1024,128]{2,1,0:T(8,128)(2,1)}, f32[3,1024,128]{2,1,0:T(8,128)S(1)}, f32[3,1024,128]{2,1,0:T(8,128)S(1)}) custom-call(s32[2]{0:T(128)S(1)} %pad_add_fusion.refs_0_.place_ref, s32[8]{0:T(128)S(1)} %and_select_fusion.refs_1_, ...), custom_call_target="tpu_custom_call" | custom-call | flops 115000000 | bytes 1000 | tf_op jit(solution)/shard_map/attn/pallas_call | solution.py:444
  140.3 15.4 %collective-permute-done.16.ahead_ref = bf16[3,1024,128]{2,1,0:T(8,128)(2,1)S(1)} collective-permute-done((bf16[3,1024,128]{2,1,0:T(8,128)(2,1)S(1)}, bf16[3,1024,128]{2,1,0:T(8,128)(2,1)S(1)}, u32[]{:S(2)}, u32[]{:S(2)}) %collective-permute-start.16) | collective-permute-done | bytes 786464 | tf_op jit(solution)/shard_map/ppermute | solution.py:48
  157.4 9.1 %post.2 = (bf16[1024,768]{1,0:T(8,128)(2,1)}, bf16[1024,768]{1,0:T(8,128)(2,1)}, f32[768,384]{1,0:T(8,128)}, f32[8,768]{1,0:T(8,128)}) custom-call(s32[2]{0:T(128)} %copy-done.17, f32[3,1024,128]{2,1,0:T(8,128)} %copy-done.15, bf16[3,1024,128]{2,1,0:T(8,128)(2,1)} %copy-done.23, bf16[192,2048]{1,0:T(8,128)(2,1)} %copy-done.12, f32[8,2048]{1,0:T(8,128)} %copy-done.14, ...), custom_call_target="tpu_custom_call" | custom-call | flops 115000000 | bytes 1000 | tf_op jit(solution)/shard_map/post/pallas_call | solution.py:584
  166.6 3.9 %collective-permute-start.20 = (bf16[192,1536]{1,0:T(8,128)(2,1)S(1)}, bf16[192,1536]{1,0:T(8,128)(2,1)S(1)}, u32[]{:S(2)}, u32[]{:S(2)}) collective-permute-start(bf16[192,1536]{1,0:T(8,128)(2,1)S(1)} %bitcast.112), channel_id=1, source_target_pairs={{0,8},{4,12},{8,0},{12,4},{16,24},{20,28},{24,16},{28,20},{1,9},{5... | collective-permute-start | bytes 1769480 | tf_op jit(solution)/shard_map/ppermute | solution.py:42
  170.4 9.3 %mid.1 = (bf16[1024,768]{1,0:T(8,128)(2,1)}, bf16[1024,768]{1,0:T(8,128)(2,1)}, bf16[768,384]{1,0:T(8,128)(2,1)}) custom-call(bf16[192,2048]{1,0:T(8,128)(2,1)} %copy-done.16, bf16[192,2048]{1,0:T(8,128)(2,1)} %copy-done.12, bf16[2048,768]{1,0:T(8,128)(2,1)} %copy-done.3, bf16[2048,768]{1,0:T(8,128)(2,1)} %get-tuple-element.98.g_ref, ...), custom_call_target="tpu_custom_call" | custom-call | flops 115000000 | bytes 1000 | tf_op jit(solution)/shard_map/mid/pallas_call | solution.py:492
  180.7 9.4 %post.3 = (bf16[1024,768]{1,0:T(8,128)(2,1)}, bf16[1024,768]{1,0:T(8,128)(2,1)}, bf16[400,768]{1,0:T(8,128)(2,1)}, bf16[384,768]{1,0:T(8,128)(2,1)}, f32[8,768]{1,0:T(8,128)}) custom-call(s32[2]{0:T(128)} %copy-done.17, f32[3,1024,128]{2,1,0:T(8,128)} %copy-done.18, ...), custom_call_target="tpu_custom_call", output_to_operand_aliasing={{0}: (11, {}), {1}: (12, {})} | custom-call | flops 9200000000 | bytes 1000 | tf_op jit(solution)/shard_map/post/pallas_call | solution.py:584
  197.3 10.9 %collective-permute-done.24 = bf16[400,768]{1,0:T(8,128)(2,1)S(1)} collective-permute-done((bf16[400,768]{1,0:T(8,128)(2,1)S(1)}, bf16[400,768]{1,0:T(8,128)(2,1)S(1)}, u32[]{:S(2)}, u32[]{:S(2)}) %collective-permute-start.24) | collective-permute-done | bytes 614432 | tf_op jit(solution)/shard_map/ppermute | solution.py:42
  210.3 9.3 %collective-permute-done.25 = bf16[208,768]{1,0:T(8,128)(2,1)S(1)} collective-permute-done((bf16[208,768]{1,0:T(8,128)(2,1)S(1)}, bf16[208,768]{1,0:T(8,128)(2,1)S(1)}, u32[]{:S(2)}, u32[]{:S(2)}) %collective-permute-start.25) | collective-permute-done | bytes 319520 | tf_op jit(solution)/shard_map/ppermute | solution.py:42
  222.7 2.9 %fusion.7 = f32[512,768]{1,0:T(8,128)} fusion(bf16[512,768]{1,0:T(8,128)(2,1)S(1)} %copy-done.1, bf16[512,768]{1,0:T(8,128)(2,1)} %refs_4_, f32[512]{0:T(512)S(1)} %get-tuple-element.181, f32[512]{0:T(512)S(1)} %get-tuple-element.182, f32[512]{0:T(512)S(1)} %add_rsqrt_fusion, f32[512]{0:T(512)S(1)} %broadcast_multiply_fusion.2, ...), kind=kLoop, calls=%fused_computation.13 | loop fusion | flops 4325376 | bytes 5513216 | tf_op jit(solution)/shard_map/add | solution.py:744
  225.6 2.0 ffn_finish.1
  228.4 2.1 collective-permute-done.26.other_ref
  230.4 1.9 mix_finish.1
  238.2 2.4 collective-permute-done.29
  241.2 2.8 %fusion.10 = f32[512,768]{1,0:T(8,128)} fusion(bf16[512,768]{1,0:T(8,128)(2,1)S(1)} %copy-done.1, f32[1024,768]{1,0:T(8,128)} %copy-done.19, bf16[512,768]{1,0:T(8,128)(2,1)S(1)} %collective-permute-done.23, f32[768]{0:T(1024)S(1)} %copy-done.33), kind=kLoop, calls=%fused_computation.16 | loop fusion | flops 1966080 | bytes 4721664 | tf_op jit(solution)/shard_map/add | solution.py:747
  (200 shorter events, 44.5 us)
Async XLA Ops:
  0.7 34.8 %collective-permute-start.1 = (bf16[512,768]{1,0:T(8,128)(2,1)}, bf16[512,768]{1,0:T(8,128)(2,1)S(1)}, u32[]{:S(2)}, u32[]{:S(2)}) collective-permute-start(bf16[512,768]{1,0:T(8,128)(2,1)} %refs_0_.3), channel_id=1, source_target_pairs={{0,2},{1,3},{2,0},{3,1},{4,6},{5,7},{6,4},{7,5},{8,10},{9,11},{10,... | collective-permute-start | bytes 2359304 | tf_op jit(solution)/shard_map/ppermute | solution.py:42
  3.7 52.6 %collective-permute-start = (bf16[512,768]{1,0:T(8,128)(2,1)}, bf16[512,768]{1,0:T(8,128)(2,1)S(1)}, u32[]{:S(2)}, u32[]{:S(2)}) collective-permute-start(bf16[512,768]{1,0:T(8,128)(2,1)} %refs_0_.3), channel_id=1, source_target_pairs={{0,1},{1,0},{2,3},{3,2},{4,5},{5,4},{6,7},{7,6},{8,9},{9,8},{10,11... | collective-permute-start | bytes 2359304 | tf_op jit(solution)/shard_map/ppermute | solution.py:42
  3.7 10.5 %collective-permute-start.3 = (bf16[96,768]{1,0:T(8,128)(2,1)}, bf16[96,768]{1,0:T(8,128)(2,1)S(1)}, u32[]{:S(2)}, u32[]{:S(2)}) collective-permute-start(bf16[96,768]{1,0:T(8,128)(2,1)} %param.23), channel_id=1, source_target_pairs={{0,16},{4,20},{8,24},{12,28},{16,0},{20,4},{24,8},{28,12},{1,17},{... | collective-permute-start | bytes 442376 | tf_op jit(solution)/shard_map/ppermute | solution.py:42
  10.8 113.2 %copy-start.13 = (f32[8,2048]{1,0:T(8,128)}, f32[8,2048]{1,0:T(8,128)S(1)}, u32[]{:S(2)}) copy-start(f32[8,2048]{1,0:T(8,128)S(1)} %get-tuple-element.173.refs_8_.sin_ref) | copy-start | bytes 196612
  10.8 113.2 %copy-start.14 = (f32[8,2048]{1,0:T(8,128)}, f32[8,2048]{1,0:T(8,128)S(1)}, u32[]{:S(2)}) copy-start(f32[8,2048]{1,0:T(8,128)S(1)} %get-tuple-element.174.refs_7_.cos_ref) | copy-start | bytes 196612
  14.3 8.7 %collective-permute-start.4 = (bf16[96,640]{1,0:T(8,128)(2,1)S(1)}, bf16[96,640]{1,0:T(8,128)(2,1)S(1)}, u32[]{:S(2)}, u32[]{:S(2)}) collective-permute-start(bf16[96,640]{1,0:T(8,128)(2,1)S(1)} %pad_maximum_fusion.12), channel_id=1, source_target_pairs={{0,16},{4,20},{8,24},{12,28},{16,0},{20,4},{24,8},{28,12},{1,17},{... | collective-permute-start | bytes 368648 | tf_op jit(solution)/shard_map/ppermute | solution.py:42
  16.0 13.0 %collective-permute-start.10 = (bf16[192,768]{1,0:T(8,128)(2,1)S(1)}, bf16[192,768]{1,0:T(8,128)(2,1)S(1)}, u32[]{:S(2)}, u32[]{:S(2)}) collective-permute-start(bf16[192,768]{1,0:T(8,128)(2,1)S(1)} %get-tuple-element.161), channel_id=1, source_target_pairs={{0,8},{4,12},{8,0},{12,4},{16,24},{20,28},{24,16},{28,20},{1,9},{5... | collective-permute-start | bytes 884744 | tf_op jit(solution)/shard_map/ppermute | solution.py:42
  23.0 10.6 %collective-permute-start.5 = (bf16[192,640]{1,0:T(8,128)(2,1)S(1)}, bf16[192,640]{1,0:T(8,128)(2,1)S(1)}, u32[]{:S(2)}, u32[]{:S(2)}) collective-permute-start(bf16[192,640]{1,0:T(8,128)(2,1)S(1)} %get-tuple-element.164), channel_id=1, source_target_pairs={{0,8},{4,12},{8,0},{12,4},{16,24},{20,28},{24,16},{28,20},{1,9},{5... | collective-permute-start | bytes 737288 | tf_op jit(solution)/shard_map/ppermute | solution.py:42
  29.0 16.3 %collective-permute-start.11 = (bf16[384,768]{1,0:T(8,128)(2,1)S(1)}, bf16[384,768]{1,0:T(8,128)(2,1)S(1)}, u32[]{:S(2)}, u32[]{:S(2)}) collective-permute-start(bf16[384,768]{1,0:T(8,128)(2,1)S(1)} %bitcast.102), channel_id=1, source_target_pairs={{0,4},{4,0},{8,12},{12,8},{16,20},{20,16},{24,28},{28,24},{1,5},{5... | collective-permute-start | bytes 1769480 | tf_op jit(solution)/shard_map/ppermute | solution.py:42
  33.7 10.3 %collective-permute-start.7 = (bf16[96,896]{1,0:T(8,128)(2,1)S(1)}, bf16[96,896]{1,0:T(8,128)(2,1)S(1)}, u32[]{:S(2)}, u32[]{:S(2)}) collective-permute-start(bf16[96,896]{1,0:T(8,128)(2,1)S(1)} %pad_maximum_fusion.10), channel_id=1, source_target_pairs={{0,16},{4,20},{8,24},{12,28},{16,0},{20,4},{24,8},{28,12},{1,17},{... | collective-permute-start | bytes 516104 | tf_op jit(solution)/shard_map/ppermute | solution.py:42
  33.9 22.2 %collective-permute-start.6 = (bf16[384,640]{1,0:T(8,128)(2,1)S(1)}, bf16[384,640]{1,0:T(8,128)(2,1)S(1)}, u32[]{:S(2)}, u32[]{:S(2)}) collective-permute-start(bf16[384,640]{1,0:T(8,128)(2,1)S(1)} %bitcast.104), channel_id=1, source_target_pairs={{0,4},{4,0},{8,12},{12,8},{16,20},{20,16},{24,28},{28,24},{1,5},{5... | collective-permute-start | bytes 1474568 | tf_op jit(solution)/shard_map/ppermute | solution.py:42
  35.5 19.2 %collective-permute-start.9 = (bf16[512,768]{1,0:T(8,128)(2,1)}, bf16[512,768]{1,0:T(8,128)(2,1)}, u32[]{:S(2)}, u32[]{:S(2)}) collective-permute-start(bf16[512,768]{1,0:T(8,128)(2,1)} %refs_4_), channel_id=1, source_target_pairs={{0,2},{1,3},{2,0},{3,1},{4,6},{5,7},{6,4},{7,5},{8,10},{9,11},{10,... | collective-permute-start | bytes 2359304 | tf_op jit(solution)/shard_map/ppermute | solution.py:42
  44.2 10.0 %collective-permute-start.8 = (bf16[192,896]{1,0:T(8,128)(2,1)S(1)}, bf16[192,896]{1,0:T(8,128)(2,1)S(1)}, u32[]{:S(2)}, u32[]{:S(2)}) collective-permute-start(bf16[192,896]{1,0:T(8,128)(2,1)S(1)} %get-tuple-element.156), channel_id=1, source_target_pairs={{0,8},{4,12},{8,0},{12,4},{16,24},{20,28},{24,16},{28,20},{1,9},{5... | collective-permute-start | bytes 1032200 | tf_op jit(solution)/shard_map/ppermute | solution.py:42
  45.4 11.8 %collective-permute-start.2 = (bf16[512,768]{1,0:T(8,128)(2,1)S(1)}, bf16[512,768]{1,0:T(8,128)(2,1)S(1)}, u32[]{:S(2)}, u32[]{:S(2)}) collective-permute-start(bf16[512,768]{1,0:T(8,128)(2,1)S(1)} %collective-permute-done.1.refs_2_), channel_id=1, source_target_pairs={{0,1},{1,0},{2,3},{3,2},{4,5},{5,4},{6,7},{7,6},{8,9},{9,8},{10,11... | collective-permute-start | bytes 2359304 | tf_op jit(solution)/shard_map/ppermute | solution.py:42
  54.9 16.2 %collective-permute-start.12 = (bf16[384,896]{1,0:T(8,128)(2,1)S(1)}, bf16[384,896]{1,0:T(8,128)(2,1)S(1)}, u32[]{:S(2)}, u32[]{:S(2)}) collective-permute-start(bf16[384,896]{1,0:T(8,128)(2,1)S(1)} %bitcast.100), channel_id=1, source_target_pairs={{0,4},{4,0},{8,12},{12,8},{16,20},{20,16},{24,28},{28,24},{1,5},{5... | collective-permute-start | bytes 2064392 | tf_op jit(solution)/shard_map/ppermute | solution.py:42
  72.4 37.8 %collective-permute-start.13 = (bf16[3,2048,128]{2,1,0:T(8,128)(2,1)S(1)}, bf16[3,2048,128]{2,1,0:T(8,128)(2,1)S(1)}, u32[]{:S(2)}, u32[]{:S(2)}) collective-permute-start(bf16[3,2048,128]{2,1,0:T(8,128)(2,1)S(1)} %get-tuple-element.78.refs_4_), channel_id=1, source_target_pairs={{0,4},{4,8},{8,12},{12,16},{16,20},{20,24},{24,28},{1,5},{5,9},{9,... | collective-permute-start | bytes 4718600 | tf_op jit(solution)/shard_map/ppermute | solution.py:48
  76.1 2.7 %collective-permute-start.14 = (bf16[512,768]{1,0:T(8,128)(2,1)}, bf16[512,768]{1,0:T(8,128)(2,1)}, u32[]{:S(2)}, u32[]{:S(2)}) collective-permute-start(bf16[512,768]{1,0:T(8,128)(2,1)} %refs_4_), channel_id=1, source_target_pairs={{0,1},{1,0},{2,3},{3,2},{4,5},{5,4},{6,7},{7,6},{8,9},{9,8},{10,11... | collective-permute-start | bytes 2359304 | tf_op jit(solution)/shard_map/ppermute | solution.py:42
  76.2 3.7 %collective-permute-start.15 = (bf16[512,768]{1,0:T(8,128)(2,1)}, bf16[512,768]{1,0:T(8,128)(2,1)}, u32[]{:S(2)}, u32[]{:S(2)}) collective-permute-start(bf16[512,768]{1,0:T(8,128)(2,1)} %collective-permute-done.9.refs_6_), channel_id=1, source_target_pairs={{0,1},{1,0},{2,3},{3,2},{4,5},{5,4},{6,7},{7,6},{8,9},{9,8},{10,11... | collective-permute-start | bytes 2359304 | tf_op jit(solution)/shard_map/ppermute | solution.py:42
  110.2 45.5 %collective-permute-start.17 = (bf16[384,1536]{1,0:T(8,128)(2,1)}, bf16[384,1536]{1,0:T(8,128)(2,1)S(1)}, u32[]{:S(2)}, u32[]{:S(2)}) collective-permute-start(bf16[384,1536]{1,0:T(8,128)(2,1)} %get-tuple-element.89), channel_id=1, source_target_pairs={{0,4},{4,0},{8,12},{12,8},{16,20},{20,16},{24,28},{28,24},{1,5},{5... | collective-permute-start | bytes 3538952 | tf_op jit(solution)/shard_map/ppermute | solution.py:42
  122.5 33.1 %collective-permute-start.16 = (bf16[3,1024,128]{2,1,0:T(8,128)(2,1)S(1)}, bf16[3,1024,128]{2,1,0:T(8,128)(2,1)S(1)}, u32[]{:S(2)}, u32[]{:S(2)}) collective-permute-start(bf16[3,1024,128]{2,1,0:T(8,128)(2,1)S(1)} %get-tuple-element.86), channel_id=1, source_target_pairs={{4,0},{8,4},{12,8},{16,12},{20,16},{24,20},{28,24},{5,1},{9,5},{13... | collective-permute-start | bytes 2359304 | tf_op jit(solution)/shard_map/ppermute | solution.py:48
  155.7 24.1 %collective-permute-start.19 = (bf16[3,1024,128]{2,1,0:T(8,128)(2,1)}, bf16[3,1024,128]{2,1,0:T(8,128)(2,1)S(1)}, u32[]{:S(2)}, u32[]{:S(2)}) collective-permute-start(bf16[3,1024,128]{2,1,0:T(8,128)(2,1)} %get-tuple-element.104), channel_id=1, source_target_pairs={{4,0},{8,4},{12,8},{16,12},{20,16},{24,20},{28,24},{5,1},{9,5},{13... | collective-permute-start | bytes 2359304 | tf_op jit(solution)/shard_map/ppermute | solution.py:48
  166.6 23.8 %collective-permute-start.20 = (bf16[192,1536]{1,0:T(8,128)(2,1)S(1)}, bf16[192,1536]{1,0:T(8,128)(2,1)S(1)}, u32[]{:S(2)}, u32[]{:S(2)}) collective-permute-start(bf16[192,1536]{1,0:T(8,128)(2,1)S(1)} %bitcast.112), channel_id=1, source_target_pairs={{0,8},{4,12},{8,0},{12,4},{16,24},{20,28},{24,16},{28,20},{1,9},{5... | collective-permute-start | bytes 1769480 | tf_op jit(solution)/shard_map/ppermute | solution.py:42
  179.7 13.2 %collective-permute-start.18 = (bf16[1024,768]{1,0:T(8,128)(2,1)}, bf16[1024,768]{1,0:T(8,128)(2,1)S(1)}, u32[]{:S(2)}, u32[]{:S(2)}) collective-permute-start(bf16[1024,768]{1,0:T(8,128)(2,1)} %get-tuple-element.101), channel_id=1, source_target_pairs={{0,1},{1,0},{2,3},{3,2},{4,5},{5,4},{6,7},{7,6},{8,9},{9,8},{10,11... | collective-permute-start | bytes 4718600 | tf_op jit(solution)/shard_map/ppermute | solution.py:42
  190.3 4.7 %collective-permute-start.21 = (bf16[1024,768]{1,0:T(8,128)(2,1)}, bf16[1024,768]{1,0:T(8,128)(2,1)S(1)}, u32[]{:S(2)}, u32[]{:S(2)}) collective-permute-start(bf16[1024,768]{1,0:T(8,128)(2,1)} %get-tuple-element.115), channel_id=1, source_target_pairs={{0,1},{1,0},{2,3},{3,2},{4,5},{5,4},{6,7},{7,6},{8,9},{9,8},{10,11... | collective-permute-start | bytes 4718600 | tf_op jit(solution)/shard_map/ppermute | solution.py:42
  192.4 15.9 %collective-permute-start.24 = (bf16[400,768]{1,0:T(8,128)(2,1)S(1)}, bf16[400,768]{1,0:T(8,128)(2,1)S(1)}, u32[]{:S(2)}, u32[]{:S(2)}) collective-permute-start(bf16[400,768]{1,0:T(8,128)(2,1)S(1)} %copy-done.35), channel_id=1, source_target_pairs={{0,4},{4,0},{8,12},{12,8},{16,20},{20,16},{24,28},{28,24},{1,5},{5... | collective-permute-start | bytes 1843208 | tf_op jit(solution)/shard_map/ppermute | solution.py:42
  196.3 23.3 %collective-permute-start.22 = (bf16[512,768]{1,0:T(8,128)(2,1)S(1)}, bf16[512,768]{1,0:T(8,128)(2,1)S(1)}, u32[]{:S(2)}, u32[]{:S(2)}) collective-permute-start(bf16[512,768]{1,0:T(8,128)(2,1)S(1)} %slice.238), channel_id=1, source_target_pairs={{0,2},{1,3},{2,0},{3,1},{4,6},{5,7},{6,4},{7,5},{8,10},{9,11},{10,... | collective-permute-start | bytes 2359304 | tf_op jit(solution)/shard_map/ppermute | solution.py:42
  197.2 23.3 %collective-permute-start.27 = (bf16[96,1536]{1,0:T(8,128)(2,1)S(1)}, bf16[96,1536]{1,0:T(8,128)(2,1)S(1)}, u32[]{:S(2)}, u32[]{:S(2)}) collective-permute-start(bf16[96,1536]{1,0:T(8,128)(2,1)S(1)} %fusion.13), channel_id=1, source_target_pairs={{0,16},{4,20},{8,24},{12,28},{16,0},{20,4},{24,8},{28,12},{1,17},{... | collective-permute-start | bytes 884744 | tf_op jit(solution)/shard_map/ppermute | solution.py:42
  209.1 10.5 %collective-permute-start.25 = (bf16[208,768]{1,0:T(8,128)(2,1)S(1)}, bf16[208,768]{1,0:T(8,128)(2,1)S(1)}, u32[]{:S(2)}, u32[]{:S(2)}) collective-permute-start(bf16[208,768]{1,0:T(8,128)(2,1)S(1)} %pad_maximum_fusion.7), channel_id=1, source_target_pairs={{0,8},{4,12},{8,0},{12,4},{16,24},{20,28},{24,16},{28,20},{1,9},{5... | collective-permute-start | bytes 958472 | tf_op jit(solution)/shard_map/ppermute | solution.py:42
  220.4 10.0 %collective-permute-start.26 = (bf16[112,768]{1,0:T(8,128)(2,1)S(1)}, bf16[112,768]{1,0:T(8,128)(2,1)}, u32[]{:S(2)}, u32[]{:S(2)}) collective-permute-start(bf16[112,768]{1,0:T(8,128)(2,1)S(1)} %pad_maximum_fusion.11), channel_id=1, source_target_pairs={{0,16},{4,20},{8,24},{12,28},{16,0},{20,4},{24,8},{28,12},{1,17},{... | collective-permute-start | bytes 516104 | tf_op jit(solution)/shard_map/ppermute | solution.py:42
  220.5 20.7 %collective-permute-start.23 = (bf16[512,768]{1,0:T(8,128)(2,1)S(1)}, bf16[512,768]{1,0:T(8,128)(2,1)S(1)}, u32[]{:S(2)}, u32[]{:S(2)}) collective-permute-start(bf16[512,768]{1,0:T(8,128)(2,1)S(1)} %slice.239), channel_id=1, source_target_pairs={{0,2},{1,3},{2,0},{3,1},{4,6},{5,7},{6,4},{7,5},{8,10},{9,11},{10,... | collective-permute-start | bytes 2359304 | tf_op jit(solution)/shard_map/ppermute | solution.py:42
  232.4 3.0 %collective-permute-start.28 = (f32[8,768]{1,0:T(8,128)}, f32[8,768]{1,0:T(8,128)S(1)}, u32[]{:S(2)}, u32[]{:S(2)}) collective-permute-start(f32[8,768]{1,0:T(8,128)} %get-tuple-element.128), channel_id=1, source_target_pairs={{0,1},{1,0},{2,3},{3,2},{4,5},{5,4},{6,7},{7,6},{8,9},{9,8},{10,11... | collective-permute-start | bytes 73736 | tf_op jit(solution)/shard_map/ppermute | solution.py:42
  236.1 4.5 %collective-permute-start.29 = (f32[8,768]{1,0:T(8,128)S(1)}, f32[8,768]{1,0:T(8,128)S(1)}, u32[]{:S(2)}, u32[]{:S(2)}) collective-permute-start(f32[8,768]{1,0:T(8,128)S(1)} %add.131), channel_id=1, source_target_pairs={{0,2},{1,3},{2,0},{3,1},{4,6},{5,7},{6,4},{7,5},{8,10},{9,11},{10,... | collective-permute-start | bytes 73736 | tf_op jit(solution)/shard_map/ppermute | solution.py:42
  (34 other events, 345.1 us)

commit v6 on v5

--- a/solution.py
+++ b/solution.py
@@ -693,7 +693,7 @@
     feed_gains, feed_bias = gains[2:], up_bias[None]
     early_ops = (feed_gains, feed_bias, first, start)
     down_own = jnp.concatenate([down_weight.T, out_own[:, pad:]], axis=1)
-    down_w, _ = gather_dp(down_own, down_order, [qkv_parts[-2]] + [None] * (bits - 2) + [(gs[2], up_w, early_ops)])
+    down_w, _ = gather_dp(down_own, down_order, [qkv_parts[-2]] + [None] * (bits - 2) + [(up_w, early_ops), gs[2]])
     tail = shift(after(kv, down_w), "dp", 1)
     normed, g, branch, back, do, ffn_send, ffn_keep, ffn_sums = ffn(
         hids, gs, feed_gains, up_w, down_w, qkv_w, feed_bias, high[None], heads, chunk

time: 245 us -> 244 us (level)
  waiting for transfers between devices: 78.2 us -> 75.3 us
  Pallas kernels: 94.5 us -> 97.3 us
    pallas_call x2, Pallas kernels: 24.9 us -> 27.7 us  [attention(): pl.pallas_call(functools.partial(attn_kernel, T=T, blk=blk, heads=heads,...]
  transfers between devices with their start and end apart: 30 -> 30, of which waited for: 17 -> 16; matrix products, arithmetic and copies ran while one was open for 10% -> 10% of each run, Pallas kernels for 39% -> 40%
where the time goes in v6:
time: 244 us; the launch traced here: 243 us
  Pallas kernels  97.3 us (40%)
  waiting for transfers between devices  75.3 us (31%)
  starting transfers between devices  32.3 us (13%)
  local copies, waits for them, and re-layouts  19.7 us (8%)
  other arithmetic  17 us (7%)
    ppermute x27, waiting for transfers between devices, swap(): return lax.ppermute(value, axis, [(i, i ^ mask) for i in range(count)])  61.5 us
    pallas_call x1, Pallas kernels, ffn(): pl.pallas_call(functools.partial(ffn_kernel, pieces=len(gs), blk=blk, chu...  30.3 us
    pallas_call x2, Pallas kernels, attention(): pl.pallas_call(functools.partial(attn_kernel, T=T, blk=blk, heads=heads,...  27.7 us
    ppermute x27, starting transfers between devices, swap(): return lax.ppermute(value, axis, [(i, i ^ mask) for i in range(count)])  25.8 us
    pallas_call x2, Pallas kernels, post(): pl.pallas_call(functools.partial(post_kernel, chunk=chunk), grid_spec=plt...  18.5 us
    ppermute x3, waiting for transfers between devices, shift(): return lax.ppermute(value, axis, route)  13.9 us
    unnamed x75, local copies, waits for them, and re-layouts  10.3 us
    pallas_call x1, Pallas kernels, mid(): pl.pallas_call(mid_kernel, grid=(T // MR,), in_specs=[cols, cols, rows, r...  9.29 us
  transfers between devices with their start and end apart: 30, of which 16 were waited for; matrix products, arithmetic and copies ran while one was open for 10% of the time, Pallas kernels for 40%

profile of v6, /device:TPU:0, one launch (start us, length us, event | category | flops | bytes accessed | tf_op | source)
XLA Modules:
  0.0 243.1 jit_solution(13104219560774583574)
XLA Ops:
  0.7 3.0 %collective-permute-start.1 = (bf16[512,768]{1,0:T(8,128)(2,1)}, bf16[512,768]{1,0:T(8,128)(2,1)S(1)}, u32[]{:S(2)}, u32[]{:S(2)}) collective-permute-start(bf16[512,768]{1,0:T(8,128)(2,1)} %refs_0_.3), channel_id=1, source_target_pairs={{0,2},{1,3},{2,0},{3,1},{4,6},{5,7},{6,4},{7,5},{8,10},{9,11},{10,... | collective-permute-start | bytes 2359304 | tf_op jit(solution)/shard_map/ppermute | solution.py:42
  3.7 2.6 %collective-permute-start.3 = (bf16[96,768]{1,0:T(8,128)(2,1)}, bf16[96,768]{1,0:T(8,128)(2,1)S(1)}, u32[]{:S(2)}, u32[]{:S(2)}) collective-permute-start(bf16[96,768]{1,0:T(8,128)(2,1)} %param.23), channel_id=1, source_target_pairs={{0,16},{4,20},{8,24},{12,28},{16,0},{20,4},{24,8},{28,12},{1,17},{... | collective-permute-start | bytes 442376 | tf_op jit(solution)/shard_map/ppermute | solution.py:42
  16.0 4.1 %collective-permute-start.9 = (bf16[192,768]{1,0:T(8,128)(2,1)S(1)}, bf16[192,768]{1,0:T(8,128)(2,1)S(1)}, u32[]{:S(2)}, u32[]{:S(2)}) collective-permute-start(bf16[192,768]{1,0:T(8,128)(2,1)S(1)} %get-tuple-element.163), channel_id=1, source_target_pairs={{0,8},{4,12},{8,0},{12,4},{16,24},{20,28},{24,16},{28,20},{1,9},{5... | collective-permute-start | bytes 884744 | tf_op jit(solution)/shard_map/ppermute | solution.py:42
  20.1 2.9 %collective-permute-done.4 = bf16[96,640]{1,0:T(8,128)(2,1)S(1)} collective-permute-done((bf16[96,640]{1,0:T(8,128)(2,1)S(1)}, bf16[96,640]{1,0:T(8,128)(2,1)S(1)}, u32[]{:S(2)}, u32[]{:S(2)}) %collective-permute-start.4) | collective-permute-done | bytes 122912 | tf_op jit(solution)/shard_map/ppermute | solution.py:42
  23.1 5.8 %collective-permute-done.9 = bf16[192,768]{1,0:T(8,128)(2,1)S(1)} collective-permute-done((bf16[192,768]{1,0:T(8,128)(2,1)S(1)}, bf16[192,768]{1,0:T(8,128)(2,1)S(1)}, u32[]{:S(2)}, u32[]{:S(2)}) %collective-permute-start.9) | collective-permute-done | bytes 294944 | tf_op jit(solution)/shard_map/ppermute | solution.py:42
  29.0 1.6 collective-permute-start.10
  30.6 3.0 %collective-permute-done.5 = bf16[192,640]{1,0:T(8,128)(2,1)S(1)} collective-permute-done((bf16[192,640]{1,0:T(8,128)(2,1)S(1)}, bf16[192,640]{1,0:T(8,128)(2,1)S(1)}, u32[]{:S(2)}, u32[]{:S(2)}) %collective-permute-start.5) | collective-permute-done | bytes 245792 | tf_op jit(solution)/shard_map/ppermute | solution.py:42
  33.9 1.6 collective-permute-start.6
  35.5 8.6 %collective-permute-done.7 = bf16[96,896]{1,0:T(8,128)(2,1)S(1)} collective-permute-done((bf16[96,896]{1,0:T(8,128)(2,1)S(1)}, bf16[96,896]{1,0:T(8,128)(2,1)S(1)}, u32[]{:S(2)}, u32[]{:S(2)}) %collective-permute-start.7) | collective-permute-done | bytes 172064 | tf_op jit(solution)/shard_map/ppermute | solution.py:42
  46.6 7.6 %collective-permute-done.8 = bf16[192,896]{1,0:T(8,128)(2,1)S(1)} collective-permute-done((bf16[192,896]{1,0:T(8,128)(2,1)S(1)}, bf16[192,896]{1,0:T(8,128)(2,1)S(1)}, u32[]{:S(2)}, u32[]{:S(2)}) %collective-permute-start.8) | collective-permute-done | bytes 344096 | tf_op jit(solution)/shard_map/ppermute | solution.py:42
  54.4 1.6 collective-permute-start.11
  59.2 7.7 %pre.1 = (bf16[2048,768]{1,0:T(8,128)(2,1)S(1)}, bf16[3,2048,128]{2,1,0:T(8,128)(2,1)S(1)}, bf16[3,2048,128]{2,1,0:T(8,128)(2,1)S(1)}) custom-call(bf16[512,768]{1,0:T(8,128)(2,1)S(1)} %copy-done, bf16[512,768]{1,0:T(8,128)(2,1)S(1)} %copy-done.10, bf16[512,768]{1,0:T(8,128)(2,1)S(1)} %copy-done.8, bf16[512,768]{1,0:T(8,128)(2,1)S(1)} %collective-permute-done.2.refs_3_, ...), custom_call_target="tpu_custom_call" | custom-call | flops 575000000 | bytes 1000 | tf_op jit(solution)/shard_map/pre/pallas_call | solution.py:199
  66.9 4.1 %collective-permute-done.11 = bf16[384,896]{1,0:T(8,128)(2,1)S(1)} collective-permute-done((bf16[384,896]{1,0:T(8,128)(2,1)S(1)}, bf16[384,896]{1,0:T(8,128)(2,1)S(1)}, u32[]{:S(2)}, u32[]{:S(2)}) %collective-permute-start.11) | collective-permute-done | bytes 688160 | tf_op jit(solution)/shard_map/ppermute | solution.py:42
  72.4 3.7 %collective-permute-start.13 = (bf16[3,2048,128]{2,1,0:T(8,128)(2,1)S(1)}, bf16[3,2048,128]{2,1,0:T(8,128)(2,1)S(1)}, u32[]{:S(2)}, u32[]{:S(2)}) collective-permute-start(bf16[3,2048,128]{2,1,0:T(8,128)(2,1)S(1)} %get-tuple-element.80.refs_4_), channel_id=1, source_target_pairs={{0,4},{4,8},{8,12},{12,16},{16,20},{20,24},{24,28},{1,5},{5,9},{9,... | collective-permute-start | bytes 4718600 | tf_op jit(solution)/shard_map/ppermute | solution.py:48
  76.7 2.1 collective-permute-done.14.refs_5_
  79.9 30.3 %ffn.1 = (bf16[2048,768]{1,0:T(8,128)(2,1)}, bf16[2048,768]{1,0:T(8,128)(2,1)}, bf16[2048,768]{1,0:T(8,128)(2,1)}, bf16[2048,768]{1,0:T(8,128)(2,1)}, bf16[3,204...) custom-call(bf16[512,768]{1,0:T(8,128)(2,1)} %refs_0_.3, ...), custom_call_target="tpu_custom_call" | custom-call | flops 575000000 | bytes 1000 | tf_op jit(solution)/shard_map/ffn/pallas_call | solution.py:289
  112.2 9.7 %attn.2 = (bf16[192,1024]{1,0:T(8,128)(2,1)S(1)}, bf16[192,1024]{1,0:T(8,128)(2,1)S(1)}, bf16[3,1024,128]{2,1,0:T(8,128)(2,1)S(1)}, f32[3,2048,128]{2,1,0:T(8,128)S(1)}) custom-call(s32[2]{0:T(128)S(1)} %pad_add_fusion.refs_0_.place_ref, s32[8]{0:T(128)S(1)} %and_select_fusion.refs_1_, s32[1,2048]{1,0:T(1,128)S(1)} %add_subtract_fusion.refs_2_, ...), custom_call_target="tpu_custom_call" | custom-call | flops 115000000 | bytes 1000 | tf_op jit(solution)/shard_map/attn/pallas_call | solution.py:444
  123.5 18.0 %attn.3 = (bf16[192,2048]{1,0:T(8,128)(2,1)S(1)}, bf16[192,2048]{1,0:T(8,128)(2,1)S(1)}, bf16[3,1024,128]{2,1,0:T(8,128)(2,1)}, f32[3,1024,128]{2,1,0:T(8,128)S(1)}, f32[3,1024,128]{2,1,0:T(8,128)S(1)}) custom-call(s32[2]{0:T(128)S(1)} %pad_add_fusion.refs_0_.place_ref, s32[8]{0:T(128)S(1)} %and_select_fusion.refs_1_, ...), custom_call_target="tpu_custom_call" | custom-call | flops 115000000 | bytes 1000 | tf_op jit(solution)/shard_map/attn/pallas_call | solution.py:444
  141.4 13.9 %collective-permute-done.16.ahead_ref = bf16[3,1024,128]{2,1,0:T(8,128)(2,1)S(1)} collective-permute-done((bf16[3,1024,128]{2,1,0:T(8,128)(2,1)S(1)}, bf16[3,1024,128]{2,1,0:T(8,128)(2,1)S(1)}, u32[]{:S(2)}, u32[]{:S(2)}) %collective-permute-start.16) | collective-permute-done | bytes 786464 | tf_op jit(solution)/shard_map/ppermute | solution.py:48
  157.0 9.1 %post.2 = (bf16[1024,768]{1,0:T(8,128)(2,1)}, bf16[1024,768]{1,0:T(8,128)(2,1)}, f32[768,384]{1,0:T(8,128)}, f32[8,768]{1,0:T(8,128)}) custom-call(s32[2]{0:T(128)} %copy-done.17, f32[3,1024,128]{2,1,0:T(8,128)} %copy-done.15, bf16[3,1024,128]{2,1,0:T(8,128)(2,1)} %copy-done.23, bf16[192,2048]{1,0:T(8,128)(2,1)} %copy-done.12, f32[8,2048]{1,0:T(8,128)} %copy-done.14, ...), custom_call_target="tpu_custom_call" | custom-call | flops 115000000 | bytes 1000 | tf_op jit(solution)/shard_map/post/pallas_call | solution.py:584
  166.2 2.6 %collective-permute-start.20 = (bf16[192,1536]{1,0:T(8,128)(2,1)S(1)}, bf16[192,1536]{1,0:T(8,128)(2,1)S(1)}, u32[]{:S(2)}, u32[]{:S(2)}) collective-permute-start(bf16[192,1536]{1,0:T(8,128)(2,1)S(1)} %bitcast.112), channel_id=1, source_target_pairs={{0,8},{4,12},{8,0},{12,4},{16,24},{20,28},{24,16},{28,20},{1,9},{5... | collective-permute-start | bytes 1769480 | tf_op jit(solution)/shard_map/ppermute | solution.py:42
  168.8 9.3 %mid.1 = (bf16[1024,768]{1,0:T(8,128)(2,1)}, bf16[1024,768]{1,0:T(8,128)(2,1)}, bf16[768,384]{1,0:T(8,128)(2,1)}) custom-call(bf16[192,2048]{1,0:T(8,128)(2,1)} %copy-done.16, bf16[192,2048]{1,0:T(8,128)(2,1)} %copy-done.12, bf16[2048,768]{1,0:T(8,128)(2,1)} %copy-done.3, bf16[2048,768]{1,0:T(8,128)(2,1)} %get-tuple-element.100.g_ref, ...), custom_call_target="tpu_custom_call" | custom-call | flops 115000000 | bytes 1000 | tf_op jit(solution)/shard_map/mid/pallas_call | solution.py:492
  179.1 9.4 %post.3 = (bf16[1024,768]{1,0:T(8,128)(2,1)}, bf16[1024,768]{1,0:T(8,128)(2,1)}, bf16[400,768]{1,0:T(8,128)(2,1)}, bf16[384,768]{1,0:T(8,128)(2,1)}, f32[8,768]{1,0:T(8,128)}) custom-call(s32[2]{0:T(128)} %copy-done.17, f32[3,1024,128]{2,1,0:T(8,128)} %copy-done.18, ...), custom_call_target="tpu_custom_call", output_to_operand_aliasing={{0}: (11, {}), {1}: (12, {})} | custom-call | flops 9200000000 | bytes 1000 | tf_op jit(solution)/shard_map/post/pallas_call | solution.py:584
  195.7 1.7 collective-permute-start.27
  197.3 9.3 %collective-permute-done.24 = bf16[400,768]{1,0:T(8,128)(2,1)S(1)} collective-permute-done((bf16[400,768]{1,0:T(8,128)(2,1)S(1)}, bf16[400,768]{1,0:T(8,128)(2,1)S(1)}, u32[]{:S(2)}, u32[]{:S(2)}) %collective-permute-start.24) | collective-permute-done | bytes 614432 | tf_op jit(solution)/shard_map/ppermute | solution.py:42
  208.8 9.9 %collective-permute-done.25 = bf16[208,768]{1,0:T(8,128)(2,1)S(1)} collective-permute-done((bf16[208,768]{1,0:T(8,128)(2,1)S(1)}, bf16[208,768]{1,0:T(8,128)(2,1)S(1)}, u32[]{:S(2)}, u32[]{:S(2)}) %collective-permute-start.25) | collective-permute-done | bytes 319520 | tf_op jit(solution)/shard_map/ppermute | solution.py:42
  221.6 2.9 %fusion.7 = f32[512,768]{1,0:T(8,128)} fusion(bf16[512,768]{1,0:T(8,128)(2,1)S(1)} %copy-done.1, bf16[512,768]{1,0:T(8,128)(2,1)} %refs_4_, f32[512]{0:T(512)S(1)} %get-tuple-element.183, f32[512]{0:T(512)S(1)} %get-tuple-element.184, f32[512]{0:T(512)S(1)} %add_rsqrt_fusion, f32[512]{0:T(512)S(1)} %broadcast_multiply_fusion.2, ...), kind=kLoop, calls=%fused_computation.13 | loop fusion | flops 4325376 | bytes 5513216 | tf_op jit(solution)/shard_map/add | solution.py:744
  224.5 2.0 ffn_finish.1
  227.2 2.3 collective-permute-done.26.other_ref
  229.5 1.9 mix_finish.1
  237.0 2.6 %collective-permute-done.29 = f32[8,768]{1,0:T(8,128)S(1)} collective-permute-done((f32[8,768]{1,0:T(8,128)S(1)}, f32[8,768]{1,0:T(8,128)S(1)}, u32[]{:S(2)}, u32[]{:S(2)}) %collective-permute-start.29) | collective-permute-done | bytes 24608 | tf_op jit(solution)/shard_map/ppermute | solution.py:42
  240.3 2.8 %fusion.10 = f32[512,768]{1,0:T(8,128)} fusion(bf16[512,768]{1,0:T(8,128)(2,1)S(1)} %copy-done.1, f32[1024,768]{1,0:T(8,128)} %copy-done.19, bf16[512,768]{1,0:T(8,128)(2,1)S(1)} %collective-permute-done.23, f32[768]{0:T(1024)S(1)} %copy-done.33), kind=kLoop, calls=%fused_computation.16 | loop fusion | flops 1966080 | bytes 4721664 | tf_op jit(solution)/shard_map/add | solution.py:747
  (200 shorter events, 44.1 us)
Async XLA Ops:
  0.7 43.6 %collective-permute-start.1 = (bf16[512,768]{1,0:T(8,128)(2,1)}, bf16[512,768]{1,0:T(8,128)(2,1)S(1)}, u32[]{:S(2)}, u32[]{:S(2)}) collective-permute-start(bf16[512,768]{1,0:T(8,128)(2,1)} %refs_0_.3), channel_id=1, source_target_pairs={{0,2},{1,3},{2,0},{3,1},{4,6},{5,7},{6,4},{7,5},{8,10},{9,11},{10,... | collective-permute-start | bytes 2359304 | tf_op jit(solution)/shard_map/ppermute | solution.py:42
  3.7 52.6 %collective-permute-start = (bf16[512,768]{1,0:T(8,128)(2,1)}, bf16[512,768]{1,0:T(8,128)(2,1)S(1)}, u32[]{:S(2)}, u32[]{:S(2)}) collective-permute-start(bf16[512,768]{1,0:T(8,128)(2,1)} %refs_0_.3), channel_id=1, source_target_pairs={{0,1},{1,0},{2,3},{3,2},{4,5},{5,4},{6,7},{7,6},{8,9},{9,8},{10,11... | collective-permute-start | bytes 2359304 | tf_op jit(solution)/shard_map/ppermute | solution.py:42
  3.7 10.5 %collective-permute-start.3 = (bf16[96,768]{1,0:T(8,128)(2,1)}, bf16[96,768]{1,0:T(8,128)(2,1)S(1)}, u32[]{:S(2)}, u32[]{:S(2)}) collective-permute-start(bf16[96,768]{1,0:T(8,128)(2,1)} %param.23), channel_id=1, source_target_pairs={{0,16},{4,20},{8,24},{12,28},{16,0},{20,4},{24,8},{28,12},{1,17},{... | collective-permute-start | bytes 442376 | tf_op jit(solution)/shard_map/ppermute | solution.py:42
  10.8 112.6 %copy-start.13 = (f32[8,2048]{1,0:T(8,128)}, f32[8,2048]{1,0:T(8,128)S(1)}, u32[]{:S(2)}) copy-start(f32[8,2048]{1,0:T(8,128)S(1)} %get-tuple-element.175.refs_8_.sin_ref) | copy-start | bytes 196612
  10.8 112.6 %copy-start.14 = (f32[8,2048]{1,0:T(8,128)}, f32[8,2048]{1,0:T(8,128)S(1)}, u32[]{:S(2)}) copy-start(f32[8,2048]{1,0:T(8,128)S(1)} %get-tuple-element.176.refs_7_.cos_ref) | copy-start | bytes 196612
  14.3 8.7 %collective-permute-start.4 = (bf16[96,640]{1,0:T(8,128)(2,1)S(1)}, bf16[96,640]{1,0:T(8,128)(2,1)S(1)}, u32[]{:S(2)}, u32[]{:S(2)}) collective-permute-start(bf16[96,640]{1,0:T(8,128)(2,1)S(1)} %pad_maximum_fusion.12), channel_id=1, source_target_pairs={{0,16},{4,20},{8,24},{12,28},{16,0},{20,4},{24,8},{28,12},{1,17},{... | collective-permute-start | bytes 368648 | tf_op jit(solution)/shard_map/ppermute | solution.py:42
  16.0 13.0 %collective-permute-start.9 = (bf16[192,768]{1,0:T(8,128)(2,1)S(1)}, bf16[192,768]{1,0:T(8,128)(2,1)S(1)}, u32[]{:S(2)}, u32[]{:S(2)}) collective-permute-start(bf16[192,768]{1,0:T(8,128)(2,1)S(1)} %get-tuple-element.163), channel_id=1, source_target_pairs={{0,8},{4,12},{8,0},{12,4},{16,24},{20,28},{24,16},{28,20},{1,9},{5... | collective-permute-start | bytes 884744 | tf_op jit(solution)/shard_map/ppermute | solution.py:42
  23.0 10.6 %collective-permute-start.5 = (bf16[192,640]{1,0:T(8,128)(2,1)S(1)}, bf16[192,640]{1,0:T(8,128)(2,1)S(1)}, u32[]{:S(2)}, u32[]{:S(2)}) collective-permute-start(bf16[192,640]{1,0:T(8,128)(2,1)S(1)} %get-tuple-element.166), channel_id=1, source_target_pairs={{0,8},{4,12},{8,0},{12,4},{16,24},{20,28},{24,16},{28,20},{1,9},{5... | collective-permute-start | bytes 737288 | tf_op jit(solution)/shard_map/ppermute | solution.py:42
  29.0 16.3 %collective-permute-start.10 = (bf16[384,768]{1,0:T(8,128)(2,1)S(1)}, bf16[384,768]{1,0:T(8,128)(2,1)S(1)}, u32[]{:S(2)}, u32[]{:S(2)}) collective-permute-start(bf16[384,768]{1,0:T(8,128)(2,1)S(1)} %bitcast.102), channel_id=1, source_target_pairs={{0,4},{4,0},{8,12},{12,8},{16,20},{20,16},{24,28},{28,24},{1,5},{5... | collective-permute-start | bytes 1769480 | tf_op jit(solution)/shard_map/ppermute | solution.py:42
  33.7 10.3 %collective-permute-start.7 = (bf16[96,896]{1,0:T(8,128)(2,1)S(1)}, bf16[96,896]{1,0:T(8,128)(2,1)S(1)}, u32[]{:S(2)}, u32[]{:S(2)}) collective-permute-start(bf16[96,896]{1,0:T(8,128)(2,1)S(1)} %pad_maximum_fusion.10), channel_id=1, source_target_pairs={{0,16},{4,20},{8,24},{12,28},{16,0},{20,4},{24,8},{28,12},{1,17},{... | collective-permute-start | bytes 516104 | tf_op jit(solution)/shard_map/ppermute | solution.py:42
  33.9 22.1 %collective-permute-start.6 = (bf16[384,640]{1,0:T(8,128)(2,1)S(1)}, bf16[384,640]{1,0:T(8,128)(2,1)S(1)}, u32[]{:S(2)}, u32[]{:S(2)}) collective-permute-start(bf16[384,640]{1,0:T(8,128)(2,1)S(1)} %bitcast.104), channel_id=1, source_target_pairs={{0,4},{4,0},{8,12},{12,8},{16,20},{20,16},{24,28},{28,24},{1,5},{5... | collective-permute-start | bytes 1474568 | tf_op jit(solution)/shard_map/ppermute | solution.py:42
  44.2 10.0 %collective-permute-start.8 = (bf16[192,896]{1,0:T(8,128)(2,1)S(1)}, bf16[192,896]{1,0:T(8,128)(2,1)S(1)}, u32[]{:S(2)}, u32[]{:S(2)}) collective-permute-start(bf16[192,896]{1,0:T(8,128)(2,1)S(1)} %get-tuple-element.158), channel_id=1, source_target_pairs={{0,8},{4,12},{8,0},{12,4},{16,24},{20,28},{24,16},{28,20},{1,9},{5... | collective-permute-start | bytes 1032200 | tf_op jit(solution)/shard_map/ppermute | solution.py:42
  44.3 22.6 %collective-permute-start.12 = (bf16[512,768]{1,0:T(8,128)(2,1)}, bf16[512,768]{1,0:T(8,128)(2,1)}, u32[]{:S(2)}, u32[]{:S(2)}) collective-permute-start(bf16[512,768]{1,0:T(8,128)(2,1)} %refs_4_), channel_id=1, source_target_pairs={{0,2},{1,3},{2,0},{3,1},{4,6},{5,7},{6,4},{7,5},{8,10},{9,11},{10,... | collective-permute-start | bytes 2359304 | tf_op jit(solution)/shard_map/ppermute | solution.py:42
  45.4 11.8 %collective-permute-start.2 = (bf16[512,768]{1,0:T(8,128)(2,1)S(1)}, bf16[512,768]{1,0:T(8,128)(2,1)S(1)}, u32[]{:S(2)}, u32[]{:S(2)}) collective-permute-start(bf16[512,768]{1,0:T(8,128)(2,1)S(1)} %collective-permute-done.1.refs_2_), channel_id=1, source_target_pairs={{0,1},{1,0},{2,3},{3,2},{4,5},{5,4},{6,7},{7,6},{8,9},{9,8},{10,11... | collective-permute-start | bytes 2359304 | tf_op jit(solution)/shard_map/ppermute | solution.py:42
  54.4 16.7 %collective-permute-start.11 = (bf16[384,896]{1,0:T(8,128)(2,1)S(1)}, bf16[384,896]{1,0:T(8,128)(2,1)S(1)}, u32[]{:S(2)}, u32[]{:S(2)}) collective-permute-start(bf16[384,896]{1,0:T(8,128)(2,1)S(1)} %bitcast.100), channel_id=1, source_target_pairs={{0,4},{4,0},{8,12},{12,8},{16,20},{20,16},{24,28},{28,24},{1,5},{5... | collective-permute-start | bytes 2064392 | tf_op jit(solution)/shard_map/ppermute | solution.py:42
  72.4 37.8 %collective-permute-start.13 = (bf16[3,2048,128]{2,1,0:T(8,128)(2,1)S(1)}, bf16[3,2048,128]{2,1,0:T(8,128)(2,1)S(1)}, u32[]{:S(2)}, u32[]{:S(2)}) collective-permute-start(bf16[3,2048,128]{2,1,0:T(8,128)(2,1)S(1)} %get-tuple-element.80.refs_4_), channel_id=1, source_target_pairs={{0,4},{4,8},{8,12},{12,16},{16,20},{20,24},{24,28},{1,5},{5,9},{9,... | collective-permute-start | bytes 4718600 | tf_op jit(solution)/shard_map/ppermute | solution.py:48
  76.1 2.7 %collective-permute-start.14 = (bf16[512,768]{1,0:T(8,128)(2,1)}, bf16[512,768]{1,0:T(8,128)(2,1)}, u32[]{:S(2)}, u32[]{:S(2)}) collective-permute-start(bf16[512,768]{1,0:T(8,128)(2,1)} %refs_4_), channel_id=1, source_target_pairs={{0,1},{1,0},{2,3},{3,2},{4,5},{5,4},{6,7},{7,6},{8,9},{9,8},{10,11... | collective-permute-start | bytes 2359304 | tf_op jit(solution)/shard_map/ppermute | solution.py:42
  76.2 3.7 %collective-permute-start.15 = (bf16[512,768]{1,0:T(8,128)(2,1)}, bf16[512,768]{1,0:T(8,128)(2,1)}, u32[]{:S(2)}, u32[]{:S(2)}) collective-permute-start(bf16[512,768]{1,0:T(8,128)(2,1)} %collective-permute-done.12.refs_6_), channel_id=1, source_target_pairs={{0,1},{1,0},{2,3},{3,2},{4,5},{5,4},{6,7},{7,6},{8,9},{9,8},{10,11... | collective-permute-start | bytes 2359304 | tf_op jit(solution)/shard_map/ppermute | solution.py:42
  110.2 45.1 %collective-permute-start.17 = (bf16[384,1536]{1,0:T(8,128)(2,1)}, bf16[384,1536]{1,0:T(8,128)(2,1)S(1)}, u32[]{:S(2)}, u32[]{:S(2)}) collective-permute-start(bf16[384,1536]{1,0:T(8,128)(2,1)} %get-tuple-element.91), channel_id=1, source_target_pairs={{0,4},{4,0},{8,12},{12,8},{16,20},{20,16},{24,28},{28,24},{1,5},{5... | collective-permute-start | bytes 3538952 | tf_op jit(solution)/shard_map/ppermute | solution.py:42
  121.9 33.4 %collective-permute-start.16 = (bf16[3,1024,128]{2,1,0:T(8,128)(2,1)S(1)}, bf16[3,1024,128]{2,1,0:T(8,128)(2,1)S(1)}, u32[]{:S(2)}, u32[]{:S(2)}) collective-permute-start(bf16[3,1024,128]{2,1,0:T(8,128)(2,1)S(1)} %get-tuple-element.88), channel_id=1, source_target_pairs={{4,0},{8,4},{12,8},{16,12},{20,16},{24,20},{28,24},{5,1},{9,5},{13... | collective-permute-start | bytes 2359304 | tf_op jit(solution)/shard_map/ppermute | solution.py:48
  155.3 22.8 %collective-permute-start.19 = (bf16[3,1024,128]{2,1,0:T(8,128)(2,1)}, bf16[3,1024,128]{2,1,0:T(8,128)(2,1)S(1)}, u32[]{:S(2)}, u32[]{:S(2)}) collective-permute-start(bf16[3,1024,128]{2,1,0:T(8,128)(2,1)} %get-tuple-element.106), channel_id=1, source_target_pairs={{4,0},{8,4},{12,8},{16,12},{20,16},{24,20},{28,24},{5,1},{9,5},{13... | collective-permute-start | bytes 2359304 | tf_op jit(solution)/shard_map/ppermute | solution.py:48
  166.2 22.5 %collective-permute-start.20 = (bf16[192,1536]{1,0:T(8,128)(2,1)S(1)}, bf16[192,1536]{1,0:T(8,128)(2,1)S(1)}, u32[]{:S(2)}, u32[]{:S(2)}) collective-permute-start(bf16[192,1536]{1,0:T(8,128)(2,1)S(1)} %bitcast.112), channel_id=1, source_target_pairs={{0,8},{4,12},{8,0},{12,4},{16,24},{20,28},{24,16},{28,20},{1,9},{5... | collective-permute-start | bytes 1769480 | tf_op jit(solution)/shard_map/ppermute | solution.py:42
  178.1 13.2 %collective-permute-start.18 = (bf16[1024,768]{1,0:T(8,128)(2,1)}, bf16[1024,768]{1,0:T(8,128)(2,1)S(1)}, u32[]{:S(2)}, u32[]{:S(2)}) collective-permute-start(bf16[1024,768]{1,0:T(8,128)(2,1)} %get-tuple-element.103), channel_id=1, source_target_pairs={{0,1},{1,0},{2,3},{3,2},{4,5},{5,4},{6,7},{7,6},{8,9},{9,8},{10,11... | collective-permute-start | bytes 4718600 | tf_op jit(solution)/shard_map/ppermute | solution.py:42
  188.7 4.7 %collective-permute-start.21 = (bf16[1024,768]{1,0:T(8,128)(2,1)}, bf16[1024,768]{1,0:T(8,128)(2,1)S(1)}, u32[]{:S(2)}, u32[]{:S(2)}) collective-permute-start(bf16[1024,768]{1,0:T(8,128)(2,1)} %get-tuple-element.117), channel_id=1, source_target_pairs={{0,1},{1,0},{2,3},{3,2},{4,5},{5,4},{6,7},{7,6},{8,9},{9,8},{10,11... | collective-permute-start | bytes 4718600 | tf_op jit(solution)/shard_map/ppermute | solution.py:42
  190.7 15.9 %collective-permute-start.24 = (bf16[400,768]{1,0:T(8,128)(2,1)S(1)}, bf16[400,768]{1,0:T(8,128)(2,1)S(1)}, u32[]{:S(2)}, u32[]{:S(2)}) collective-permute-start(bf16[400,768]{1,0:T(8,128)(2,1)S(1)} %copy-done.35), channel_id=1, source_target_pairs={{0,4},{4,0},{8,12},{12,8},{16,20},{20,16},{24,28},{28,24},{1,5},{5... | collective-permute-start | bytes 1843208 | tf_op jit(solution)/shard_map/ppermute | solution.py:42
  194.7 23.9 %collective-permute-start.22 = (bf16[512,768]{1,0:T(8,128)(2,1)S(1)}, bf16[512,768]{1,0:T(8,128)(2,1)S(1)}, u32[]{:S(2)}, u32[]{:S(2)}) collective-permute-start(bf16[512,768]{1,0:T(8,128)(2,1)S(1)} %slice.238), channel_id=1, source_target_pairs={{0,2},{1,3},{2,0},{3,1},{4,6},{5,7},{6,4},{7,5},{8,10},{9,11},{10,... | collective-permute-start | bytes 2359304 | tf_op jit(solution)/shard_map/ppermute | solution.py:42
  195.7 23.9 %collective-permute-start.27 = (bf16[96,1536]{1,0:T(8,128)(2,1)S(1)}, bf16[96,1536]{1,0:T(8,128)(2,1)S(1)}, u32[]{:S(2)}, u32[]{:S(2)}) collective-permute-start(bf16[96,1536]{1,0:T(8,128)(2,1)S(1)} %fusion.13), channel_id=1, source_target_pairs={{0,16},{4,20},{8,24},{12,28},{16,0},{20,4},{24,8},{28,12},{1,17},{... | collective-permute-start | bytes 884744 | tf_op jit(solution)/shard_map/ppermute | solution.py:42
  207.5 11.2 %collective-permute-start.25 = (bf16[208,768]{1,0:T(8,128)(2,1)S(1)}, bf16[208,768]{1,0:T(8,128)(2,1)S(1)}, u32[]{:S(2)}, u32[]{:S(2)}) collective-permute-start(bf16[208,768]{1,0:T(8,128)(2,1)S(1)} %pad_maximum_fusion.7), channel_id=1, source_target_pairs={{0,8},{4,12},{8,0},{12,4},{16,24},{20,28},{24,16},{28,20},{1,9},{5... | collective-permute-start | bytes 958472 | tf_op jit(solution)/shard_map/ppermute | solution.py:42
  219.5 10.0 %collective-permute-start.26 = (bf16[112,768]{1,0:T(8,128)(2,1)S(1)}, bf16[112,768]{1,0:T(8,128)(2,1)}, u32[]{:S(2)}, u32[]{:S(2)}) collective-permute-start(bf16[112,768]{1,0:T(8,128)(2,1)S(1)} %pad_maximum_fusion.11), channel_id=1, source_target_pairs={{0,16},{4,20},{8,24},{12,28},{16,0},{20,4},{24,8},{28,12},{1,17},{... | collective-permute-start | bytes 516104 | tf_op jit(solution)/shard_map/ppermute | solution.py:42
  219.6 20.7 %collective-permute-start.23 = (bf16[512,768]{1,0:T(8,128)(2,1)S(1)}, bf16[512,768]{1,0:T(8,128)(2,1)S(1)}, u32[]{:S(2)}, u32[]{:S(2)}) collective-permute-start(bf16[512,768]{1,0:T(8,128)(2,1)S(1)} %slice.239), channel_id=1, source_target_pairs={{0,2},{1,3},{2,0},{3,1},{4,6},{5,7},{6,4},{7,5},{8,10},{9,11},{10,... | collective-permute-start | bytes 2359304 | tf_op jit(solution)/shard_map/ppermute | solution.py:42
  231.4 3.0 %collective-permute-start.28 = (f32[8,768]{1,0:T(8,128)}, f32[8,768]{1,0:T(8,128)S(1)}, u32[]{:S(2)}, u32[]{:S(2)}) collective-permute-start(f32[8,768]{1,0:T(8,128)} %get-tuple-element.130), channel_id=1, source_target_pairs={{0,1},{1,0},{2,3},{3,2},{4,5},{5,4},{6,7},{7,6},{8,9},{9,8},{10,11... | collective-permute-start | bytes 73736 | tf_op jit(solution)/shard_map/ppermute | solution.py:42
  235.2 4.5 %collective-permute-start.29 = (f32[8,768]{1,0:T(8,128)S(1)}, f32[8,768]{1,0:T(8,128)S(1)}, u32[]{:S(2)}, u32[]{:S(2)}) collective-permute-start(f32[8,768]{1,0:T(8,128)S(1)} %add.131), channel_id=1, source_target_pairs={{0,2},{1,3},{2,0},{3,1},{4,6},{5,7},{6,4},{7,5},{8,10},{9,11},{10,... | collective-permute-start | bytes 73736 | tf_op jit(solution)/shard_map/ppermute | solution.py:42
  (34 other events, 331.0 us)
